TPU v7x, 32 devices: a whole 2x2x4 slice. The times are simulated.
32 devices in a mesh: station: 4 (over y, x), tm: 8 (over z, core).
Axes of the slice: x: 2, y: 2, z: 4, core: 2. Of those that a mesh axis runs over, the one named last changes fastest.
Arguments:
- queries: bfloat16 [64, 256, 512], P('station', 'tm'), may hold values from -36 to 36
- grid_keys: bfloat16 [64, 256, 512], P('station', 'tm'), may hold values from -12 to 12
- values: bfloat16 [64, 256, 512], P('station', 'tm'), may hold values from -6 to 6
- glob_queries: bfloat16 [256, 512], P('tm'), may hold values from -36 to 36
- glob_keys: bfloat16 [256, 512], P('tm'), may hold values from -8.4 to 8.4
- glob_values: bfloat16 [256, 512], P('tm'), may hold values from -6 to 6
- out_weight: bfloat16 [512, 512], replicated, may hold values from -0.5 to 0.5
Outputs:
- grid_output: bfloat16 [64, 256, 512], P('station', 'tm')
- glob_output: bfloat16 [256, 512], P('tm')
All inputs are finite; a program needn't handle non-finite values.
Results may differ from a plain program's by a relative error of at most 0.0052.
Values may be sent and summed in bfloat16 or wider, within the bound.
No kernel may reach another device: no remote copies, remote signals or barrier semaphores. Data moves between devices by JAX's collectives and lax.ppermute only.
A program may use at most 320 MiB of HBM per device.

v0:
```python
import math

import jax
import jax.numpy as jnp
from jax import lax
from jax.sharding import PartitionSpec as P

H = 8
HD = 64
RAD = 4
G = 256


NEG_FILL = -1e30


def with_halo(array, sides, width):
    for axis, dim in sides:
        count, length = (lax.axis_size(axis), array.shape[dim])
        up = [(i, (i + 1) % count) for i in range(count - 1)]
        down = [(j, i) for i, j in up]
        last = lax.slice_in_dim(array, length - width, length, axis=dim)
        leading = lax.slice_in_dim(array, 0, width, axis=dim)
        before = lax.ppermute(last, axis, up)
        after = lax.ppermute(leading, axis, down)
        array = jnp.concatenate([before, array, after], axis=dim)
    return array


def merged_2(part, axis, combine):
    gathered = jax.tree.map(lambda a: lax.all_gather(a, axis), part)

    def take(source):
        return jax.tree.map(lambda a: lax.dynamic_index_in_dim(a, source, 0, False), gathered)

    return lax.fori_loop(
        1, lax.axis_size(axis), lambda source, state: combine(state, take(source)), take(0)
    )


def band_attend(
    query_band, pair_band, band_top, band_left, total_rows, total_cols, glob_k, glob_v, radius
):
    row_count, col_count, model_width = query_band.shape
    head_count = glob_k.shape[1]
    head_size = model_width // head_count
    block_side = 2 * radius
    block_across = col_count // block_side
    block_count = 2 * block_across
    cell_count = block_side * block_side
    reach_count = 4 * cell_count
    query_blocks = (
        query_band.reshape(2, block_side, block_across, block_side, model_width)
        .transpose(0, 2, 1, 3, 4)
        .reshape(block_count, cell_count, head_count, head_size)
    )
    grid_view = pair_band.reshape(3, block_side, block_across + 1, block_side, 2 * model_width)
    stacked = jnp.stack(
        [
            jnp.stack(
                [
                    grid_view[lower : lower + 2, :, rightward : rightward + block_across]
                    for rightward in range(2)
                ],
                0,
            )
            for lower in range(2)
        ],
        0,
    )
    windows = stacked.transpose(2, 4, 0, 3, 1, 5, 6).reshape(
        block_count, reach_count, 2 * model_width
    )
    window_keys = windows[:, :, :model_width].reshape(
        block_count, reach_count, head_count, head_size
    )
    window_vals = windows[:, :, model_width:].reshape(
        block_count, reach_count, head_count, head_size
    )
    block_ids = jnp.arange(block_count, dtype=jnp.int32)
    block_row = band_top + block_side * (block_ids // block_across)
    block_col = band_left + block_side * (block_ids % block_across)
    query_ids = jnp.arange(cell_count, dtype=jnp.int32)
    key_ids = jnp.arange(reach_count, dtype=jnp.int32)
    query_row = block_row[:, None] + query_ids[None, :] // block_side
    query_col = block_col[:, None] + query_ids[None, :] % block_side
    key_row = (
        block_row[:, None]
        + key_ids // (2 * cell_count) * block_side
        + key_ids // (2 * block_side) % block_side
        - radius
    )
    key_col = (
        block_col[:, None] + key_ids // block_side % 2 * block_side + key_ids % block_side - radius
    )
    in_window = (jnp.abs(query_row[:, :, None] - key_row[:, None, :]) <= radius) & (
        jnp.abs(query_col[:, :, None] - key_col[:, None, :]) <= radius
    )
    in_window = (
        in_window
        & ((key_row >= 0) & (key_row < total_rows) & (key_col >= 0) & (key_col < total_cols))[
            :, None, :
        ]
    )
    score_scale = 1.0 / math.sqrt(head_size)
    window_scores = (
        jnp.einsum("bqhd,bkhd->bhqk", query_blocks, window_keys, preferred_element_type=jnp.float32)
        * score_scale
    )
    window_scores = jnp.where(in_window[:, None], window_scores, NEG_FILL)
    global_scores = (
        jnp.einsum("bqhd,ghd->bhqg", query_blocks, glob_k, preferred_element_type=jnp.float32)
        * score_scale
    )
    top_score = jnp.maximum(jnp.max(window_scores, -1), jnp.max(global_scores, -1))[..., None]
    window_exp = jnp.exp(window_scores - top_score)
    global_exp = jnp.exp(global_scores - top_score)
    denominator = jnp.sum(window_exp, -1, keepdims=True) + jnp.sum(global_exp, -1, keepdims=True)
    window_weights = (window_exp / denominator).astype(jnp.bfloat16)
    global_weights = (global_exp / denominator).astype(jnp.bfloat16)
    attended = jnp.einsum(
        "bhqk,bkhd->bqhd", window_weights, window_vals, preferred_element_type=jnp.float32
    )
    attended = attended + jnp.einsum(
        "bhqg,ghd->bqhd", global_weights, glob_v, preferred_element_type=jnp.float32
    )
    return attended.astype(jnp.bfloat16).reshape(block_count * cell_count, model_width)


def unblock(flat_out, row_count, col_count, radius):
    block_side = 2 * radius
    block_across = col_count // block_side
    return (
        flat_out.reshape(2, block_across, block_side, block_side, -1)
        .transpose(0, 2, 1, 3, 4)
        .reshape(row_count, col_count, -1)
    )


def split_product(weights, value_rows):
    upper = weights.astype(jnp.bfloat16)
    lower = (weights - upper.astype(jnp.float32)).astype(jnp.bfloat16)
    result = jnp.einsum("ghk,khd->ghd", upper, value_rows, preferred_element_type=jnp.float32)
    return result + jnp.einsum(
        "ghk,khd->ghd", lower, value_rows, preferred_element_type=jnp.float32
    )


def combine_parts(former, latter):
    top_score = jnp.maximum(former[0], latter[0])
    fade_former = jnp.exp(former[0] - top_score)
    fade_latter = jnp.exp(latter[0] - top_score)
    denominator = former[1] * fade_former + latter[1] * fade_latter
    glob_count, head_count = top_score.shape
    accum = (
        former[2].reshape(glob_count, head_count, -1) * fade_former[..., None]
        + latter[2].reshape(glob_count, head_count, -1) * fade_latter[..., None]
    )
    return (top_score, denominator, accum.reshape(glob_count, -1))


def body(queries, grid_keys, values, glob_queries, glob_keys, glob_values, out_weight):
    row_count, col_count, model_width = queries.shape
    own_globals = glob_queries.shape[0]
    all_q, all_k, all_v = (
        lax.all_gather(glob_queries, "tm", axis=0, tiled=True),
        lax.all_gather(glob_keys, "tm", axis=0, tiled=True),
        lax.all_gather(glob_values, "tm", axis=0, tiled=True),
    )
    glob_k = all_k.reshape(G, H, HD)
    glob_v = all_v.reshape(G, H, HD)
    paired = jnp.concatenate([grid_keys, values], -1)
    padded = with_halo(paired, (("station", 0), ("tm", 1)), RAD)
    score_scale = 1.0 / math.sqrt(HD)
    local_keys = grid_keys.reshape(row_count * col_count, H, HD)
    local_vals = values.reshape(row_count * col_count, H, HD)
    glob_q = all_q.reshape(G, H, HD)
    scores = (
        jnp.einsum("ghd,khd->ghk", glob_q, local_keys, preferred_element_type=jnp.float32)
        * score_scale
    )
    local_top = jnp.max(scores, -1)
    weights = jnp.exp(scores - local_top[..., None])
    local_total = jnp.sum(weights, -1)
    local_accum = split_product(weights, local_vals)
    row_start = lax.axis_index("station") * row_count
    col_start = lax.axis_index("tm") * col_count
    total_rows = row_count * lax.axis_size("station")
    total_cols = col_count * lax.axis_size("tm")
    band_rows = 4 * RAD

    def one_band(band_index):
        band_start = band_index * band_rows
        flat_out = band_attend(
            queries,
            padded,
            row_start + band_start,
            col_start,
            total_rows,
            total_cols,
            glob_k,
            glob_v,
            RAD,
        )
        projected = jnp.dot(flat_out, out_weight, preferred_element_type=jnp.float32).astype(
            jnp.bfloat16
        )
        return unblock(projected, band_rows, col_count, RAD)

    grid_output = lax.map(one_band, jnp.arange(row_count // band_rows, dtype=jnp.int32)).reshape(
        row_count, col_count, model_width
    )
    glob_start = lax.axis_index("tm") * own_globals
    merged = merged_2(
        (local_top, local_total, local_accum.reshape(G, model_width)),
        ("station", "tm"),
        combine_parts,
    )
    own_top = lax.dynamic_slice_in_dim(merged[0], glob_start, own_globals, 0)
    own_total = lax.dynamic_slice_in_dim(merged[1], glob_start, own_globals, 0)
    own_accum = lax.dynamic_slice_in_dim(merged[2], glob_start, own_globals, 0)
    own_q = glob_queries.reshape(own_globals, H, HD)
    own_scores = (
        jnp.einsum("ghd,khd->ghk", own_q, glob_k, preferred_element_type=jnp.float32) * score_scale
    )
    new_top = jnp.maximum(own_top, jnp.max(own_scores, -1))
    fade_own = jnp.exp(own_top - new_top)
    own_weights = jnp.exp(own_scores - new_top[..., None])
    denominator = own_total * fade_own + jnp.sum(own_weights, -1)
    accum = own_accum.reshape(own_globals, H, HD) * fade_own[..., None]
    accum = accum + split_product(own_weights, glob_v)
    attended = (
        (accum / denominator[..., None]).reshape(own_globals, model_width).astype(jnp.bfloat16)
    )
    glob_output = jnp.dot(attended, out_weight, preferred_element_type=jnp.float32).astype(
        jnp.bfloat16
    )
    return (grid_output, glob_output)


def solution(mesh):
    return jax.shard_map(
        body,
        mesh=mesh,
        in_specs=(
            P("station", "tm", None),
            P("station", "tm", None),
            P("station", "tm", None),
            P("tm", None),
            P("tm", None),
            P("tm", None),
            P(),
        ),
        out_specs=(P("station", "tm", None), P("tm", None)),
        check_vma=False,
    )
```

profile of v0, /device:TPU:1, one launch (start us, length us, event | category | flops | bytes accessed | tf_op | source)
XLA Modules:
  0.0 287.5 jit_solution(5829359850660120315)
XLA Ops:
  7.2 16.1 %all_gather.26 = bf16[256,512]{1,0:T(8,128)(2,1)S(1)} all-gather(bf16[32,512]{1,0:T(8,128)(2,1)} %param.12), channel_id=1, replica_groups=mesh['station'=4,'tm'=8] {'tm'}, dimensions={0}, use_global_device_ids=true | all-gather | bytes 294912 | tf_op jit(solution)/shard_map/all_gather | solution.py:166
  23.5 1.6 reshape.477
  25.1 1.6 reshape.479
  32.2 3.8 %collective-permute-start = (bf16[4,32,1024]{2,1,0:T(8,128)(2,1)}, bf16[4,32,1024]{2,1,0:T(8,128)(2,1)}, u32[]{:S(2)}, u32[]{:S(2)}) collective-permute-start(bf16[4,32,1024]{2,1,0:T(8,128)(2,1)} %get-tuple-element.247), channel_id=1, source_target_pairs={{0,8},{8,16},{16,24},{1,9},{9,17},{17,25},{2,10},{10,18},{18,26},{... | collective-permute-start | bytes 786440 | tf_op jit(solution)/shard_map/ppermute | solution.py:24
  36.0 1.3 collective-permute-start.1
  37.4 15.3 %all_gather.24 = bf16[256,512]{1,0:T(8,128)(2,1)S(1)} all-gather(bf16[32,512]{1,0:T(8,128)(2,1)S(1)} %copy-done.10), channel_id=1, replica_groups=mesh['station'=4,'tm'=8] {'tm'}, dimensions={0}, use_global_device_ids=true | all-gather | bytes 294912 | tf_op jit(solution)/shard_map/all_gather | solution.py:167
  53.6 1.6 reshape.471
  55.3 1.2 copy.79
  56.6 48.2 %all-gather = f32[8192,8]{0,1:T(8,128)} all-gather(f32[256,8]{0,1:T(8,128)S(1)} %get-tuple-element.253), channel_id=2, replica_groups=mesh['station'=4,'tm'=8] {'station','tm'}, dimensions={0}, use_global_device_ids=true | all-gather | bytes 270336 | tf_op jit(solution)/shard_map/all_gather | solution.py:31
  104.8 2.9 %fusion.9 = f32[256,8]{0,1:T(8,128)S(1)} fusion(f32[8,512,256]{2,1,0:T(8,128)} %copy-done.1, f32[256,8]{0,1:T(8,128)S(1)} %get-tuple-element.253), kind=kLoop, calls=%fused_computation.27 | loop fusion | flops 3143680 | bytes 4210688 | tf_op jit(solution)/shard_map/reduce_sum | solution.py:184
  107.7 42.1 %all-gather.1 = f32[8192,8]{0,1:T(8,128)} all-gather(f32[256,8]{0,1:T(8,128)S(1)} %fusion.9), channel_id=3, replica_groups=mesh['station'=4,'tm'=8] {'station','tm'}, dimensions={0}, use_global_device_ids=true | all-gather | bytes 270336 | tf_op jit(solution)/shard_map/all_gather | solution.py:31
  150.9 1.9 copy-done.2
  153.4 14.2 %all_gather.25 = bf16[256,512]{1,0:T(8,128)(2,1)S(1)} all-gather(bf16[32,512]{1,0:T(8,128)(2,1)S(1)} %copy-done.11), channel_id=1, replica_groups=mesh['station'=4,'tm'=8] {'tm'}, dimensions={0}, use_global_device_ids=true | all-gather | bytes 294912 | tf_op jit(solution)/shard_map/all_gather | solution.py:168
  169.5 1.1 pad_maximum_fusion.3
  170.6 1.9 collective-permute-start.2
  172.6 2.6 collective-permute-start.3
  175.5 4.0 %collective-permute-done.3 = bf16[24,4,1024]{2,1,0:T(4,128)(2,1)S(1)} collective-permute-done((bf16[24,4,1024]{2,1,0:T(4,128)(2,1)S(1)}, bf16[24,4,1024]{2,1,0:T(4,128)(2,1)S(1)}, u32[]{:S(2)}, u32[]{:S(2)}) %collective-permute-start.3) | collective-permute-done | bytes 196640 | tf_op jit(solution)/shard_map/ppermute | solution.py:25
  179.6 2.1 pad_maximum_fusion
  183.6 2.5 fusion.56
  186.1 3.9 %copy.74 = bf16[8,256,512]{1,2,0:T(8,128)(2,1)} copy(bf16[8,256,512]{2,1,0:T(8,128)(2,1)} %get-tuple-element.239) | data formatting | bytes 4194304 | tf_op jit(solution)/shard_map/while/body/eval_jaxpr/slice | solution.py:77
  190.0 3.9 %copy.75 = bf16[8,256,512]{1,2,0:T(8,128)(2,1)} copy(bf16[8,256,512]{2,1,0:T(8,128)(2,1)} %get-tuple-element.240) | data formatting | bytes 4194304 | tf_op jit(solution)/shard_map/while/body/eval_jaxpr/slice | solution.py:74
  193.9 2.6 fusion.6
  196.7 2.4 fusion.7
  199.1 3.1 %fusion.18 = f32[8,8,64,64]{2,3,0,1:T(8,128)S(1)} fusion(bf16[256,8,64,1]{0,2,1,3:T(8,128)(2,1)S(1)} %bitcast.159, f32[8,256,8,64]{1,3,2,0:T(8,128)S(1)} %bitcast.147, f32[8,8,64]{2,1,0:T(8,128)S(1)} %add.384, f32[8,8,64]{2,1,0:T(8,128)S(1)} %max.21), kind=kOutput, calls=%fused_computation.38 | convolution fusion | flops 138412032 | bytes 5537792 | tf_op jit(solution)/shard_map/while/body/eval_jaxpr/bhqg,ghd->bqhd/dot_general | solution.py:124
  202.2 2.4 fusion.12
  208.5 70.0 %while.23 = (s32[]{:T(128)}, f32[256,8]{0,1:T(8,128)S(1)}, f32[256,8]{0,1:T(8,128)S(1)}, f32[256,512]{0,1:T(8,128)S(1)}, f32[32,256,8]{1,2,0:T(8,128)}, /*index=...) while((s32[]{:T(128)}, f32[256,8]{0,1:T(8,128)S(1)}, ...), condition=%wide.region_7.8_spmd, body=%wide.region_6.7_spmd.sunk | while | flops 405509 | bytes 3752079 | solution.py:36
  211.5 1.1 constant_dynamic-slice_fusion.3
  213.8 1.1 constant_dynamic-slice_fusion.3
  216.0 1.1 constant_dynamic-slice_fusion.3
  222.8 1.1 constant_dynamic-slice_fusion.3
  225.1 1.1 constant_dynamic-slice_fusion.3
  227.3 1.1 constant_dynamic-slice_fusion.3
  (197 shorter events, 81.0 us)
Async XLA Ops:
  7.2 198.8 %copy-start = (bf16[512,512]{1,0:T(8,128)(2,1)S(1)}, bf16[512,512]{1,0:T(8,128)(2,1)}, u32[]{:S(2)}) copy-start(bf16[512,512]{1,0:T(8,128)(2,1)} %param.15) | copy-start | bytes 1572868
  7.2 200.1 %all-gather.4.cloned.1.call-start = ((), (), s32[]{:S(2)}) async-start(), calls=%async_computation | async-start | bytes 17301504 | tf_op jit(solution)/shard_map/all_gather | solution.py:31
  28.2 1.9 copy-start.1
  29.2 2.0 copy-start.5
  29.2 2.1 copy-start.6
  29.2 8.1 %copy-start.10 = (bf16[32,512]{1,0:T(8,128)(2,1)S(1)}, bf16[32,512]{1,0:T(8,128)(2,1)}, u32[]{:S(2)}) copy-start(bf16[32,512]{1,0:T(8,128)(2,1)} %param.13) | copy-start | bytes 98308
  30.2 22.6 %copy-start.8 = (bf16[16,32,512]{2,1,0:T(8,128)(2,1)S(1)}, bf16[16,32,512]{2,1,0:T(8,128)(2,1)}, u32[]{:S(2)}) copy-start(bf16[16,32,512]{2,1,0:T(8,128)(2,1)} %param.9) | copy-start | bytes 1572868
  32.2 137.3 %collective-permute-start = (bf16[4,32,1024]{2,1,0:T(8,128)(2,1)}, bf16[4,32,1024]{2,1,0:T(8,128)(2,1)}, u32[]{:S(2)}, u32[]{:S(2)}) collective-permute-start(bf16[4,32,1024]{2,1,0:T(8,128)(2,1)} %get-tuple-element.247), channel_id=1, source_target_pairs={{0,8},{8,16},{16,24},{1,9},{9,17},{17,25},{2,10},{10,18},{18,26},{... | collective-permute-start | bytes 786440 | tf_op jit(solution)/shard_map/ppermute | solution.py:24
  36.0 133.5 %collective-permute-start.1 = (bf16[4,32,1024]{2,1,0:T(8,128)(2,1)}, bf16[4,32,1024]{2,1,0:T(8,128)(2,1)}, u32[]{:S(2)}, u32[]{:S(2)}) collective-permute-start(bf16[4,32,1024]{2,1,0:T(8,128)(2,1)} %get-tuple-element.248), channel_id=1, source_target_pairs={{8,0},{16,8},{24,16},{9,1},{17,9},{25,17},{10,2},{18,10},{26,18},{... | collective-permute-start | bytes 786440 | tf_op jit(solution)/shard_map/ppermute | solution.py:25
  56.5 93.7 %copy-start.4 = (bf16[8,64,8,64]{3,1,0,2:T(8,128)(2,1)S(1)}, bf16[8,64,8,64]{3,1,0,2:T(8,128)(2,1)}, u32[]{:S(2)}) copy-start(bf16[8,64,8,64]{3,1,0,2:T(8,128)(2,1)} %copy.79) | copy-start | bytes 1572868
  150.2 3.3 %copy-start.11 = (bf16[32,512]{1,0:T(8,128)(2,1)S(1)}, bf16[32,512]{1,0:T(8,128)(2,1)}, u32[]{:S(2)}) copy-start(bf16[32,512]{1,0:T(8,128)(2,1)} %param.14) | copy-start | bytes 98308
  150.2 17.5 %copy-start.9 = (bf16[32,512]{1,0:T(8,128)(2,1)S(1)}, bf16[32,512]{1,0:T(8,128)(2,1)}, u32[]{:S(2)}) copy-start(bf16[32,512]{1,0:T(8,128)(2,1)} %param.12) | copy-start | bytes 98308
  150.9 1.9 copy-start.2
  170.6 4.9 %collective-permute-start.2 = (bf16[24,4,1024]{2,1,0:T(4,128)(2,1)S(1)}, bf16[24,4,1024]{2,1,0:T(4,128)(2,1)S(1)}, u32[]{:S(2)}, u32[]{:S(2)}) collective-permute-start(bf16[24,4,1024]{2,1,0:T(4,128)(2,1)S(1)} %get-tuple-element.245), channel_id=1, source_target_pairs={{0,1},{1,2},{2,3},{3,4},{4,5},{5,6},{6,7},{8,9},{9,10},{10,11},{11... | collective-permute-start | bytes 589832 | tf_op jit(solution)/shard_map/ppermute | solution.py:24
  172.6 7.0 %collective-permute-start.3 = (bf16[24,4,1024]{2,1,0:T(4,128)(2,1)S(1)}, bf16[24,4,1024]{2,1,0:T(4,128)(2,1)S(1)}, u32[]{:S(2)}, u32[]{:S(2)}) collective-permute-start(bf16[24,4,1024]{2,1,0:T(4,128)(2,1)S(1)} %get-tuple-element.246), channel_id=1, source_target_pairs={{1,0},{2,1},{3,2},{4,3},{5,4},{6,5},{7,6},{9,8},{10,9},{11,10},{12... | collective-permute-start | bytes 589832 | tf_op jit(solution)/shard_map/ppermute | solution.py:25
  193.9 2.8 copy-start.3
  199.1 3.1 %copy-start.7 = (bf16[8,256,512]{1,2,0:T(8,128)(2,1)S(1)}, bf16[8,256,512]{1,2,0:T(8,128)(2,1)}, u32[]{:S(2)}) copy-start(bf16[8,256,512]{1,2,0:T(8,128)(2,1)} %copy.74) | copy-start | bytes 6291460
Sparse Core Ops, SparseCore 0:
  31.3 120.3 all-gather.3
where the time goes:
time: 292 us; the launch traced here: 287 us
  blocking collectives  136 us (47%)
  local copies, waits for them, and re-layouts  68.8 us (24%)
  other arithmetic  40.3 us (14%)
  between operations  14.5 us (5%)
  matrix products  13.2 us (5%)
  starting transfers between devices  9.64 us (3%)
  waiting for transfers between devices  4.07 us (1%)
    all_gather x2, blocking collectives, merged_2(): gathered = jax.tree.map(lambda a: lax.all_gather(a, axis), part)  90.3 us
    dynamic_slice x64, local copies, waits for them, and re-layouts, take(): lax.dynamic_index_in_dim(a, source, 0, False)  41 us
    add x31, other arithmetic, combine_parts(): denominator = former[1] * fade_former + latter[1] * fade_latter  22.7 us
    all_gather x1, blocking collectives, body(): lax.all_gather(glob_queries, 'tm', axis=0, tiled=True)  16.1 us
    all_gather x1, blocking collectives, body(): lax.all_gather(glob_keys, 'tm', axis=0, tiled=True)  15.3 us
    all_gather x1, blocking collectives, body(): lax.all_gather(glob_values, 'tm', axis=0, tiled=True)  14.2 us
    add x31, other arithmetic, combine_parts(): former[2].reshape(glob_count, head_count, -1) * fade_former[..., None]  6.59 us
    slice x2, local copies, waits for them, and re-layouts, band_attend(): windows[:, :, model_width:]  6.37 us
  transfers between devices with their start and end apart: 5, of which 1 were waited for; matrix products, arithmetic and copies ran while one was open for 14% of the time, Pallas kernels for 0%

commit v1 on v0

v1 whole, which is shorter than its diff:
```python
import functools

import jax
import jax.numpy as jnp
from jax import lax
from jax.experimental import pallas as pl
from jax.experimental.pallas import tpu as pltpu
from jax.sharding import PartitionSpec as P

H = 8
HD = 64
RAD = 4
SIDE = 2 * RAD
PAIR = 2 * HD
STAT = 128
NEG_FILL = -1e30
VMEM = pltpu.VMEM
BF = jnp.bfloat16
F32 = jnp.float32


def dot_nt(a, b):
    return lax.dot_general(a, b, (((1,), (1,)), ((), ())), preferred_element_type=F32)


def dot_nn(a, b):
    return lax.dot_general(a, b, (((1,), (0,)), ((), ())), preferred_element_type=F32)


def low_half(shape):
    return lax.broadcasted_iota(jnp.int32, shape, len(shape) - 1) < HD


def head_rows(q):
    q = q * jnp.asarray(HD**-0.5, q.dtype)
    low = low_half(q.shape)
    zero = jnp.zeros_like(q)
    return jnp.concatenate([jnp.where(low, q, zero), jnp.where(low, zero, q)], 0)


def with_ones(v):
    return jnp.concatenate([v, jnp.ones_like(v)], 1)


def softmax_pair(q, keys, vals, biases, round_top=False):
    n = q.shape[0]
    rows = head_rows(q)
    scores = []
    for key, bias in zip(keys, biases):
        s = dot_nt(rows, key)
        scores.append(s if bias is None else s + bias)
    top = functools.reduce(jnp.maximum, [jnp.max(s, -1, keepdims=True) for s in scores])
    if round_top:
        top = top.astype(BF).astype(F32)
    weights = [jnp.exp(s - top).astype(BF) for s in scores]
    outs = []
    for head in range(2):
        part = slice(head * n, head * n + n)
        outs.append(
            functools.reduce(
                jnp.add, [dot_nn(w[part], with_ones(v)) for w, v in zip(weights, vals)]
            )
        )
    totals = [o[:, PAIR:] for o in outs]
    low = low_half((n, PAIR))
    attended = jnp.where(low, outs[0][:, :PAIR], outs[1][:, :PAIR]) / jnp.where(
        low, totals[0], totals[1]
    )
    return attended, (top[:n], top[n:]), totals


def partial_softmax(q, keys, vals, out_refs):
    n = q.shape[0]
    lane = lax.broadcasted_iota(jnp.int32, (n, STAT), 1)
    stats = jnp.zeros((n, STAT), F32)
    pieces = []
    for p in range(H // 2):
        cut = slice(p * PAIR, (p + 1) * PAIR)
        out, tops, totals = softmax_pair(
            q[:, cut], [k[:, cut] for k in keys], [v[:, cut] for v in vals],
            [None] * len(keys), True,
        )
        pieces.append(out.astype(BF))
        for i in range(2):
            stats = jnp.where(lane == 2 * p + i, tops[i], stats)
            stats = jnp.where(lane == H + 2 * p + i, totals[i], stats)
    full = jnp.concatenate(pieces + [stats.astype(BF)], 1)
    start = 0
    for ref in out_refs:
        ref[...] = full[start : start + ref.shape[0]]
        start += ref.shape[0]


def global_kernel(pieces, *refs):
    q = jnp.concatenate([refs[i][...] for i in range(pieces)], 0)
    ka, kb, va, vb = refs[pieces : pieces + 4]
    partial_softmax(q, [ka, kb], [va, vb], refs[pieces + 4 :])


def spread(stat_lanes):
    n = stat_lanes.shape[0]
    upper = stat_lanes.astype(BF)
    lower = (stat_lanes - upper.astype(F32)).astype(BF)
    source = lax.broadcasted_iota(jnp.int32, (STAT, H * HD), 0) - H
    target = lax.broadcasted_iota(jnp.int32, (STAT, H * HD), 1) // HD
    pick = (source == target).astype(BF)
    return dot_nn(upper, pick) + dot_nn(lower, pick)


def merge(first, second):
    width = H * HD
    lane = lax.broadcasted_iota(jnp.int32, (first.shape[0], STAT), 1)
    stats = [x[:, width:].astype(F32) for x in (first, second)]
    top = jnp.maximum(stats[0], stats[1])
    mass = [s * pltpu.roll(jnp.exp(s - top), H, 1) for s in stats]
    total = mass[0] + mass[1]
    held = (lane >= H) & (lane < 2 * H)
    safe = jnp.where(held, total, 1.0)
    shares = [spread(jnp.where(held, m, 0.0) / safe) for m in mass]
    out = first[:, :width].astype(F32) * shares[0] + second[:, :width].astype(F32) * shares[1]
    return out, jnp.where(lane < H, top, jnp.where(held, total, 0.0))


def ordered(flag_ref, index, own, other):
    mine_first = flag_ref[index] == 0
    return jnp.where(mine_first, own, other), jnp.where(mine_first, other, own)


def merge_kernel(flag_index, flags, own, other, *outs):
    a, b = own[...], other[...]
    if flag_index is not None:
        a, b = ordered(flags, flag_index, a, b)
    out, stats = merge(a, b)
    full = jnp.concatenate([out.astype(BF), stats.astype(BF)], 1)
    start = 0
    for ref in outs:
        ref[...] = full[start : start + ref.shape[0]]
        start += ref.shape[0]


def last_merge_kernel(flag_index, flags, own, other, extra, weight, out_ref):
    a, b = ordered(flags, flag_index, own[...], other[...])
    out, stats = merge(a, b)
    both = jnp.concatenate([out, stats], 1)
    out, _ = merge(both, extra[...].astype(F32))
    out_ref[...] = dot_nn(out.astype(BF), weight[...]).astype(BF)


def row_window(up, own, down, block, cols, lanes):
    rows = own.shape[0]
    first, stop = block * SIDE - RAD, block * SIDE + SIDE + RAD
    parts = []
    if first < 0:
        parts.append(up[:, cols, lanes])
    parts.append(own[max(first, 0) : min(stop, rows), cols, lanes])
    if stop > rows:
        parts.append(down[:, cols, lanes])
    return jnp.concatenate(parts, 0) if len(parts) > 1 else parts[0]


def window_bias(flags, block, blocks, wrap):
    key_cols = 3 * SIDE if wrap else 2 * SIDE
    shape = (SIDE, SIDE, 2 * SIDE, key_cols)
    n, k = SIDE * SIDE, 2 * SIDE * key_cols
    q = lax.broadcasted_iota(jnp.int32, (n, k), 0)
    key = lax.broadcasted_iota(jnp.int32, (n, k), 1)
    q_row, q_col = q // SIDE, q % SIDE
    k_row, k_col = key // key_cols, key % key_cols
    if wrap:
        q_col = jnp.where(q_col < RAD, q_col + RAD, q_col + RAD + SIDE)
    else:
        q_col = q_col + RAD
    ok = (jnp.abs(q_row + RAD - k_row) <= RAD) & (jnp.abs(q_col - k_col) <= RAD)
    if block == 0:
        ok = ok & ((k_row >= RAD) | (flags[0] != 0))
    if block == blocks - 1:
        ok = ok & ((k_row < SIDE + RAD) | (flags[1] != 0))
    if wrap:
        ok = ok & ((k_col < SIDE + RAD) | (k_col >= 2 * SIDE) | (flags[3] != 0))
        ok = ok & ((k_col < SIDE) | (k_col >= SIDE + RAD) | (flags[2] != 0))
    bias = jnp.where(ok, 0.0, NEG_FILL)
    return jnp.concatenate([bias, bias], 0)


def inner_kernel(block, blocks, own_part, *refs):
    flags, q_ref, k_ref, v_ref, halo_up, halo_down, gk_own, gk_other = refs[:8]
    rows, cols, width = q_ref.shape
    own_keys = gk_own.shape[0] // 2
    bias = window_bias(flags, block, blocks, False)
    out_ref = refs[-2] if own_part else refs[-1]
    halves = RAD
    gks, gvs = global_views(gk_own, gk_other)
    for p in range(H // 2):
        lanes = slice(p * PAIR, (p + 1) * PAIR)
        gk = jnp.concatenate([g[:, lanes] for g in gks], 0)
        gv = jnp.concatenate([g[:, lanes] for g in gvs], 0)
        for j in range(cols // SIDE - 1):
            span = slice(j * SIDE, (j + 2) * SIDE)
            keys = row_window(halo_up.at[:RAD], k_ref, halo_down.at[:RAD], block, span, lanes)
            vals = row_window(halo_up.at[RAD:], v_ref, halo_down.at[RAD:], block, span, lanes)
            q = q_ref[
                block * SIDE : (block + 1) * SIDE, j * SIDE + RAD : (j + 1) * SIDE + RAD, lanes
            ].reshape(SIDE * SIDE, PAIR)
            out, _, _ = softmax_pair(
                q, [keys.reshape(-1, PAIR), gk], [vals.reshape(-1, PAIR), gv], [bias, None]
            )
            out_ref[j, :, lanes] = out.astype(BF)
    if own_part:
        gq_ref = refs[8]
        partial_softmax(gq_ref[...], gks, gvs, [refs[-1]])


def global_views(own, other):
    keys, vals = [], []
    for ref in (own, other):
        for i in range(ref.shape[0]):
            keys.append(ref[i, 0])
            vals.append(ref[i, 1])
    return [jnp.concatenate(keys, 0)], [jnp.concatenate(vals, 0)]


def swap_halves(x):
    return pltpu.roll(x.astype(F32), RAD, 1).astype(x.dtype)


def pack_kernel(flags, k_ref, v_ref, halo_up, halo_down, outer_ref, inner_ref):
    cols = k_ref.shape[1]
    first = flags[4] == 0
    groups = []
    for span in (slice(0, SIDE), slice(cols - SIDE, cols)):
        keys = jnp.concatenate([halo_up[:RAD, span], k_ref[:, span], halo_down[:RAD, span]], 0)
        vals = jnp.concatenate([halo_up[RAD:, span], v_ref[:, span], halo_down[RAD:, span]], 0)
        groups.append((keys, swap_halves(vals)))
    low = lax.broadcasted_iota(jnp.int32, groups[0][0].shape, 1) < RAD
    left = jnp.where(low, groups[0][0], groups[0][1])
    right = jnp.where(low, groups[1][1], groups[1][0])
    outer_ref[...] = jnp.where(first, left, right)
    inner_ref[...] = jnp.where(first, right, left)


def edge_kernel(blocks, flags, q_ref, k_ref, v_ref, halo_up, halo_down, gk_own, gk_other,
                outer_ref, inner_ref, weight, *refs):
    inner_blocks, out_ref = refs[:-1], refs[-1]
    rows, cols, width = q_ref.shape
    across = cols // SIDE
    gks, gvs = global_views(gk_own, gk_other)
    first = flags[4] == 0
    outer, inner = outer_ref[...], inner_ref[...]
    right = jnp.where(first, inner, outer)
    left = jnp.where(first, outer, inner)
    low = lax.broadcasted_iota(jnp.int32, right.shape, 1) < RAD
    edge_k = jnp.where(low, right, left)
    edge_v = swap_halves(jnp.where(low, left, right))
    starts = (cols - SIDE, 0)
    for block in range(blocks):
        bias = window_bias(flags, block, blocks, True)
        band = slice(block * SIDE, block * SIDE + 2 * SIDE)
        q_rows = slice(block * SIDE, (block + 1) * SIDE)
        pieces = []
        for p in range(H // 2):
            lanes = slice(p * PAIR, (p + 1) * PAIR)
            gk, gv = gks[0][:, lanes], gvs[0][:, lanes]
            windows = []
            for half, own, edge in ((slice(0, RAD), k_ref, edge_k), (slice(RAD, 2 * RAD), v_ref, edge_v)):
                last, lead = [
                    row_window(halo_up.at[half], own, halo_down.at[half], block, slice(s, s + SIDE), lanes)
                    for s in starts
                ]
                windows.append(
                    jnp.concatenate([last, edge[band, :, lanes], lead], 1).reshape(-1, PAIR)
                )
            q = jnp.concatenate(
                [q_ref[q_rows, cols - RAD :, lanes], q_ref[q_rows, :RAD, lanes]], 1
            ).reshape(SIDE * SIDE, PAIR)
            out, _, _ = softmax_pair(
                q, [windows[0], gk], [windows[1], gv], [bias, None]
            )
            pieces.append(out.astype(BF))
        wrapped = jnp.concatenate(pieces, 1)
        done = inner_blocks[block][...].reshape((across - 1) * SIDE * SIDE, width)
        all_rows = jnp.concatenate([done, wrapped], 0)
        projected = dot_nn(all_rows, weight[...]).reshape(across, SIDE, SIDE, width)
        for j in range(across):
            before = projected[(j - 1) % across][:, RAD:]
            after = projected[j][:, :RAD]
            out_ref[q_rows, j * SIDE : (j + 1) * SIDE, :] = jnp.concatenate(
                [before, after], 1
            ).astype(BF)


def call(kernel, inputs, out_shapes, flops, flags=None):
    specs = [pl.BlockSpec(memory_space=VMEM)] * len(inputs)
    if flags is not None:
        specs = [pl.BlockSpec(memory_space=pltpu.SMEM)] + specs
        inputs = [flags, *inputs]
    return pl.pallas_call(
        kernel,
        out_shape=[jax.ShapeDtypeStruct(s, BF) for s in out_shapes],
        in_specs=specs,
        out_specs=[pl.BlockSpec(memory_space=VMEM)] * len(out_shapes),
        compiler_params=pltpu.CompilerParams(vmem_limit_bytes=48 * 2**20),
        cost_estimate=pl.CostEstimate(flops=flops, bytes_accessed=2**20, transcendentals=0),
    )(*inputs)


def body(queries, grid_keys, values, glob_queries, glob_keys, glob_values, out_weight):
    rows, cols, width = queries.shape
    tokens = rows * cols
    own = glob_queries.shape[0]
    stations, across = lax.axis_size("station"), lax.axis_size("tm")
    chips = across // 2
    payload = width + STAT
    blocks = rows // SIDE
    station, column = lax.axis_index("station"), lax.axis_index("tm")
    station_bits = [1 << b for b in range(stations.bit_length() - 1)]
    chip_bits = [1 << b for b in range(chips.bit_length() - 1)]

    def over_tm(x, mask):
        return lax.ppermute(x, "tm", [(i, i ^ mask) for i in range(across)])

    def over_station(x, mask):
        return lax.ppermute(x, "station", [(i, i ^ mask) for i in range(stations)])

    flags = jnp.stack(
        [
            station > 0,
            station < stations - 1,
            column < across - 1,
            column > 0,
            column % 2 == 1,
        ]
        + [(station & bit) > 0 for bit in station_bits]
    ).astype(jnp.int32)

    up = [(i, i + 1) for i in range(stations - 1)]
    down = [(j, i) for i, j in up]
    other_keys, other_vals = over_tm(grid_keys, 1), over_tm(values, 1)
    q_pieces = [glob_queries] + [over_tm(glob_queries, 2 * m) for m in range(1, chips)]
    halo_up = lax.ppermute(jnp.concatenate([grid_keys[rows - RAD :], values[rows - RAD :]], 0), "station", up)
    halo_down = lax.ppermute(jnp.concatenate([grid_keys[:RAD], values[:RAD]], 0), "station", down)
    kv = jnp.stack([glob_keys, glob_values])
    kv_own = jnp.stack([kv] + [over_tm(kv, 2 * m) for m in range(1, chips)])
    kv_other = over_tm(kv_own, 1)

    flat = [x.reshape(tokens, width) for x in (grid_keys, other_keys, values, other_vals)]
    half = chips * own // 2
    kept, sent = call(
        functools.partial(global_kernel, chips),
        [*q_pieces, *flat],
        [(half, payload)] * 2,
        2 * 10**9,
    )
    shared = [queries, grid_keys, values, halo_up, halo_down, kv_own, kv_other]
    inner_shape = (cols // SIDE - 1, SIDE * SIDE, width)
    first_block, extra = call(
        functools.partial(inner_kernel, 0, blocks, True),
        [*shared, glob_queries],
        [inner_shape, (own, payload)],
        2 * 10**9,
        flags,
    )
    later_blocks = [
        call(functools.partial(inner_kernel, b, blocks, False), shared, [inner_shape], 2 * 10**9, flags)[0]
        for b in range(1, blocks)
    ]
    outer, inner = call(
        pack_kernel,
        [grid_keys, values, halo_up, halo_down],
        [(rows + 2 * RAD, SIDE, width)] * 2,
        10**8,
        flags,
    )
    facing = [(i, i + 1) for i in range(1, across - 1, 2)]
    outer = lax.ppermute(outer, "tm", facing + [(j, i) for i, j in facing])
    inner = over_tm(inner, 1)
    (grid_output,) = call(
        functools.partial(edge_kernel, blocks),
        [*shared, outer, inner, out_weight, first_block, *later_blocks],
        [(rows, cols, width)],
        3 * 10**9,
        flags,
    )

    for bit in reversed(chip_bits):
        arrived = over_tm(sent, 2 * bit)
        split = [(half // 2, payload)] * 2 if bit > 1 else [(half, payload)]
        merged = call(functools.partial(merge_kernel, None), [kept, arrived], split, 10**8, flags)
        kept, sent = merged if bit > 1 else (merged[0], None)
        half //= 2
    first_flag = 5
    for i, bit in enumerate(station_bits):
        arrived = over_station(kept, bit)
        if i < len(station_bits) - 1:
            (kept,) = call(
                functools.partial(merge_kernel, first_flag + i), [kept, arrived], [(own, payload)], 10**8, flags
            )
        else:
            (glob_output,) = call(
                functools.partial(last_merge_kernel, first_flag + i),
                [kept, arrived, extra, out_weight],
                [(own, width)],
                10**8,
                flags,
            )
    return grid_output, glob_output


def solution(mesh):
    return jax.shard_map(
        body,
        mesh=mesh,
        in_specs=(
            P("station", "tm", None),
            P("station", "tm", None),
            P("station", "tm", None),
            P("tm", None),
            P("tm", None),
            P("tm", None),
            P(),
        ),
        out_specs=(P("station", "tm", None), P("tm", None)),
        check_vma=False,
    )
```

time: 292 us -> 57.4 us (0.20)
  the two profiles are of different devices: /device:TPU:1 before, /device:TPU:0 now
where the time goes in v1:
time: 57.4 us; the launch traced here: 57.1 us
  Pallas kernels  21 us (37%)
  starting transfers between devices  19.8 us (34%)
  waiting for transfers between devices  13.4 us (23%)
  local copies, waits for them, and re-layouts  1.13 us (2%)
  between operations  0.96 us (2%)
  other arithmetic  0.88 us (2%)
    pallas_call x9, Pallas kernels, call(): pl.pallas_call(kernel, out_shape=[jax.ShapeDtypeStruct(s, BF) for s in ou...  21 us
    ppermute x12, starting transfers between devices, over_tm(): return lax.ppermute(x, 'tm', [(i, i ^ mask) for i in range(across)])  12.8 us
    ppermute x1, waiting for transfers between devices, body(): lax.ppermute(jnp.concatenate([grid_keys[:RAD], values[:RAD]], 0), 'statio...  7.56 us
    ppermute x12, waiting for transfers between devices, over_tm(): return lax.ppermute(x, 'tm', [(i, i ^ mask) for i in range(across)])  4.62 us
    ppermute x1, starting transfers between devices, body(): lax.ppermute(jnp.concatenate([grid_keys[rows - RAD:], values[rows - RAD:]...  3.4 us
    ppermute x2, starting transfers between devices, over_station(): return lax.ppermute(x, 'station', [(i, i ^ mask) for i in range(stations)])  1.63 us
    ppermute x1, starting transfers between devices, body(): lax.ppermute(jnp.concatenate([grid_keys[:RAD], values[:RAD]], 0), 'statio...  1.29 us
    ppermute x1, waiting for transfers between devices, body(): lax.ppermute(jnp.concatenate([grid_keys[rows - RAD:], values[rows - RAD:]...  1.18 us
  transfers between devices with their start and end apart: 17, of which 3 were waited for; matrix products, arithmetic and copies ran while one was open for 3% of the time, Pallas kernels for 34%

profile of v1, /device:TPU:0, one launch (start us, length us, event | category | flops | bytes accessed | tf_op | source)
XLA Modules:
  0.0 57.1 jit_solution(14515111451530849015)
XLA Ops:
  0.6 5.1 %collective-permute-start.10 = (bf16[32,512]{1,0:T(8,128)(2,1)}, bf16[32,512]{1,0:T(8,128)(2,1)S(1)}, u32[]{:S(2)}, u32[]{:S(2)}) collective-permute-start(bf16[32,512]{1,0:T(8,128)(2,1)} %refs_0_.1), channel_id=1, source_target_pairs={{0,6},{1,7},{2,4},{3,5},{4,2},{5,3},{6,0},{7,1},{8,14},{9,15},{10,... | collective-permute-start | bytes 98312 | tf_op jit(solution)/shard_map/ppermute | solution.py:319
  5.8 0.5 collective-permute-start.12
  6.3 0.8 %fusion = (bf16[1,2,32,512]{3,2,1,0:T(8,128)(2,1)S(1)}, bf16[2,32,512]{2,1,0:T(8,128)(2,1)S(1)}) fusion(bf16[1,32,512]{2,1,0:T(8,128)(2,1)} %bitcast.25, bf16[1,32,512]{2,1,0:T(8,128)(2,1)} %bitcast.26), kind=kLoop, calls=%fused_computation.4 | loop fusion | flops 32768 | bytes 196608 | tf_op jit(solution)/shard_map/stack | solution.py:342
  7.1 2.1 %collective-permute-start.2 = (bf16[2,32,512]{2,1,0:T(8,128)(2,1)S(1)}, bf16[2,32,512]{2,1,0:T(8,128)(2,1)S(1)}, u32[]{:S(2)}, u32[]{:S(2)}) collective-permute-start(bf16[2,32,512]{2,1,0:T(8,128)(2,1)S(1)} %get-tuple-element.23), channel_id=1, source_target_pairs={{0,2},{1,3},{2,0},{3,1},{4,6},{5,7},{6,4},{7,5},{8,10},{9,11},{10,... | collective-permute-start | bytes 196616 | tf_op jit(solution)/shard_map/ppermute | solution.py:319
  9.1 1.0 %fusion.1 = (bf16[4,32,512]{2,1,0:T(8,128)(2,1)S(1)}, bf16[4,32,512]{2,1,0:T(8,128)(2,1)S(1)}) fusion(bf16[16,32,512]{2,1,0:T(8,128)(2,1)} %k_ref.3), kind=kLoop, calls=%fused_computation.5 | loop fusion | bytes 524288 | tf_op jit(solution)/shard_map/slice | solution.py:340
  10.2 0.0 copy-start.4
  10.2 0.1 collective-permute-start.3
  10.3 2.4 %collective-permute-start.4 = (bf16[2,32,512]{2,1,0:T(8,128)(2,1)S(1)}, bf16[2,32,512]{2,1,0:T(8,128)(2,1)S(1)}, u32[]{:S(2)}, u32[]{:S(2)}) collective-permute-start(bf16[2,32,512]{2,1,0:T(8,128)(2,1)S(1)} %get-tuple-element.23), channel_id=1, source_target_pairs={{0,6},{1,7},{2,4},{3,5},{4,2},{5,3},{6,0},{7,1},{8,14},{9,15},{10,... | collective-permute-start | bytes 196616 | tf_op jit(solution)/shard_map/ppermute | solution.py:319
  12.7 1.1 %collective-permute-start.9 = (bf16[32,512]{1,0:T(8,128)(2,1)S(1)}, bf16[32,512]{1,0:T(8,128)(2,1)S(1)}, u32[]{:S(2)}, u32[]{:S(2)}) collective-permute-start(bf16[32,512]{1,0:T(8,128)(2,1)S(1)} %copy-done.4), channel_id=1, source_target_pairs={{0,4},{1,5},{2,6},{3,7},{4,0},{5,1},{6,2},{7,3},{8,12},{9,13},{10,... | collective-permute-start | bytes 98312 | tf_op jit(solution)/shard_map/ppermute | solution.py:319
  13.8 4.6 %collective-permute-done.3 = bf16[2,32,512]{2,1,0:T(8,128)(2,1)S(1)} collective-permute-done((bf16[2,32,512]{2,1,0:T(8,128)(2,1)S(1)}, bf16[2,32,512]{2,1,0:T(8,128)(2,1)S(1)}, u32[]{:S(2)}, u32[]{:S(2)}) %collective-permute-start.3) | collective-permute-done | bytes 65568 | tf_op jit(solution)/shard_map/ppermute | solution.py:319
  18.4 3.4 %collective-permute-start = (bf16[8,32,512]{2,1,0:T(8,128)(2,1)S(1)}, bf16[8,32,512]{2,1,0:T(8,128)(2,1)S(1)}, u32[]{:S(2)}, u32[]{:S(2)}) collective-permute-start(bf16[8,32,512]{2,1,0:T(8,128)(2,1)S(1)} %pad_maximum_fusion), channel_id=1, source_target_pairs={{0,8},{8,16},{16,24},{1,9},{9,17},{17,25},{2,10},{10,18},{18,26},{... | collective-permute-start | bytes 786440 | tf_op jit(solution)/shard_map/ppermute | solution.py:339
  21.8 1.3 %collective-permute-start.1 = (bf16[8,32,512]{2,1,0:T(8,128)(2,1)S(1)}, bf16[8,32,512]{2,1,0:T(8,128)(2,1)S(1)}, u32[]{:S(2)}, u32[]{:S(2)}) collective-permute-start(bf16[8,32,512]{2,1,0:T(8,128)(2,1)S(1)} %pad_maximum_fusion.1), channel_id=1, source_target_pairs={{8,0},{16,8},{24,16},{9,1},{17,9},{25,17},{10,2},{18,10},{26,18},{... | collective-permute-start | bytes 786440 | tf_op jit(solution)/shard_map/ppermute | solution.py:340
  23.2 0.1 collective-permute-start.5
  23.3 2.1 %shard_map.90 = (bf16[64,640]{1,0:T(8,128)(2,1)S(1)}, bf16[64,640]{1,0:T(8,128)(2,1)S(1)}) custom-call(bf16[32,512]{1,0:T(8,128)(2,1)S(1)} %copy-done.4, bf16[32,512]{1,0:T(8,128)(2,1)S(1)} %collective-permute-done.8.refs_1_, bf16[32,512]{1,0:T(8,128)(2,1)S(1)} %collective-permute-done.9.refs_2_, bf16[32,512]{1,0:T(8,128)(2,1)S(1)} %collective-permute-done.10.refs_3_, ...), custom_call_target="tpu_custom_call" | custom-call | flops 2000000000 | bytes 1048576 | tf_op jit(solution)/shard_map/pallas_call | solution.py:296
  25.4 0.1 collective-permute-start.13
  25.5 0.1 stack.55
  25.6 1.2 %collective-permute-done.halo_up.refs_4_ = bf16[8,32,512]{2,1,0:T(8,128)(2,1)S(1)} collective-permute-done((bf16[8,32,512]{2,1,0:T(8,128)(2,1)S(1)}, bf16[8,32,512]{2,1,0:T(8,128)(2,1)S(1)}, u32[]{:S(2)}, u32[]{:S(2)}) %collective-permute-start) | collective-permute-done | bytes 262176 | tf_op jit(solution)/shard_map/ppermute | solution.py:339
  26.8 7.6 %collective-permute-done.1.halo_down.refs_5_ = bf16[8,32,512]{2,1,0:T(8,128)(2,1)S(1)} collective-permute-done((bf16[8,32,512]{2,1,0:T(8,128)(2,1)S(1)}, bf16[8,32,512]{2,1,0:T(8,128)(2,1)S(1)}, u32[]{:S(2)}, u32[]{:S(2)}) %collective-permute-start.1) | collective-permute-done | bytes 262176 | tf_op jit(solution)/shard_map/ppermute | solution.py:340
  34.3 0.7 %shard_map.86 = (bf16[24,8,512]{2,1,0:T(8,128)(2,1)S(1)}, bf16[24,8,512]{2,1,0:T(8,128)(2,1)S(1)}) custom-call(s32[7]{0:T(128)S(1)} %convert_element_type.3.flags.refs_0_, bf16[16,32,512]{2,1,0:T(8,128)(2,1)S(1)} %copy-done, bf16[16,32,512]{2,1,0:T(8,128)(2,1)S(1)} %copy-done.1, bf16[8,32,512]{2,1,0:T(8,128)(2,1)S(1)} %collective-permute-done.halo_up.refs_4_, ...), custom_call_target="tpu_custom_call" | custom-call | flops 100000000 | bytes 1048576 | tf_op jit(solution)/shard_map/pallas_call | solution.py:296
  35.0 0.7 %collective-permute-start.6 = (bf16[24,8,512]{2,1,0:T(8,128)(2,1)S(1)}, bf16[24,8,512]{2,1,0:T(8,128)(2,1)S(1)}, u32[]{:S(2)}, u32[]{:S(2)}) collective-permute-start(bf16[24,8,512]{2,1,0:T(8,128)(2,1)S(1)} %get-tuple-element.10), channel_id=1, source_target_pairs={{1,2},{3,4},{5,6},{2,1},{4,3},{6,5},{9,10},{11,12},{13,14},{10,9},... | collective-permute-start | bytes 589832 | tf_op jit(solution)/shard_map/ppermute | solution.py:374
  35.7 0.1 collective-permute-start.7
  35.8 0.8 %shard_map.91 = (bf16[32,640]{1,0:T(8,128)(2,1)S(1)}, bf16[32,640]{1,0:T(8,128)(2,1)S(1)}) custom-call(s32[7]{0:T(128)S(1)} %convert_element_type.3.flags.refs_0_, bf16[64,640]{1,0:T(8,128)(2,1)S(1)} %get-tuple-element.13.own, bf16[64,640]{1,0:T(8,128)(2,1)S(1)} %collective-permute-done.13.other), custom_call_target="tpu_custom_call" | custom-call | flops 100000000 | bytes 1048576 | tf_op jit(solution)/shard_map/pallas_call | solution.py:296
  36.6 1.4 %collective-permute-start.14 = (bf16[32,640]{1,0:T(8,128)(2,1)S(1)}, bf16[32,640]{1,0:T(8,128)(2,1)S(1)}, u32[]{:S(2)}, u32[]{:S(2)}) collective-permute-start(bf16[32,640]{1,0:T(8,128)(2,1)S(1)} %get-tuple-element.16), channel_id=1, source_target_pairs={{0,2},{1,3},{2,0},{3,1},{4,6},{5,7},{6,4},{7,5},{8,10},{9,11},{10,... | collective-permute-start | bytes 122888 | tf_op jit(solution)/shard_map/ppermute | solution.py:319
  38.0 5.3 %shard_map.87 = (bf16[3,64,512]{2,1,0:T(8,128)(2,1)S(1)}, bf16[32,640]{1,0:T(8,128)(2,1)S(1)}) custom-call(s32[7]{0:T(128)S(1)} %convert_element_type.3.flags.refs_0_, bf16[16,32,512]{2,1,0:T(8,128)(2,1)S(1)} %copy-done.3, bf16[16,32,512]{2,1,0:T(8,128)(2,1)S(1)} %copy-done, bf16[16,32,512]{2,1,0:T(8,128)(2,1)S(1)} %copy-done.1, ...), custom_call_target="tpu_custom_call" | custom-call | flops 2000000000 | bytes 1048576 | tf_op jit(solution)/shard_map/pallas_call | solution.py:296
  43.3 0.8 %shard_map.92.own = bf16[32,640]{1,0:T(8,128)(2,1)S(1)} custom-call(s32[7]{0:T(128)S(1)} %convert_element_type.3.flags.refs_0_, bf16[32,640]{1,0:T(8,128)(2,1)S(1)} %get-tuple-element.15.own, bf16[32,640]{1,0:T(8,128)(2,1)S(1)} %collective-permute-done.14.other), custom_call_target="tpu_custom_call" | custom-call | flops 100000000 | bytes 1048576 | tf_op jit(solution)/shard_map/pallas_call | solution.py:296
  44.1 0.0 copy-start.2
  44.1 1.6 %collective-permute-start.15 = (bf16[32,640]{1,0:T(8,128)(2,1)S(1)}, bf16[32,640]{1,0:T(8,128)(2,1)S(1)}, u32[]{:S(2)}, u32[]{:S(2)}) collective-permute-start(bf16[32,640]{1,0:T(8,128)(2,1)S(1)} %shard_map.92.own), channel_id=1, source_target_pairs={{0,8},{8,0},{16,24},{24,16},{1,9},{9,1},{17,25},{25,17},{2,10},{10... | collective-permute-start | bytes 122888 | tf_op jit(solution)/shard_map/ppermute | solution.py:322
  45.7 4.3 %shard_map.88.refs_1_ = bf16[3,64,512]{2,1,0:T(8,128)(2,1)S(1)} custom-call(s32[7]{0:T(128)S(1)} %convert_element_type.3.flags.refs_0_, bf16[16,32,512]{2,1,0:T(8,128)(2,1)S(1)} %copy-done.3, bf16[16,32,512]{2,1,0:T(8,128)(2,1)S(1)} %copy-done, bf16[16,32,512]{2,1,0:T(8,128)(2,1)S(1)} %copy-done.1, ...), custom_call_target="tpu_custom_call" | custom-call | flops 2000000000 | bytes 1048576 | tf_op jit(solution)/shard_map/pallas_call | solution.py:296
  50.0 0.8 %shard_map.93.own = bf16[32,640]{1,0:T(8,128)(2,1)S(1)} custom-call(s32[7]{0:T(128)S(1)} %convert_element_type.3.flags.refs_0_, bf16[32,640]{1,0:T(8,128)(2,1)S(1)} %shard_map.92.own, bf16[32,640]{1,0:T(8,128)(2,1)S(1)} %collective-permute-done.15.other), custom_call_target="tpu_custom_call" | custom-call | flops 100000000 | bytes 1048576 | tf_op jit(solution)/shard_map/pallas_call | solution.py:296
  50.8 0.1 collective-permute-start.16
  51.0 4.5 %shard_map.89 = bf16[16,32,512]{2,1,0:T(8,128)(2,1)} custom-call(s32[7]{0:T(128)S(1)} %convert_element_type.3.flags.refs_0_, bf16[16,32,512]{2,1,0:T(8,128)(2,1)S(1)} %copy-done.3, bf16[16,32,512]{2,1,0:T(8,128)(2,1)S(1)} %copy-done, bf16[16,32,512]{2,1,0:T(8,128)(2,1)S(1)} %copy-done.1, bf16[8,32,512]{2,1,0:T(8,128)(2,1)S(1)} %collective-permute-done.halo_up.refs_4_, ...), custom_call_target="tpu_custom_call" | custom-call | flops 3000000000 | bytes 1048576 | tf_op jit(solution)/shard_map/pallas_call | solution.py:296
  55.5 1.7 %shard_map.94 = bf16[32,512]{1,0:T(8,128)(2,1)} custom-call(s32[7]{0:T(128)S(1)} %convert_element_type.3.flags.refs_0_, bf16[32,640]{1,0:T(8,128)(2,1)S(1)} %shard_map.93.own, bf16[32,640]{1,0:T(8,128)(2,1)S(1)} %collective-permute-done.16.other, bf16[32,640]{1,0:T(8,128)(2,1)S(1)} %get-tuple-element.17.extra, bf16[512,512]{1,0:T(8,128)(2,1)S(1)} %copy-done.2), custom_call_target="tpu_custom_call" | custom-call | flops 100000000 | bytes 1048576 | tf_op jit(solution)/shard_map/pallas_call | solution.py:296
  (29 shorter events, 0.2 us)
Async XLA Ops:
  0.6 9.5 %copy-start.1 = (bf16[16,32,512]{2,1,0:T(8,128)(2,1)S(1)}, bf16[16,32,512]{2,1,0:T(8,128)(2,1)}, u32[]{:S(2)}) copy-start(bf16[16,32,512]{2,1,0:T(8,128)(2,1)} %v_ref.3) | copy-start | bytes 1572868
  0.6 9.6 %collective-permute-start.10 = (bf16[32,512]{1,0:T(8,128)(2,1)}, bf16[32,512]{1,0:T(8,128)(2,1)S(1)}, u32[]{:S(2)}, u32[]{:S(2)}) collective-permute-start(bf16[32,512]{1,0:T(8,128)(2,1)} %refs_0_.1), channel_id=1, source_target_pairs={{0,6},{1,7},{2,4},{3,5},{4,2},{5,3},{6,0},{7,1},{8,14},{9,15},{10,... | collective-permute-start | bytes 98312 | tf_op jit(solution)/shard_map/ppermute | solution.py:319
  5.8 4.6 %collective-permute-start.8 = (bf16[32,512]{1,0:T(8,128)(2,1)}, bf16[32,512]{1,0:T(8,128)(2,1)S(1)}, u32[]{:S(2)}, u32[]{:S(2)}) collective-permute-start(bf16[32,512]{1,0:T(8,128)(2,1)} %refs_0_.1), channel_id=1, source_target_pairs={{0,2},{1,3},{2,0},{3,1},{4,6},{5,7},{6,4},{7,5},{8,10},{9,11},{10,... | collective-permute-start | bytes 98312 | tf_op jit(solution)/shard_map/ppermute | solution.py:319
  5.8 17.5 %collective-permute-start.11 = (bf16[16,32,512]{2,1,0:T(8,128)(2,1)}, bf16[16,32,512]{2,1,0:T(8,128)(2,1)S(1)}, u32[]{:S(2)}, u32[]{:S(2)}) collective-permute-start(bf16[16,32,512]{2,1,0:T(8,128)(2,1)} %k_ref.3), channel_id=1, source_target_pairs={{0,1},{1,0},{2,3},{3,2},{4,5},{5,4},{6,7},{7,6},{8,9},{9,8},{10,11... | collective-permute-start | bytes 1572872 | tf_op jit(solution)/shard_map/ppermute | solution.py:319
  5.8 17.5 %collective-permute-start.12 = (bf16[16,32,512]{2,1,0:T(8,128)(2,1)}, bf16[16,32,512]{2,1,0:T(8,128)(2,1)S(1)}, u32[]{:S(2)}, u32[]{:S(2)}) collective-permute-start(bf16[16,32,512]{2,1,0:T(8,128)(2,1)} %v_ref.3), channel_id=1, source_target_pairs={{0,1},{1,0},{2,3},{3,2},{4,5},{5,4},{6,7},{7,6},{8,9},{9,8},{10,11... | collective-permute-start | bytes 1572872 | tf_op jit(solution)/shard_map/ppermute | solution.py:319
  7.1 5.7 %collective-permute-start.2 = (bf16[2,32,512]{2,1,0:T(8,128)(2,1)S(1)}, bf16[2,32,512]{2,1,0:T(8,128)(2,1)S(1)}, u32[]{:S(2)}, u32[]{:S(2)}) collective-permute-start(bf16[2,32,512]{2,1,0:T(8,128)(2,1)S(1)} %get-tuple-element.23), channel_id=1, source_target_pairs={{0,2},{1,3},{2,0},{3,1},{4,6},{5,7},{6,4},{7,5},{8,10},{9,11},{10,... | collective-permute-start | bytes 196616 | tf_op jit(solution)/shard_map/ppermute | solution.py:319
  10.2 2.5 %copy-start.4 = (bf16[32,512]{1,0:T(8,128)(2,1)S(1)}, bf16[32,512]{1,0:T(8,128)(2,1)}, u32[]{:S(2)}) copy-start(bf16[32,512]{1,0:T(8,128)(2,1)} %refs_0_.1) | copy-start | bytes 98308
  10.2 8.2 %collective-permute-start.3 = (bf16[2,32,512]{2,1,0:T(8,128)(2,1)S(1)}, bf16[2,32,512]{2,1,0:T(8,128)(2,1)S(1)}, u32[]{:S(2)}, u32[]{:S(2)}) collective-permute-start(bf16[2,32,512]{2,1,0:T(8,128)(2,1)S(1)} %get-tuple-element.23), channel_id=1, source_target_pairs={{0,4},{1,5},{2,6},{3,7},{4,0},{5,1},{6,2},{7,3},{8,12},{9,13},{10,... | collective-permute-start | bytes 196616 | tf_op jit(solution)/shard_map/ppermute | solution.py:319
  10.3 11.5 %collective-permute-start.4 = (bf16[2,32,512]{2,1,0:T(8,128)(2,1)S(1)}, bf16[2,32,512]{2,1,0:T(8,128)(2,1)S(1)}, u32[]{:S(2)}, u32[]{:S(2)}) collective-permute-start(bf16[2,32,512]{2,1,0:T(8,128)(2,1)S(1)} %get-tuple-element.23), channel_id=1, source_target_pairs={{0,6},{1,7},{2,4},{3,5},{4,2},{5,3},{6,0},{7,1},{8,14},{9,15},{10,... | collective-permute-start | bytes 196616 | tf_op jit(solution)/shard_map/ppermute | solution.py:319
  12.7 10.6 %copy-start = (bf16[16,32,512]{2,1,0:T(8,128)(2,1)S(1)}, bf16[16,32,512]{2,1,0:T(8,128)(2,1)}, u32[]{:S(2)}) copy-start(bf16[16,32,512]{2,1,0:T(8,128)(2,1)} %k_ref.3) | copy-start | bytes 1572868
  12.7 10.5 %collective-permute-start.9 = (bf16[32,512]{1,0:T(8,128)(2,1)S(1)}, bf16[32,512]{1,0:T(8,128)(2,1)S(1)}, u32[]{:S(2)}, u32[]{:S(2)}) collective-permute-start(bf16[32,512]{1,0:T(8,128)(2,1)S(1)} %copy-done.4), channel_id=1, source_target_pairs={{0,4},{1,5},{2,6},{3,7},{4,0},{5,1},{6,2},{7,3},{8,12},{9,13},{10,... | collective-permute-start | bytes 98312 | tf_op jit(solution)/shard_map/ppermute | solution.py:319
  18.4 8.3 %collective-permute-start = (bf16[8,32,512]{2,1,0:T(8,128)(2,1)S(1)}, bf16[8,32,512]{2,1,0:T(8,128)(2,1)S(1)}, u32[]{:S(2)}, u32[]{:S(2)}) collective-permute-start(bf16[8,32,512]{2,1,0:T(8,128)(2,1)S(1)} %pad_maximum_fusion), channel_id=1, source_target_pairs={{0,8},{8,16},{16,24},{1,9},{9,17},{17,25},{2,10},{10,18},{18,26},{... | collective-permute-start | bytes 786440 | tf_op jit(solution)/shard_map/ppermute | solution.py:339
  21.8 12.5 %collective-permute-start.1 = (bf16[8,32,512]{2,1,0:T(8,128)(2,1)S(1)}, bf16[8,32,512]{2,1,0:T(8,128)(2,1)S(1)}, u32[]{:S(2)}, u32[]{:S(2)}) collective-permute-start(bf16[8,32,512]{2,1,0:T(8,128)(2,1)S(1)} %pad_maximum_fusion.1), channel_id=1, source_target_pairs={{8,0},{16,8},{24,16},{9,1},{17,9},{25,17},{10,2},{18,10},{26,18},{... | collective-permute-start | bytes 786440 | tf_op jit(solution)/shard_map/ppermute | solution.py:340
  23.2 14.8 %collective-permute-start.5 = (bf16[4,2,32,512]{3,2,1,0:T(8,128)(2,1)S(1)}, bf16[4,2,32,512]{3,2,1,0:T(8,128)(2,1)S(1)}, u32[]{:S(2)}, u32[]{:S(2)}) collective-permute-start(bf16[4,2,32,512]{3,2,1,0:T(8,128)(2,1)S(1)} %pad_maximum_fusion.2.refs_6_.gk_own), channel_id=1, source_target_pairs={{0,1},{1,0},{2,3},{3,2},{4,5},{5,4},{6,7},{7,6},{8,9},{9,8},{10,11... | collective-permute-start | bytes 786440 | tf_op jit(solution)/shard_map/ppermute | solution.py:319
  25.4 10.4 %collective-permute-start.13 = (bf16[64,640]{1,0:T(8,128)(2,1)S(1)}, bf16[64,640]{1,0:T(8,128)(2,1)S(1)}, u32[]{:S(2)}, u32[]{:S(2)}) collective-permute-start(bf16[64,640]{1,0:T(8,128)(2,1)S(1)} %get-tuple-element.14), channel_id=1, source_target_pairs={{0,4},{1,5},{2,6},{3,7},{4,0},{5,1},{6,2},{7,3},{8,12},{9,13},{10,... | collective-permute-start | bytes 245768 | tf_op jit(solution)/shard_map/ppermute | solution.py:319
  25.6 12.4 %copy-start.3 = (bf16[16,32,512]{2,1,0:T(8,128)(2,1)S(1)}, bf16[16,32,512]{2,1,0:T(8,128)(2,1)}, u32[]{:S(2)}) copy-start(bf16[16,32,512]{2,1,0:T(8,128)(2,1)} %q_ref.1) | copy-start | bytes 1572868
  35.0 15.9 %collective-permute-start.6 = (bf16[24,8,512]{2,1,0:T(8,128)(2,1)S(1)}, bf16[24,8,512]{2,1,0:T(8,128)(2,1)S(1)}, u32[]{:S(2)}, u32[]{:S(2)}) collective-permute-start(bf16[24,8,512]{2,1,0:T(8,128)(2,1)S(1)} %get-tuple-element.10), channel_id=1, source_target_pairs={{1,2},{3,4},{5,6},{2,1},{4,3},{6,5},{9,10},{11,12},{13,14},{10,9},... | collective-permute-start | bytes 589832 | tf_op jit(solution)/shard_map/ppermute | solution.py:374
  35.7 15.2 %collective-permute-start.7 = (bf16[24,8,512]{2,1,0:T(8,128)(2,1)S(1)}, bf16[24,8,512]{2,1,0:T(8,128)(2,1)S(1)}, u32[]{:S(2)}, u32[]{:S(2)}) collective-permute-start(bf16[24,8,512]{2,1,0:T(8,128)(2,1)S(1)} %get-tuple-element.11), channel_id=1, source_target_pairs={{0,1},{1,0},{2,3},{3,2},{4,5},{5,4},{6,7},{7,6},{8,9},{9,8},{10,11... | collective-permute-start | bytes 589832 | tf_op jit(solution)/shard_map/ppermute | solution.py:319
  36.6 6.7 %collective-permute-start.14 = (bf16[32,640]{1,0:T(8,128)(2,1)S(1)}, bf16[32,640]{1,0:T(8,128)(2,1)S(1)}, u32[]{:S(2)}, u32[]{:S(2)}) collective-permute-start(bf16[32,640]{1,0:T(8,128)(2,1)S(1)} %get-tuple-element.16), channel_id=1, source_target_pairs={{0,2},{1,3},{2,0},{3,1},{4,6},{5,7},{6,4},{7,5},{8,10},{9,11},{10,... | collective-permute-start | bytes 122888 | tf_op jit(solution)/shard_map/ppermute | solution.py:319
  44.1 6.8 %copy-start.2 = (bf16[512,512]{1,0:T(8,128)(2,1)S(1)}, bf16[512,512]{1,0:T(8,128)(2,1)}, u32[]{:S(2)}) copy-start(bf16[512,512]{1,0:T(8,128)(2,1)} %weight.3) | copy-start | bytes 1572868
  44.1 5.9 %collective-permute-start.15 = (bf16[32,640]{1,0:T(8,128)(2,1)S(1)}, bf16[32,640]{1,0:T(8,128)(2,1)S(1)}, u32[]{:S(2)}, u32[]{:S(2)}) collective-permute-start(bf16[32,640]{1,0:T(8,128)(2,1)S(1)} %shard_map.92.own), channel_id=1, source_target_pairs={{0,8},{8,0},{16,24},{24,16},{1,9},{9,1},{17,25},{25,17},{2,10},{10... | collective-permute-start | bytes 122888 | tf_op jit(solution)/shard_map/ppermute | solution.py:322
  50.8 4.6 %collective-permute-start.16 = (bf16[32,640]{1,0:T(8,128)(2,1)S(1)}, bf16[32,640]{1,0:T(8,128)(2,1)S(1)}, u32[]{:S(2)}, u32[]{:S(2)}) collective-permute-start(bf16[32,640]{1,0:T(8,128)(2,1)S(1)} %shard_map.93.own), channel_id=1, source_target_pairs={{0,16},{8,24},{16,0},{24,8},{1,17},{9,25},{17,1},{25,9},{2,18},{10... | collective-permute-start | bytes 122888 | tf_op jit(solution)/shard_map/ppermute | solution.py:322

commit v2 on v1

--- a/solution.py
+++ b/solution.py
@@ -14,6 +14,8 @@
 PAIR = 2 * HD
 STAT = 128
 NEG_FILL = -1e30
+VMEM_GRANT = 24 * 2**20
+PACK_GRANT = 56 * 2**20
 VMEM = pltpu.VMEM
 BF = jnp.bfloat16
 F32 = jnp.float32
@@ -53,19 +55,10 @@
     if round_top:
         top = top.astype(BF).astype(F32)
     weights = [jnp.exp(s - top).astype(BF) for s in scores]
-    outs = []
-    for head in range(2):
-        part = slice(head * n, head * n + n)
-        outs.append(
-            functools.reduce(
-                jnp.add, [dot_nn(w[part], with_ones(v)) for w, v in zip(weights, vals)]
-            )
-        )
-    totals = [o[:, PAIR:] for o in outs]
+    out = functools.reduce(jnp.add, [dot_nn(w, with_ones(v)) for w, v in zip(weights, vals)])
+    totals = (out[:n, PAIR:], out[n:, PAIR:])
     low = low_half((n, PAIR))
-    attended = jnp.where(low, outs[0][:, :PAIR], outs[1][:, :PAIR]) / jnp.where(
-        low, totals[0], totals[1]
-    )
+    attended = jnp.where(low, out[:n, :PAIR], out[n:, :PAIR]) / jnp.where(low, *totals)
     return attended, (top[:n], top[n:]), totals
 
 
@@ -91,58 +84,73 @@
         start += ref.shape[0]
 
 
+def pack_first_kernel(k_ref, v_ref, gq, gk, gv, up_ref, down_ref, glob_ref, both_ref, sems):
+    last = k_ref.shape[0] - RAD
+    moves = [(ref, glob_ref.at[i]) for i, ref in enumerate((gq, gk, gv))]
+    for i, ref in enumerate((k_ref, v_ref)):
+        rows = pl.ds(i * RAD, RAD)
+        moves.append((ref.at[pl.ds(last, RAD)], up_ref.at[rows]))
+        moves.append((ref.at[pl.ds(0, RAD)], down_ref.at[rows]))
+        moves.append((ref, both_ref.at[i]))
+    copies = [pltpu.make_async_copy(*move, sems.at[i]) for i, move in enumerate(moves)]
+    for copy in copies:
+        copy.start()
+    for copy in copies:
+        copy.wait()
+
+
 def global_kernel(pieces, *refs):
-    q = jnp.concatenate([refs[i][...] for i in range(pieces)], 0)
-    ka, kb, va, vb = refs[pieces : pieces + 4]
-    partial_softmax(q, [ka, kb], [va, vb], refs[pieces + 4 :])
-
-
-def spread(stat_lanes):
-    n = stat_lanes.shape[0]
-    upper = stat_lanes.astype(BF)
-    lower = (stat_lanes - upper.astype(F32)).astype(BF)
-    source = lax.broadcasted_iota(jnp.int32, (STAT, H * HD), 0) - H
-    target = lax.broadcasted_iota(jnp.int32, (STAT, H * HD), 1) // HD
+    gq, gk, gv, k_ref, v_ref, facing = refs[:6]
+    others, outs, kv_ref = refs[6 : pieces + 5], refs[pieces + 5 : -1], refs[-1]
+    kv_ref[0, 0], kv_ref[0, 1] = gk[...], gv[...]
+    for i, ref in enumerate(others):
+        kv_ref[i + 1] = ref[1:]
+    q = jnp.concatenate([gq[...]] + [ref[0] for ref in others], 0)
+    tokens = k_ref.shape[0] * k_ref.shape[1]
+    keys, vals = [
+        [x.reshape(tokens, -1) for x in (own[...], facing[i])] for i, own in enumerate((k_ref, v_ref))
+    ]
+    partial_softmax(q, keys, vals, outs)
+
+
+def spread(stats):
+    upper = stats.astype(BF)
+    lower = (stats - upper.astype(F32)).astype(BF)
+    source = lax.broadcasted_iota(jnp.int32, (2 * STAT, H * HD), 0) % STAT - H
+    target = lax.broadcasted_iota(jnp.int32, (2 * STAT, H * HD), 1) // HD
     pick = (source == target).astype(BF)
-    return dot_nn(upper, pick) + dot_nn(lower, pick)
-
-
-def merge(first, second):
-    width = H * HD
-    lane = lax.broadcasted_iota(jnp.int32, (first.shape[0], STAT), 1)
-    stats = [x[:, width:].astype(F32) for x in (first, second)]
-    top = jnp.maximum(stats[0], stats[1])
-    mass = [s * pltpu.roll(jnp.exp(s - top), H, 1) for s in stats]
-    total = mass[0] + mass[1]
+    return dot_nn(jnp.concatenate([upper, lower], 1), pick)
+
+
+def merge(parts):
+    width, n = H * HD, parts[0].shape[0]
+    lane = lax.broadcasted_iota(jnp.int32, (n, STAT), 1)
+    stats = [x[:, width:].astype(F32) for x in parts]
+    top = functools.reduce(jnp.maximum, stats)
     held = (lane >= H) & (lane < 2 * H)
-    safe = jnp.where(held, total, 1.0)
-    shares = [spread(jnp.where(held, m, 0.0) / safe) for m in mass]
-    out = first[:, :width].astype(F32) * shares[0] + second[:, :width].astype(F32) * shares[1]
-    return out, jnp.where(lane < H, top, jnp.where(held, total, 0.0))
-
-
-def ordered(flag_ref, index, own, other):
-    mine_first = flag_ref[index] == 0
-    return jnp.where(mine_first, own, other), jnp.where(mine_first, other, own)
-
-
-def merge_kernel(flag_index, flags, own, other, *outs):
-    a, b = own[...], other[...]
-    if flag_index is not None:
-        a, b = ordered(flags, flag_index, a, b)
-    out, stats = merge(a, b)
-    full = jnp.concatenate([out.astype(BF), stats.astype(BF)], 1)
-    start = 0
-    for ref in outs:
-        ref[...] = full[start : start + ref.shape[0]]
-        start += ref.shape[0]
-
-
-def last_merge_kernel(flag_index, flags, own, other, extra, weight, out_ref):
-    a, b = ordered(flags, flag_index, own[...], other[...])
-    out, stats = merge(a, b)
-    both = jnp.concatenate([out, stats], 1)
-    out, _ = merge(both, extra[...].astype(F32))
+    mass = [jnp.where(held, s * pltpu.roll(jnp.exp(s - top), H, 1), 0.0) for s in stats]
+    total = functools.reduce(jnp.add, mass)
+    inverse = 1.0 / jnp.where(held, total, 1.0)
+    shares = spread(jnp.concatenate([m * inverse for m in mass], 0))
+    out = functools.reduce(
+        jnp.add,
+        [x[:, :width].astype(F32) * shares[i * n : (i + 1) * n] for i, x in enumerate(parts)],
+    )
+    return out, jnp.where(lane < H, top, total)
+
+
+def merge_kernel(*refs):
+    out, stats = merge([ref[...] for ref in refs[:-1]])
+    refs[-1][...] = jnp.concatenate([out.astype(BF), stats.astype(BF)], 1)
+
+
+def last_merge_kernel(first_flag, flags, *refs):
+    *ins, extra, weight, out_ref = refs
+    parts = [ref[...] for ref in ins]
+    for b in range(len(parts).bit_length() - 1):
+        swap = flags[first_flag + b] != 0
+        parts = [jnp.where(swap, parts[m ^ (1 << b)], part) for m, part in enumerate(parts)]
+    out, _ = merge([*parts, extra[...]])
     out_ref[...] = dot_nn(out.astype(BF), weight[...]).astype(BF)
 
 
@@ -188,7 +196,6 @@
     own_keys = gk_own.shape[0] // 2
     bias = window_bias(flags, block, blocks, False)
     out_ref = refs[-2] if own_part else refs[-1]
-    halves = RAD
     gks, gvs = global_views(gk_own, gk_other)
     for p in range(H // 2):
         lanes = slice(p * PAIR, (p + 1) * PAIR)
@@ -298,14 +305,13 @@
         out_shape=[jax.ShapeDtypeStruct(s, BF) for s in out_shapes],
         in_specs=specs,
         out_specs=[pl.BlockSpec(memory_space=VMEM)] * len(out_shapes),
-        compiler_params=pltpu.CompilerParams(vmem_limit_bytes=48 * 2**20),
+        compiler_params=pltpu.CompilerParams(vmem_limit_bytes=VMEM_GRANT),
         cost_estimate=pl.CostEstimate(flops=flops, bytes_accessed=2**20, transcendentals=0),
     )(*inputs)
 
 
 def body(queries, grid_keys, values, glob_queries, glob_keys, glob_values, out_weight):
     rows, cols, width = queries.shape
-    tokens = rows * cols
     own = glob_queries.shape[0]
     stations, across = lax.axis_size("station"), lax.axis_size("tm")
     chips = across // 2
@@ -313,7 +319,6 @@
     blocks = rows // SIDE
     station, column = lax.axis_index("station"), lax.axis_index("tm")
     station_bits = [1 << b for b in range(stations.bit_length() - 1)]
-    chip_bits = [1 << b for b in range(chips.bit_length() - 1)]
 
     def over_tm(x, mask):
         return lax.ppermute(x, "tm", [(i, i ^ mask) for i in range(across)])
@@ -334,22 +339,30 @@
 
     up = [(i, i + 1) for i in range(stations - 1)]
     down = [(j, i) for i, j in up]
-    other_keys, other_vals = over_tm(grid_keys, 1), over_tm(values, 1)
-    q_pieces = [glob_queries] + [over_tm(glob_queries, 2 * m) for m in range(1, chips)]
-    halo_up = lax.ppermute(jnp.concatenate([grid_keys[rows - RAD :], values[rows - RAD :]], 0), "station", up)
-    halo_down = lax.ppermute(jnp.concatenate([grid_keys[:RAD], values[:RAD]], 0), "station", down)
-    kv = jnp.stack([glob_keys, glob_values])
-    kv_own = jnp.stack([kv] + [over_tm(kv, 2 * m) for m in range(1, chips)])
+    to_up, to_down, glob, both = pl.pallas_call(
+        pack_first_kernel,
+        out_shape=[
+            jax.ShapeDtypeStruct(shape, BF)
+            for shape in [(2 * RAD, cols, width)] * 2 + [(3, own, width), (2, rows, cols, width)]
+        ],
+        in_specs=[pl.BlockSpec(memory_space=pltpu.HBM)] * 5,
+        out_specs=[pl.BlockSpec(memory_space=VMEM)] * 4,
+        scratch_shapes=[pltpu.SemaphoreType.DMA((9,))],
+        compiler_params=pltpu.CompilerParams(vmem_limit_bytes=PACK_GRANT),
+        cost_estimate=pl.CostEstimate(flops=10**6, bytes_accessed=2**20, transcendentals=0),
+    )(grid_keys, values, glob_queries, glob_keys, glob_values)
+    halo_up = lax.ppermute(to_up, "station", up)
+    halo_down = lax.ppermute(to_down, "station", down)
+    facing_block = over_tm(both, 1)
+    pieces = [over_tm(glob, 2 * m) for m in range(1, chips)]
+
+    *parts, kv_own = call(
+        functools.partial(global_kernel, chips),
+        [glob_queries, glob_keys, glob_values, grid_keys, values, facing_block, *pieces],
+        [(own, payload)] * chips + [(chips, 2, own, width)],
+        2 * 10**9,
+    )
     kv_other = over_tm(kv_own, 1)
-
-    flat = [x.reshape(tokens, width) for x in (grid_keys, other_keys, values, other_vals)]
-    half = chips * own // 2
-    kept, sent = call(
-        functools.partial(global_kernel, chips),
-        [*q_pieces, *flat],
-        [(half, payload)] * 2,
-        2 * 10**9,
-    )
     shared = [queries, grid_keys, values, halo_up, halo_down, kv_own, kv_other]
     inner_shape = (cols // SIDE - 1, SIDE * SIDE, width)
     first_block, extra = call(
@@ -381,27 +394,16 @@
         flags,
     )
 
-    for bit in reversed(chip_bits):
-        arrived = over_tm(sent, 2 * bit)
-        split = [(half // 2, payload)] * 2 if bit > 1 else [(half, payload)]
-        merged = call(functools.partial(merge_kernel, None), [kept, arrived], split, 10**8, flags)
-        kept, sent = merged if bit > 1 else (merged[0], None)
-        half //= 2
-    first_flag = 5
-    for i, bit in enumerate(station_bits):
-        arrived = over_station(kept, bit)
-        if i < len(station_bits) - 1:
-            (kept,) = call(
-                functools.partial(merge_kernel, first_flag + i), [kept, arrived], [(own, payload)], 10**8, flags
-            )
-        else:
-            (glob_output,) = call(
-                functools.partial(last_merge_kernel, first_flag + i),
-                [kept, arrived, extra, out_weight],
-                [(own, width)],
-                10**8,
-                flags,
-            )
+    parts = parts[:1] + [over_tm(part, 2 * m) for m, part in enumerate(parts) if m]
+    (merged,) = call(merge_kernel, parts, [(own, payload)], 10**8)
+    parts = [merged] + [over_station(merged, m) for m in range(1, stations)]
+    (glob_output,) = call(
+        functools.partial(last_merge_kernel, 5),
+        [*parts, extra, out_weight],
+        [(own, width)],
+        10**8,
+        flags,
+    )
     return grid_output, glob_output
 
 

time: 57.4 us -> 42.3 us (0.74)
  waiting for transfers between devices: 13.4 us -> 5.39 us
  Pallas kernels: 21 us -> 14.2 us
  starting transfers between devices: 19.8 us -> 21.5 us
  local copies, waits for them, and re-layouts: 1.13 us -> 0.14 us
  other arithmetic: 0.88 us -> 0.01 us
    pallas_call x9 -> x7, Pallas kernels: 21 us -> 11.4 us  [call(): pl.pallas_call(kernel, out_shape=[jax.ShapeDtypeStruct(s, BF) for s in ou...]
    ppermute x2, waiting for transfers between devices: 8.74 us -> 1.93 us  [the longest x1 1.93 us: body(): halo_down = lax.ppermute(to_down, 'station', down)]
    pallas_call x0 -> x1, Pallas kernels: none -> 2.83 us  [body(): pl.pallas_call(pack_first_kernel, out_shape=[jax.ShapeDtypeStruct(shape,...]
    ppermute x2 -> x3, starting transfers between devices: 1.63 us -> 3.55 us  [over_station(): return lax.ppermute(x, 'station', [(i, i ^ mask) for i in range(stations)])]
    ppermute x12 -> x9, waiting for transfers between devices: 4.62 us -> 3.45 us  [over_tm(): return lax.ppermute(x, 'tm', [(i, i ^ mask) for i in range(across)])]
    slice x2 -> x0, local copies, waits for them, and re-layouts: 1 us -> none  [the longest x1 0.98 us: body(): grid_keys[:RAD]]
    another operation x2 -> x0, other arithmetic: 0.82 us -> none  [body(): kv_own = jnp.stack([kv] + [over_tm(kv, 2 * m) for m in range(1, chips)])]
    ppermute x12 -> x9, starting transfers between devices: 12.8 us -> 12.3 us  [over_tm(): return lax.ppermute(x, 'tm', [(i, i ^ mask) for i in range(across)])]
  transfers between devices with their start and end apart: 17 -> 15, of which waited for: 3 -> 2; matrix products, arithmetic and copies ran while one was open for 3% -> 0% of each run, Pallas kernels for 34% -> 23%
where the time goes in v2:
time: 42.3 us; the launch traced here: 42.1 us
  starting transfers between devices  21.5 us (51%)
  Pallas kernels  14.2 us (34%)
  waiting for transfers between devices  5.39 us (13%)
  between operations  0.84 us (2%)
    ppermute x9, starting transfers between devices, over_tm(): return lax.ppermute(x, 'tm', [(i, i ^ mask) for i in range(across)])  12.3 us
    pallas_call x7, Pallas kernels, call(): pl.pallas_call(kernel, out_shape=[jax.ShapeDtypeStruct(s, BF) for s in ou...  11.4 us
    ppermute x1, starting transfers between devices, body(): halo_up = lax.ppermute(to_up, 'station', up)  3.62 us
    ppermute x3, starting transfers between devices, over_station(): return lax.ppermute(x, 'station', [(i, i ^ mask) for i in range(stations)])  3.55 us
    ppermute x9, waiting for transfers between devices, over_tm(): return lax.ppermute(x, 'tm', [(i, i ^ mask) for i in range(across)])  3.45 us
    pallas_call x1, Pallas kernels, body(): pl.pallas_call(pack_first_kernel, out_shape=[jax.ShapeDtypeStruct(shape,...  2.83 us
    ppermute x1, waiting for transfers between devices, body(): halo_down = lax.ppermute(to_down, 'station', down)  1.93 us
    ppermute x1, starting transfers between devices, body(): halo_down = lax.ppermute(to_down, 'station', down)  1.29 us
  transfers between devices with their start and end apart: 15, of which 2 were waited for; matrix products, arithmetic and copies ran while one was open for 0% of the time, Pallas kernels for 23%

profile of v2, /device:TPU:0, one launch (start us, length us, event | category | flops | bytes accessed | tf_op | source)
XLA Modules:
  0.0 42.1 jit_solution(15082154303150072823)
XLA Ops:
  0.7 2.8 %shard_map.86 = (bf16[8,32,512]{2,1,0:T(8,128)(2,1)}, bf16[8,32,512]{2,1,0:T(8,128)(2,1)}, bf16[3,32,512]{2,1,0:T(8,128)(2,1)}, bf16[2,16,32,512]{3,2,1,0:T(8,128)(2,1)}) custom-call(bf16[16,32,512]{2,1,0:T(8,128)(2,1)} %k_ref.5, bf16[16,32,512]{2,1,0:T(8,128)(2,1)} %v_ref.5, bf16[32,512]{1,0:T(8,128)(2,1)} %refs_8_.1, bf16[32,512]{1,0:T(8,128)(2,1)} %refs_1_.3, ...), custom_call_target="tpu_custom_call" | custom-call | flops 1000000 | bytes 1048576 | tf_op jit(solution)/shard_map/pallas_call | solution.py:342
  3.5 0.5 %collective-permute-start.2 = (bf16[2,16,32,512]{3,2,1,0:T(8,128)(2,1)}, bf16[2,16,32,512]{3,2,1,0:T(8,128)(2,1)S(1)}, u32[]{:S(2)}, u32[]{:S(2)}) collective-permute-start(bf16[2,16,32,512]{3,2,1,0:T(8,128)(2,1)} %get-tuple-element.17), channel_id=1, source_target_pairs={{0,1},{1,0},{2,3},{3,2},{4,5},{5,4},{6,7},{7,6},{8,9},{9,8},{10,11... | collective-permute-start | bytes 3145736 | tf_op jit(solution)/shard_map/ppermute | solution.py:324
  4.0 2.6 %collective-permute-start.3 = (bf16[3,32,512]{2,1,0:T(8,128)(2,1)}, bf16[3,32,512]{2,1,0:T(8,128)(2,1)S(1)}, u32[]{:S(2)}, u32[]{:S(2)}) collective-permute-start(bf16[3,32,512]{2,1,0:T(8,128)(2,1)} %get-tuple-element.18), channel_id=1, source_target_pairs={{0,2},{1,3},{2,0},{3,1},{4,6},{5,7},{6,4},{7,5},{8,10},{9,11},{10,... | collective-permute-start | bytes 294920 | tf_op jit(solution)/shard_map/ppermute | solution.py:324
  6.7 2.6 %collective-permute-start.4 = (bf16[3,32,512]{2,1,0:T(8,128)(2,1)}, bf16[3,32,512]{2,1,0:T(8,128)(2,1)S(1)}, u32[]{:S(2)}, u32[]{:S(2)}) collective-permute-start(bf16[3,32,512]{2,1,0:T(8,128)(2,1)} %get-tuple-element.18), channel_id=1, source_target_pairs={{0,4},{1,5},{2,6},{3,7},{4,0},{5,1},{6,2},{7,3},{8,12},{9,13},{10,... | collective-permute-start | bytes 294920 | tf_op jit(solution)/shard_map/ppermute | solution.py:324
  9.3 3.6 %collective-permute-start = (bf16[8,32,512]{2,1,0:T(8,128)(2,1)}, bf16[8,32,512]{2,1,0:T(8,128)(2,1)S(1)}, u32[]{:S(2)}, u32[]{:S(2)}) collective-permute-start(bf16[8,32,512]{2,1,0:T(8,128)(2,1)} %get-tuple-element.15), channel_id=1, source_target_pairs={{0,8},{8,16},{16,24},{1,9},{9,17},{17,25},{2,10},{10,18},{18,26},{... | collective-permute-start | bytes 786440 | tf_op jit(solution)/shard_map/ppermute | solution.py:354
  12.9 1.3 %collective-permute-start.1 = (bf16[8,32,512]{2,1,0:T(8,128)(2,1)}, bf16[8,32,512]{2,1,0:T(8,128)(2,1)S(1)}, u32[]{:S(2)}, u32[]{:S(2)}) collective-permute-start(bf16[8,32,512]{2,1,0:T(8,128)(2,1)} %get-tuple-element.16), channel_id=1, source_target_pairs={{8,0},{16,8},{24,16},{9,1},{17,9},{25,17},{10,2},{18,10},{26,18},{... | collective-permute-start | bytes 786440 | tf_op jit(solution)/shard_map/ppermute | solution.py:355
  14.2 3.4 %collective-permute-done.4.refs_7_ = bf16[3,32,512]{2,1,0:T(8,128)(2,1)S(1)} collective-permute-done((bf16[3,32,512]{2,1,0:T(8,128)(2,1)}, bf16[3,32,512]{2,1,0:T(8,128)(2,1)S(1)}, u32[]{:S(2)}, u32[]{:S(2)}) %collective-permute-start.4) | collective-permute-done | bytes 98336 | tf_op jit(solution)/shard_map/ppermute | solution.py:324
  17.6 0.0 collective-permute-done.2.refs_5_
  17.7 1.7 %shard_map.87 = (bf16[32,640]{1,0:T(8,128)(2,1)S(1)}, bf16[32,640]{1,0:T(8,128)(2,1)S(1)}, bf16[32,640]{1,0:T(8,128)(2,1)S(1)}, bf16[32,640]{1,0:T(8,128)(2,1)S(1)}, bf16[4,2,32,512]{3,2,1,0:T(8,128)(2,1)S(1)}) custom-call(bf16[32,512]{1,0:T(8,128)(2,1)S(1)} %copy-done.5, bf16[32,512]{1,0:T(8,128)(2,1)S(1)} %copy-done.3, bf16[32,512]{1,0:T(8,128)(2,1)S(1)} %copy-done.4, ...), custom_call_target="tpu_custom_call" | custom-call | flops 2000000000 | bytes 1048576 | tf_op jit(solution)/shard_map/pallas_call | solution.py:303
  19.4 0.1 collective-permute-start.6
  19.5 2.0 %collective-permute-start.9 = (bf16[32,640]{1,0:T(8,128)(2,1)S(1)}, bf16[32,640]{1,0:T(8,128)(2,1)S(1)}, u32[]{:S(2)}, u32[]{:S(2)}) collective-permute-start(bf16[32,640]{1,0:T(8,128)(2,1)S(1)} %get-tuple-element.24), channel_id=1, source_target_pairs={{0,2},{1,3},{2,0},{3,1},{4,6},{5,7},{6,4},{7,5},{8,10},{9,11},{10,... | collective-permute-start | bytes 122888 | tf_op jit(solution)/shard_map/ppermute | solution.py:324
  21.5 1.2 %collective-permute-start.10 = (bf16[32,640]{1,0:T(8,128)(2,1)S(1)}, bf16[32,640]{1,0:T(8,128)(2,1)S(1)}, u32[]{:S(2)}, u32[]{:S(2)}) collective-permute-start(bf16[32,640]{1,0:T(8,128)(2,1)S(1)} %get-tuple-element.25), channel_id=1, source_target_pairs={{0,4},{1,5},{2,6},{3,7},{4,0},{5,1},{6,2},{7,3},{8,12},{9,13},{10,... | collective-permute-start | bytes 122888 | tf_op jit(solution)/shard_map/ppermute | solution.py:324
  22.7 0.0 collective-permute-done.halo_up.refs_4_
  22.7 1.3 %collective-permute-start.11 = (bf16[32,640]{1,0:T(8,128)(2,1)S(1)}, bf16[32,640]{1,0:T(8,128)(2,1)S(1)}, u32[]{:S(2)}, u32[]{:S(2)}) collective-permute-start(bf16[32,640]{1,0:T(8,128)(2,1)S(1)} %get-tuple-element.26), channel_id=1, source_target_pairs={{0,6},{1,7},{2,4},{3,5},{4,2},{5,3},{6,0},{7,1},{8,14},{9,15},{10,... | collective-permute-start | bytes 122888 | tf_op jit(solution)/shard_map/ppermute | solution.py:324
  24.0 0.1 stack.31
  24.1 1.9 %collective-permute-done.1.halo_down.refs_5_ = bf16[8,32,512]{2,1,0:T(8,128)(2,1)S(1)} collective-permute-done((bf16[8,32,512]{2,1,0:T(8,128)(2,1)}, bf16[8,32,512]{2,1,0:T(8,128)(2,1)S(1)}, u32[]{:S(2)}, u32[]{:S(2)}) %collective-permute-start.1) | collective-permute-done | bytes 262176 | tf_op jit(solution)/shard_map/ppermute | solution.py:355
  26.0 0.7 %shard_map.88 = (bf16[24,8,512]{2,1,0:T(8,128)(2,1)S(1)}, bf16[24,8,512]{2,1,0:T(8,128)(2,1)S(1)}) custom-call(s32[7]{0:T(128)S(1)} %convert_element_type.3.flags.refs_0_, bf16[16,32,512]{2,1,0:T(8,128)(2,1)S(1)} %copy-done, bf16[16,32,512]{2,1,0:T(8,128)(2,1)S(1)} %copy-done.1, bf16[8,32,512]{2,1,0:T(8,128)(2,1)S(1)} %collective-permute-done.halo_up.refs_4_, ...), custom_call_target="tpu_custom_call" | custom-call | flops 100000000 | bytes 1048576 | tf_op jit(solution)/shard_map/pallas_call | solution.py:303
  26.7 0.7 %collective-permute-start.7 = (bf16[24,8,512]{2,1,0:T(8,128)(2,1)S(1)}, bf16[24,8,512]{2,1,0:T(8,128)(2,1)S(1)}, u32[]{:S(2)}, u32[]{:S(2)}) collective-permute-start(bf16[24,8,512]{2,1,0:T(8,128)(2,1)S(1)} %get-tuple-element.20), channel_id=1, source_target_pairs={{1,2},{3,4},{5,6},{2,1},{4,3},{6,5},{9,10},{11,12},{13,14},{10,9},... | collective-permute-start | bytes 589832 | tf_op jit(solution)/shard_map/ppermute | solution.py:387
  27.4 0.0 collective-permute-done.9.refs_1_
  27.4 2.0 %collective-permute-start.8 = (bf16[24,8,512]{2,1,0:T(8,128)(2,1)S(1)}, bf16[24,8,512]{2,1,0:T(8,128)(2,1)S(1)}, u32[]{:S(2)}, u32[]{:S(2)}) collective-permute-start(bf16[24,8,512]{2,1,0:T(8,128)(2,1)S(1)} %get-tuple-element.21), channel_id=1, source_target_pairs={{0,1},{1,0},{2,3},{3,2},{4,5},{5,4},{6,7},{7,6},{8,9},{9,8},{10,11... | collective-permute-start | bytes 589832 | tf_op jit(solution)/shard_map/ppermute | solution.py:324
  29.5 0.0 collective-permute-done.10.refs_2_
  29.5 0.0 collective-permute-done.11.refs_3_
  29.5 0.3 shard_map.92.refs_0_
  29.7 1.6 %collective-permute-start.12 = (bf16[32,640]{1,0:T(8,128)(2,1)S(1)}, bf16[32,640]{1,0:T(8,128)(2,1)S(1)}, u32[]{:S(2)}, u32[]{:S(2)}) collective-permute-start(bf16[32,640]{1,0:T(8,128)(2,1)S(1)} %shard_map.92.refs_0_), channel_id=1, source_target_pairs={{0,8},{8,0},{16,24},{24,16},{1,9},{9,1},{17,25},{25,17},{2,10},{10... | collective-permute-start | bytes 122888 | tf_op jit(solution)/shard_map/ppermute | solution.py:327
  31.3 0.6 %collective-permute-start.13 = (bf16[32,640]{1,0:T(8,128)(2,1)S(1)}, bf16[32,640]{1,0:T(8,128)(2,1)S(1)}, u32[]{:S(2)}, u32[]{:S(2)}) collective-permute-start(bf16[32,640]{1,0:T(8,128)(2,1)S(1)} %shard_map.92.refs_0_), channel_id=1, source_target_pairs={{0,16},{8,24},{16,0},{24,8},{1,17},{9,25},{17,1},{25,9},{2,18},{10... | collective-permute-start | bytes 122888 | tf_op jit(solution)/shard_map/ppermute | solution.py:327
  31.9 1.4 %collective-permute-start.14 = (bf16[32,640]{1,0:T(8,128)(2,1)S(1)}, bf16[32,640]{1,0:T(8,128)(2,1)S(1)}, u32[]{:S(2)}, u32[]{:S(2)}) collective-permute-start(bf16[32,640]{1,0:T(8,128)(2,1)S(1)} %shard_map.92.refs_0_), channel_id=1, source_target_pairs={{0,24},{8,16},{16,8},{24,0},{1,25},{9,17},{17,9},{25,1},{2,26},{10... | collective-permute-start | bytes 122888 | tf_op jit(solution)/shard_map/ppermute | solution.py:327
  33.3 2.1 %shard_map.89 = (bf16[3,64,512]{2,1,0:T(8,128)(2,1)S(1)}, bf16[32,640]{1,0:T(8,128)(2,1)S(1)}) custom-call(s32[7]{0:T(128)S(1)} %convert_element_type.3.flags.refs_0_, bf16[16,32,512]{2,1,0:T(8,128)(2,1)S(1)} %copy-done.6, bf16[16,32,512]{2,1,0:T(8,128)(2,1)S(1)} %copy-done, bf16[16,32,512]{2,1,0:T(8,128)(2,1)S(1)} %copy-done.1, ...), custom_call_target="tpu_custom_call" | custom-call | flops 2000000000 | bytes 1048576 | tf_op jit(solution)/shard_map/pallas_call | solution.py:303
  35.4 0.0 copy-start.2
  35.4 1.8 %shard_map.90.refs_1_ = bf16[3,64,512]{2,1,0:T(8,128)(2,1)S(1)} custom-call(s32[7]{0:T(128)S(1)} %convert_element_type.3.flags.refs_0_, bf16[16,32,512]{2,1,0:T(8,128)(2,1)S(1)} %copy-done.6, bf16[16,32,512]{2,1,0:T(8,128)(2,1)S(1)} %copy-done, bf16[16,32,512]{2,1,0:T(8,128)(2,1)S(1)} %copy-done.1, ...), custom_call_target="tpu_custom_call" | custom-call | flops 2000000000 | bytes 1048576 | tf_op jit(solution)/shard_map/pallas_call | solution.py:303
  37.2 0.0 collective-permute-done.8.inner_ref
  37.2 3.3 %shard_map.91 = bf16[16,32,512]{2,1,0:T(8,128)(2,1)} custom-call(s32[7]{0:T(128)S(1)} %convert_element_type.3.flags.refs_0_, bf16[16,32,512]{2,1,0:T(8,128)(2,1)S(1)} %copy-done.6, bf16[16,32,512]{2,1,0:T(8,128)(2,1)S(1)} %copy-done, bf16[16,32,512]{2,1,0:T(8,128)(2,1)S(1)} %copy-done.1, bf16[8,32,512]{2,1,0:T(8,128)(2,1)S(1)} %collective-permute-done.halo_up.refs_4_, ...), custom_call_target="tpu_custom_call" | custom-call | flops 3000000000 | bytes 1048576 | tf_op jit(solution)/shard_map/pallas_call | solution.py:303
  40.5 1.6 %shard_map.93 = bf16[32,512]{1,0:T(8,128)(2,1)} custom-call(s32[7]{0:T(128)S(1)} %convert_element_type.3.flags.refs_0_, bf16[32,640]{1,0:T(8,128)(2,1)S(1)} %shard_map.92.refs_0_, bf16[32,640]{1,0:T(8,128)(2,1)S(1)} %collective-permute-done.12.refs_1_, bf16[32,640]{1,0:T(8,128)(2,1)S(1)} %collective-permute-done.13.refs_2_, ...), custom_call_target="tpu_custom_call" | custom-call | flops 100000000 | bytes 1048576 | tf_op jit(solution)/shard_map/pallas_call | solution.py:303
  (22 shorter events, 0.1 us)
Async XLA Ops:
  0.6 17.0 %copy-start = (bf16[16,32,512]{2,1,0:T(8,128)(2,1)S(1)}, bf16[16,32,512]{2,1,0:T(8,128)(2,1)}, u32[]{:S(2)}) copy-start(bf16[16,32,512]{2,1,0:T(8,128)(2,1)} %k_ref.5) | copy-start | bytes 1572868
  0.6 17.0 %copy-start.1 = (bf16[16,32,512]{2,1,0:T(8,128)(2,1)S(1)}, bf16[16,32,512]{2,1,0:T(8,128)(2,1)}, u32[]{:S(2)}) copy-start(bf16[16,32,512]{2,1,0:T(8,128)(2,1)} %v_ref.5) | copy-start | bytes 1572868
  0.7 17.0 %copy-start.5 = (bf16[32,512]{1,0:T(8,128)(2,1)S(1)}, bf16[32,512]{1,0:T(8,128)(2,1)}, u32[]{:S(2)}) copy-start(bf16[32,512]{1,0:T(8,128)(2,1)} %refs_8_.1) | copy-start | bytes 98308
  0.7 17.0 %copy-start.3 = (bf16[32,512]{1,0:T(8,128)(2,1)S(1)}, bf16[32,512]{1,0:T(8,128)(2,1)}, u32[]{:S(2)}) copy-start(bf16[32,512]{1,0:T(8,128)(2,1)} %refs_1_.3) | copy-start | bytes 98308
  0.7 17.0 %copy-start.4 = (bf16[32,512]{1,0:T(8,128)(2,1)S(1)}, bf16[32,512]{1,0:T(8,128)(2,1)}, u32[]{:S(2)}) copy-start(bf16[32,512]{1,0:T(8,128)(2,1)} %refs_2_.3) | copy-start | bytes 98308
  3.5 14.1 %collective-permute-start.2 = (bf16[2,16,32,512]{3,2,1,0:T(8,128)(2,1)}, bf16[2,16,32,512]{3,2,1,0:T(8,128)(2,1)S(1)}, u32[]{:S(2)}, u32[]{:S(2)}) collective-permute-start(bf16[2,16,32,512]{3,2,1,0:T(8,128)(2,1)} %get-tuple-element.17), channel_id=1, source_target_pairs={{0,1},{1,0},{2,3},{3,2},{4,5},{5,4},{6,7},{7,6},{8,9},{9,8},{10,11... | collective-permute-start | bytes 3145736 | tf_op jit(solution)/shard_map/ppermute | solution.py:324
  4.0 8.9 %collective-permute-start.3 = (bf16[3,32,512]{2,1,0:T(8,128)(2,1)}, bf16[3,32,512]{2,1,0:T(8,128)(2,1)S(1)}, u32[]{:S(2)}, u32[]{:S(2)}) collective-permute-start(bf16[3,32,512]{2,1,0:T(8,128)(2,1)} %get-tuple-element.18), channel_id=1, source_target_pairs={{0,2},{1,3},{2,0},{3,1},{4,6},{5,7},{6,4},{7,5},{8,10},{9,11},{10,... | collective-permute-start | bytes 294920 | tf_op jit(solution)/shard_map/ppermute | solution.py:324
  6.7 11.0 %collective-permute-start.4 = (bf16[3,32,512]{2,1,0:T(8,128)(2,1)}, bf16[3,32,512]{2,1,0:T(8,128)(2,1)S(1)}, u32[]{:S(2)}, u32[]{:S(2)}) collective-permute-start(bf16[3,32,512]{2,1,0:T(8,128)(2,1)} %get-tuple-element.18), channel_id=1, source_target_pairs={{0,4},{1,5},{2,6},{3,7},{4,0},{5,1},{6,2},{7,3},{8,12},{9,13},{10,... | collective-permute-start | bytes 294920 | tf_op jit(solution)/shard_map/ppermute | solution.py:324
  9.3 8.4 %collective-permute-start.5 = (bf16[3,32,512]{2,1,0:T(8,128)(2,1)}, bf16[3,32,512]{2,1,0:T(8,128)(2,1)S(1)}, u32[]{:S(2)}, u32[]{:S(2)}) collective-permute-start(bf16[3,32,512]{2,1,0:T(8,128)(2,1)} %get-tuple-element.18), channel_id=1, source_target_pairs={{0,6},{1,7},{2,4},{3,5},{4,2},{5,3},{6,0},{7,1},{8,14},{9,15},{10,... | collective-permute-start | bytes 294920 | tf_op jit(solution)/shard_map/ppermute | solution.py:324
  9.3 13.4 %collective-permute-start = (bf16[8,32,512]{2,1,0:T(8,128)(2,1)}, bf16[8,32,512]{2,1,0:T(8,128)(2,1)S(1)}, u32[]{:S(2)}, u32[]{:S(2)}) collective-permute-start(bf16[8,32,512]{2,1,0:T(8,128)(2,1)} %get-tuple-element.15), channel_id=1, source_target_pairs={{0,8},{8,16},{16,24},{1,9},{9,17},{17,25},{2,10},{10,18},{18,26},{... | collective-permute-start | bytes 786440 | tf_op jit(solution)/shard_map/ppermute | solution.py:354
  12.9 13.1 %collective-permute-start.1 = (bf16[8,32,512]{2,1,0:T(8,128)(2,1)}, bf16[8,32,512]{2,1,0:T(8,128)(2,1)S(1)}, u32[]{:S(2)}, u32[]{:S(2)}) collective-permute-start(bf16[8,32,512]{2,1,0:T(8,128)(2,1)} %get-tuple-element.16), channel_id=1, source_target_pairs={{8,0},{16,8},{24,16},{9,1},{17,9},{25,17},{10,2},{18,10},{26,18},{... | collective-permute-start | bytes 786440 | tf_op jit(solution)/shard_map/ppermute | solution.py:355
  19.4 12.5 %collective-permute-start.6 = (bf16[4,2,32,512]{3,2,1,0:T(8,128)(2,1)S(1)}, bf16[4,2,32,512]{3,2,1,0:T(8,128)(2,1)S(1)}, u32[]{:S(2)}, u32[]{:S(2)}) collective-permute-start(bf16[4,2,32,512]{3,2,1,0:T(8,128)(2,1)S(1)} %get-tuple-element.19.refs_6_.gk_own), channel_id=1, source_target_pairs={{0,1},{1,0},{2,3},{3,2},{4,5},{5,4},{6,7},{7,6},{8,9},{9,8},{10,11... | collective-permute-start | bytes 786440 | tf_op jit(solution)/shard_map/ppermute | solution.py:324
  19.5 7.9 %collective-permute-start.9 = (bf16[32,640]{1,0:T(8,128)(2,1)S(1)}, bf16[32,640]{1,0:T(8,128)(2,1)S(1)}, u32[]{:S(2)}, u32[]{:S(2)}) collective-permute-start(bf16[32,640]{1,0:T(8,128)(2,1)S(1)} %get-tuple-element.24), channel_id=1, source_target_pairs={{0,2},{1,3},{2,0},{3,1},{4,6},{5,7},{6,4},{7,5},{8,10},{9,11},{10,... | collective-permute-start | bytes 122888 | tf_op jit(solution)/shard_map/ppermute | solution.py:324
  21.5 8.0 %collective-permute-start.10 = (bf16[32,640]{1,0:T(8,128)(2,1)S(1)}, bf16[32,640]{1,0:T(8,128)(2,1)S(1)}, u32[]{:S(2)}, u32[]{:S(2)}) collective-permute-start(bf16[32,640]{1,0:T(8,128)(2,1)S(1)} %get-tuple-element.25), channel_id=1, source_target_pairs={{0,4},{1,5},{2,6},{3,7},{4,0},{5,1},{6,2},{7,3},{8,12},{9,13},{10,... | collective-permute-start | bytes 122888 | tf_op jit(solution)/shard_map/ppermute | solution.py:324
  22.7 6.8 %collective-permute-start.11 = (bf16[32,640]{1,0:T(8,128)(2,1)S(1)}, bf16[32,640]{1,0:T(8,128)(2,1)S(1)}, u32[]{:S(2)}, u32[]{:S(2)}) collective-permute-start(bf16[32,640]{1,0:T(8,128)(2,1)S(1)} %get-tuple-element.26), channel_id=1, source_target_pairs={{0,6},{1,7},{2,4},{3,5},{4,2},{5,3},{6,0},{7,1},{8,14},{9,15},{10,... | collective-permute-start | bytes 122888 | tf_op jit(solution)/shard_map/ppermute | solution.py:324
  24.1 9.2 %copy-start.6 = (bf16[16,32,512]{2,1,0:T(8,128)(2,1)S(1)}, bf16[16,32,512]{2,1,0:T(8,128)(2,1)}, u32[]{:S(2)}) copy-start(bf16[16,32,512]{2,1,0:T(8,128)(2,1)} %q_ref.1) | copy-start | bytes 1572868
  26.7 10.4 %collective-permute-start.7 = (bf16[24,8,512]{2,1,0:T(8,128)(2,1)S(1)}, bf16[24,8,512]{2,1,0:T(8,128)(2,1)S(1)}, u32[]{:S(2)}, u32[]{:S(2)}) collective-permute-start(bf16[24,8,512]{2,1,0:T(8,128)(2,1)S(1)} %get-tuple-element.20), channel_id=1, source_target_pairs={{1,2},{3,4},{5,6},{2,1},{4,3},{6,5},{9,10},{11,12},{13,14},{10,9},... | collective-permute-start | bytes 589832 | tf_op jit(solution)/shard_map/ppermute | solution.py:387
  27.4 9.7 %collective-permute-start.8 = (bf16[24,8,512]{2,1,0:T(8,128)(2,1)S(1)}, bf16[24,8,512]{2,1,0:T(8,128)(2,1)S(1)}, u32[]{:S(2)}, u32[]{:S(2)}) collective-permute-start(bf16[24,8,512]{2,1,0:T(8,128)(2,1)S(1)} %get-tuple-element.21), channel_id=1, source_target_pairs={{0,1},{1,0},{2,3},{3,2},{4,5},{5,4},{6,7},{7,6},{8,9},{9,8},{10,11... | collective-permute-start | bytes 589832 | tf_op jit(solution)/shard_map/ppermute | solution.py:324
  29.7 10.8 %collective-permute-start.12 = (bf16[32,640]{1,0:T(8,128)(2,1)S(1)}, bf16[32,640]{1,0:T(8,128)(2,1)S(1)}, u32[]{:S(2)}, u32[]{:S(2)}) collective-permute-start(bf16[32,640]{1,0:T(8,128)(2,1)S(1)} %shard_map.92.refs_0_), channel_id=1, source_target_pairs={{0,8},{8,0},{16,24},{24,16},{1,9},{9,1},{17,25},{25,17},{2,10},{10... | collective-permute-start | bytes 122888 | tf_op jit(solution)/shard_map/ppermute | solution.py:327
  31.3 9.2 %collective-permute-start.13 = (bf16[32,640]{1,0:T(8,128)(2,1)S(1)}, bf16[32,640]{1,0:T(8,128)(2,1)S(1)}, u32[]{:S(2)}, u32[]{:S(2)}) collective-permute-start(bf16[32,640]{1,0:T(8,128)(2,1)S(1)} %shard_map.92.refs_0_), channel_id=1, source_target_pairs={{0,16},{8,24},{16,0},{24,8},{1,17},{9,25},{17,1},{25,9},{2,18},{10... | collective-permute-start | bytes 122888 | tf_op jit(solution)/shard_map/ppermute | solution.py:327
  31.9 8.6 %collective-permute-start.14 = (bf16[32,640]{1,0:T(8,128)(2,1)S(1)}, bf16[32,640]{1,0:T(8,128)(2,1)S(1)}, u32[]{:S(2)}, u32[]{:S(2)}) collective-permute-start(bf16[32,640]{1,0:T(8,128)(2,1)S(1)} %shard_map.92.refs_0_), channel_id=1, source_target_pairs={{0,24},{8,16},{16,8},{24,0},{1,25},{9,17},{17,9},{25,1},{2,26},{10... | collective-permute-start | bytes 122888 | tf_op jit(solution)/shard_map/ppermute | solution.py:327
  35.4 1.8 %copy-start.2 = (bf16[512,512]{1,0:T(8,128)(2,1)S(1)}, bf16[512,512]{1,0:T(8,128)(2,1)}, u32[]{:S(2)}) copy-start(bf16[512,512]{1,0:T(8,128)(2,1)} %refs_5_.1) | copy-start | bytes 1572868

commit v3 on v2

v3 whole, which is shorter than its diff:
```python
import functools

import jax
import jax.numpy as jnp
from jax import lax
from jax.experimental import pallas as pl
from jax.experimental.pallas import tpu as pltpu
from jax.sharding import PartitionSpec as P

H = 8
HD = 64
RAD = 4
SIDE = 2 * RAD
PAIR = 2 * HD
STAT = 128
NEG_FILL = -1e30
VMEM_GRANT = 24 * 2**20
PACK_GRANT = 56 * 2**20
VMEM = pltpu.VMEM
BF = jnp.bfloat16
F32 = jnp.float32


def dot_nt(a, b):
    return lax.dot_general(a, b, (((1,), (1,)), ((), ())), preferred_element_type=F32)


def dot_nn(a, b):
    return lax.dot_general(a, b, (((1,), (0,)), ((), ())), preferred_element_type=F32)


def low_half(shape):
    return lax.broadcasted_iota(jnp.int32, shape, len(shape) - 1) < HD


def head_rows(q):
    q = q * jnp.asarray(HD**-0.5, q.dtype)
    low = low_half(q.shape)
    zero = jnp.zeros_like(q)
    return jnp.concatenate([jnp.where(low, q, zero), jnp.where(low, zero, q)], 0)


def with_ones(v):
    return jnp.concatenate([v, jnp.ones_like(v)], 1)


def softmax_pair(q, keys, vals, biases, round_top=False):
    n = q.shape[0]
    rows = head_rows(q)
    scores = []
    for key, bias in zip(keys, biases):
        s = dot_nt(rows, key)
        scores.append(s if bias is None else s + bias)
    top = functools.reduce(jnp.maximum, [jnp.max(s, -1, keepdims=True) for s in scores])
    if round_top:
        top = top.astype(BF).astype(F32)
    weights = [jnp.exp(s - top).astype(BF) for s in scores]
    out = functools.reduce(jnp.add, [dot_nn(w, with_ones(v)) for w, v in zip(weights, vals)])
    totals = (out[:n, PAIR:], out[n:, PAIR:])
    low = low_half((n, PAIR))
    attended = jnp.where(low, out[:n, :PAIR], out[n:, :PAIR]) / jnp.where(low, *totals)
    return attended, (top[:n], top[n:]), totals


def partial_softmax(q, keys, vals, out_refs):
    n = q.shape[0]
    lane = lax.broadcasted_iota(jnp.int32, (n, STAT), 1)
    stats = jnp.zeros((n, STAT), F32)
    pieces = []
    for p in range(H // 2):
        cut = slice(p * PAIR, (p + 1) * PAIR)
        out, tops, totals = softmax_pair(
            q[:, cut], [k[:, cut] for k in keys], [v[:, cut] for v in vals],
            [None] * len(keys), True,
        )
        pieces.append(out.astype(BF))
        for i in range(2):
            stats = jnp.where(lane == 2 * p + i, tops[i], stats)
            stats = jnp.where(lane == H + 2 * p + i, totals[i], stats)
    full = jnp.concatenate(pieces + [stats.astype(BF)], 1)
    start = 0
    for ref in out_refs:
        ref[...] = full[start : start + ref.shape[0]]
        start += ref.shape[0]


def swap_halves(x):
    return pltpu.roll(x.astype(F32), RAD, 1).astype(x.dtype)


def pack_first_kernel(k_ref, v_ref, gq, gk, gv, outer_ref, glob_ref, edges, sems):
    cols = k_ref.shape[1]
    moves = [
        (ref.at[:, pl.ds(start, SIDE)], edges.at[2 * j + i])
        for j, start in enumerate((0, cols - SIDE))
        for i, ref in enumerate((k_ref, v_ref))
    ]
    moves += [(ref, glob_ref.at[i]) for i, ref in enumerate((gq, gk, gv))]
    copies = [pltpu.make_async_copy(*move, sems.at[i]) for i, move in enumerate(moves)]
    for copy in copies:
        copy.start()
    for copy in copies:
        copy.wait()
    left, right = [(edges[2 * j], swap_halves(edges[2 * j + 1])) for j in range(2)]
    low = lax.broadcasted_iota(jnp.int32, left[0].shape, 1) < RAD
    second = lax.axis_index("tm") % 2 == 1
    outer_ref[...] = jnp.where(second, jnp.where(low, right[1], right[0]), jnp.where(low, *left))


def pack_second_kernel(k_ref, v_ref, facing_k, facing_v, outer_ref, up_ref, down_ref, *edge_refs):
    rows, cols = k_ref.shape[:2]
    second = lax.axis_index("tm") % 2 == 1
    outer = outer_ref[...]
    low = lax.broadcasted_iota(jnp.int32, outer.shape, 1) < RAD
    for i, (own, facing) in enumerate(((k_ref, facing_k), (v_ref, facing_v))):
        right = jnp.where(second, outer, facing[:, :SIDE])
        left = jnp.where(second, facing[:, cols - SIDE :], outer)
        edge = jnp.where(low, right, left)
        edge_refs[i][...] = edge
        for ref, band in ((up_ref, slice(rows - RAD, rows)), (down_ref, slice(0, RAD))):
            ref[i * RAD : (i + 1) * RAD, :cols] = own[band]
            ref[i * RAD : (i + 1) * RAD, cols:] = edge[band]
        outer = swap_halves(outer)


def global_kernel(pieces, *refs):
    gq, *blocks = refs[:5]
    others, outs = refs[5 : pieces + 4], refs[pieces + 4 :]
    q = jnp.concatenate([gq[...]] + [ref[0] for ref in others], 0)
    own_k, own_v, facing_k, facing_v = [ref[...].reshape(-1, ref.shape[2]) for ref in blocks]
    partial_softmax(q, [own_k, facing_k], [own_v, facing_v], outs)


def spread(stats):
    upper = stats.astype(BF)
    lower = (stats - upper.astype(F32)).astype(BF)
    source = lax.broadcasted_iota(jnp.int32, (2 * STAT, H * HD), 0) % STAT - H
    target = lax.broadcasted_iota(jnp.int32, (2 * STAT, H * HD), 1) // HD
    pick = (source == target).astype(BF)
    return dot_nn(jnp.concatenate([upper, lower], 1), pick)


def merge(parts):
    width, n = H * HD, parts[0].shape[0]
    lane = lax.broadcasted_iota(jnp.int32, (n, STAT), 1)
    stats = [x[:, width:].astype(F32) for x in parts]
    top = functools.reduce(jnp.maximum, stats)
    held = (lane >= H) & (lane < 2 * H)
    mass = [jnp.where(held, s * pltpu.roll(jnp.exp(s - top), H, 1), 0.0) for s in stats]
    total = functools.reduce(jnp.add, mass)
    inverse = 1.0 / jnp.where(held, total, 1.0)
    shares = spread(jnp.concatenate([m * inverse for m in mass], 0))
    out = functools.reduce(
        jnp.add,
        [x[:, :width].astype(F32) * shares[i * n : (i + 1) * n] for i, x in enumerate(parts)],
    )
    return out, jnp.where(lane < H, top, total)


def merge_kernel(count, *refs):
    gk, gv, *others = refs[count:-2]
    out_ref, kv_ref = refs[-2:]
    out, stats = merge([ref[...] for ref in refs[:count]])
    out_ref[...] = jnp.concatenate([out.astype(BF), stats.astype(BF)], 1)
    kv_ref[0, 0], kv_ref[0, 1] = gk[...], gv[...]
    for i, ref in enumerate(others):
        kv_ref[i + 1] = ref[1:]


def last_merge_kernel(*refs):
    *ins, extra, weight, out_ref = refs
    parts = [ref[...].astype(F32) for ref in ins]
    for b in range(len(parts).bit_length() - 1):
        swap = lax.axis_index("station") // (1 << b) % 2 == 1
        parts = [jnp.where(swap, parts[m ^ (1 << b)], part) for m, part in enumerate(parts)]
    out, _ = merge([*parts, extra[...]])
    out_ref[...] = dot_nn(out.astype(BF), weight[...]).astype(BF)


def row_window(up, own, down, block, lanes, cols, halo_cols):
    rows = own.shape[0]
    first, stop = block * SIDE - RAD, block * SIDE + SIDE + RAD
    parts = []
    if first < 0:
        parts.append(up[:, halo_cols, lanes])
    parts.append(own[max(first, 0) : min(stop, rows), cols, lanes])
    if stop > rows:
        parts.append(down[:, halo_cols, lanes])
    return jnp.concatenate(parts, 0) if len(parts) > 1 else parts[0]


def window_bias(block, blocks, wrap):
    key_cols = 3 * SIDE if wrap else 2 * SIDE
    shape = (SIDE, SIDE, 2 * SIDE, key_cols)
    n, k = SIDE * SIDE, 2 * SIDE * key_cols
    q = lax.broadcasted_iota(jnp.int32, (n, k), 0)
    key = lax.broadcasted_iota(jnp.int32, (n, k), 1)
    q_row, q_col = q // SIDE, q % SIDE
    k_row, k_col = key // key_cols, key % key_cols
    if wrap:
        q_col = jnp.where(q_col < RAD, q_col + RAD, q_col + RAD + SIDE)
    else:
        q_col = q_col + RAD
    ok = (jnp.abs(q_row + RAD - k_row) <= RAD) & (jnp.abs(q_col - k_col) <= RAD)
    bias = jnp.where(ok, 0.0, NEG_FILL)
    station, column = lax.axis_index("station"), lax.axis_index("tm")
    outside = []
    if block == 0:
        outside.append((station == 0, k_row < RAD))
    if block == blocks - 1:
        outside.append((station == lax.axis_size("station") - 1, k_row >= SIDE + RAD))
    if wrap:
        outside.append((column == lax.axis_size("tm") - 1, (k_col >= SIDE) & (k_col < SIDE + RAD)))
        outside.append((column == 0, (k_col >= SIDE + RAD) & (k_col < 2 * SIDE)))
    for edge, where in outside:
        bias = bias + jnp.where(where, jnp.where(edge, NEG_FILL, 0.0), 0.0)
    return jnp.concatenate([bias, bias], 0)


def global_views(own, other):
    keys, vals = [], []
    for ref in (own, other):
        for i in range(ref.shape[0]):
            keys.append(ref[i, 0])
            vals.append(ref[i, 1])
    return [jnp.concatenate(keys, 0)], [jnp.concatenate(vals, 0)]


def grid_kernel(q_ref, k_ref, v_ref, halo_up, halo_down, gk_own, gk_other, edge_k, edge_v, gq, weight,
                out_ref, extra_ref):
    rows, cols, width = q_ref.shape
    blocks, across = rows // SIDE, cols // SIDE
    gks, gvs = global_views(gk_own, gk_other)
    group = slice(0, SIDE)
    beyond = slice(cols, cols + SIDE)
    for block in range(blocks):
        biases = [window_bias(block, blocks, wrap) for wrap in (False, True)]
        q_rows = slice(block * SIDE, (block + 1) * SIDE)
        done = []
        for j in range(across):
            wrap = j == across - 1
            pieces = []
            for p in range(H // 2):
                lanes = slice(p * PAIR, (p + 1) * PAIR)
                windows = []
                for i, (own, edge) in enumerate(((k_ref, edge_k), (v_ref, edge_v))):
                    up, down = [ref.at[i * RAD : (i + 1) * RAD] for ref in (halo_up, halo_down)]
                    spans = [slice(j * SIDE, (j + 2) * SIDE)]
                    if wrap:
                        spans = [slice(cols - SIDE, cols), None, group]
                    parts = [
                        row_window(up, edge, down, block, lanes, group, beyond)
                        if span is None
                        else row_window(up, own, down, block, lanes, span, span)
                        for span in spans
                    ]
                    window = jnp.concatenate(parts, 1) if wrap else parts[0]
                    windows.append(window.reshape(-1, PAIR))
                if wrap:
                    q = jnp.concatenate(
                        [q_ref[q_rows, cols - RAD :, lanes], q_ref[q_rows, :RAD, lanes]], 1
                    )
                else:
                    q = q_ref[q_rows, j * SIDE + RAD : (j + 1) * SIDE + RAD, lanes]
                out, _, _ = softmax_pair(
                    q.reshape(SIDE * SIDE, PAIR),
                    [windows[0], gks[0][:, lanes]],
                    [windows[1], gvs[0][:, lanes]],
                    [biases[wrap], None],
                )
                pieces.append(out.astype(BF))
            done.append(jnp.concatenate(pieces, 1))
        projected = dot_nn(jnp.concatenate(done, 0), weight[...]).reshape(across, SIDE, SIDE, width)
        for j in range(across):
            before = projected[(j - 1) % across][:, RAD:]
            after = projected[j][:, :RAD]
            out_ref[q_rows, j * SIDE : (j + 1) * SIDE, :] = jnp.concatenate([before, after], 1).astype(BF)
    partial_softmax(gq[...], gks, gvs, [extra_ref])


def call(kernel, inputs, out_shapes, flops):
    specs = [pl.BlockSpec(memory_space=VMEM)] * len(inputs)
    return pl.pallas_call(
        kernel,
        out_shape=[jax.ShapeDtypeStruct(s, BF) for s in out_shapes],
        in_specs=specs,
        out_specs=[pl.BlockSpec(memory_space=VMEM)] * len(out_shapes),
        compiler_params=pltpu.CompilerParams(vmem_limit_bytes=VMEM_GRANT),
        cost_estimate=pl.CostEstimate(flops=flops, bytes_accessed=2**20, transcendentals=0),
    )(*inputs)


def body(queries, grid_keys, values, glob_queries, glob_keys, glob_values, out_weight):
    rows, cols, width = queries.shape
    own = glob_queries.shape[0]
    stations, across = lax.axis_size("station"), lax.axis_size("tm")
    chips = across // 2
    payload = width + STAT

    def over_tm(x, mask):
        return lax.ppermute(x, "tm", [(i, i ^ mask) for i in range(across)])

    def over_station(x, mask):
        return lax.ppermute(x, "station", [(i, i ^ mask) for i in range(stations)])

    up = [(i, i + 1) for i in range(stations - 1)]
    down = [(j, i) for i, j in up]
    facing = [over_tm(grid_keys, 1), over_tm(values, 1)]
    outer, glob = pl.pallas_call(
        pack_first_kernel,
        out_shape=[
            jax.ShapeDtypeStruct(shape, BF)
            for shape in [(rows, SIDE, width), (3, own, width)]
        ],
        in_specs=[pl.BlockSpec(memory_space=pltpu.HBM)] * 5,
        out_specs=[pl.BlockSpec(memory_space=VMEM)] * 2,
        scratch_shapes=[VMEM((4, rows, SIDE, width), BF), pltpu.SemaphoreType.DMA((7,))],
        compiler_params=pltpu.CompilerParams(vmem_limit_bytes=PACK_GRANT),
        cost_estimate=pl.CostEstimate(flops=10**6, bytes_accessed=2**20, transcendentals=0),
    )(grid_keys, values, glob_queries, glob_keys, glob_values)
    chip_edges = [(i, i + 1) for i in range(1, across - 1, 2)]
    outer = lax.ppermute(outer, "tm", chip_edges + [(j, i) for i, j in chip_edges])
    to_up, to_down, *edges = call(
        pack_second_kernel,
        [grid_keys, values, *facing, outer],
        [(2 * RAD, cols + SIDE, width)] * 2 + [(rows, SIDE, width)] * 2,
        10**6,
    )
    halo_up = lax.ppermute(to_up, "station", up)
    halo_down = lax.ppermute(to_down, "station", down)
    pieces = [over_tm(glob, 2 * m) for m in range(1, chips)]

    parts = list(call(
        functools.partial(global_kernel, chips),
        [glob_queries, grid_keys, values, *facing, *pieces],
        [(own, payload)] * chips,
        2 * 10**9,
    ))
    parts = parts[:1] + [over_tm(part, 2 * m) for m, part in enumerate(parts) if m]
    merged, kv_own = call(
        functools.partial(merge_kernel, chips),
        [*parts, glob_keys, glob_values, *pieces],
        [(own, payload), (chips, 2, own, width)],
        10**8,
    )
    kv_other = over_tm(kv_own, 1)
    grid_output, extra = call(
        grid_kernel,
        [queries, grid_keys, values, halo_up, halo_down, kv_own, kv_other, *edges, glob_queries, out_weight],
        [(rows, cols, width), (own, payload)],
        6 * 10**9,
    )

    parts = [merged] + [over_station(merged, m) for m in range(1, stations)]
    (glob_output,) = call(
        last_merge_kernel,
        [*parts, extra, out_weight],
        [(own, width)],
        10**8,
    )
    return grid_output, glob_output


def solution(mesh):
    return jax.shard_map(
        body,
        mesh=mesh,
        in_specs=(
            P("station", "tm", None),
            P("station", "tm", None),
            P("station", "tm", None),
            P("tm", None),
            P("tm", None),
            P("tm", None),
            P(),
        ),
        out_specs=(P("station", "tm", None), P("tm", None)),
        check_vma=False,
    )
```

time: 42.3 us -> 41.1 us (0.972)
  starting transfers between devices: 21.5 us -> 26 us
  Pallas kernels: 14.2 us -> 9.96 us
  waiting for transfers between devices: 5.39 us -> 4.07 us
    ppermute x9, starting transfers between devices: 12.3 us -> 16.6 us  [over_tm(): return lax.ppermute(x, 'tm', [(i, i ^ mask) for i in range(across)])]
    pallas_call x7 -> x5, Pallas kernels: 11.4 us -> 8.05 us  [call(): pl.pallas_call(kernel, out_shape=[jax.ShapeDtypeStruct(s, BF) for s in ou...]
    ppermute x1, waiting for transfers between devices: 1.93 us -> 0.01 us  [body(): halo_down = lax.ppermute(to_down, 'station', down)]
    pallas_call x1, Pallas kernels: 2.83 us -> 1.91 us  [body(): pl.pallas_call(pack_first_kernel, out_shape=[jax.ShapeDtypeStruct(shape,...]
    ppermute x9, waiting for transfers between devices: 3.45 us -> 4.05 us  [over_tm(): return lax.ppermute(x, 'tm', [(i, i ^ mask) for i in range(across)])]
    ppermute x3, starting transfers between devices: 3.55 us -> 4.04 us  [over_station(): return lax.ppermute(x, 'station', [(i, i ^ mask) for i in range(stations)])]
  transfers between devices with their start and end apart: 15 -> 15, of which waited for: 2 -> 2; matrix products, arithmetic and copies ran while one was open for 0% -> 0% of each run, Pallas kernels for 23% -> 22%
where the time goes in v3:
time: 41.1 us; the launch traced here: 40.9 us
  starting transfers between devices  26 us (63%)
  Pallas kernels  9.96 us (24%)
  waiting for transfers between devices  4.07 us (10%)
  between operations  0.81 us (2%)
    ppermute x9, starting transfers between devices, over_tm(): return lax.ppermute(x, 'tm', [(i, i ^ mask) for i in range(across)])  16.6 us
    pallas_call x5, Pallas kernels, call(): pl.pallas_call(kernel, out_shape=[jax.ShapeDtypeStruct(s, BF) for s in ou...  8.05 us
    ppermute x9, waiting for transfers between devices, over_tm(): return lax.ppermute(x, 'tm', [(i, i ^ mask) for i in range(across)])  4.05 us
    ppermute x3, starting transfers between devices, over_station(): return lax.ppermute(x, 'station', [(i, i ^ mask) for i in range(stations)])  4.04 us
    ppermute x1, starting transfers between devices, body(): halo_up = lax.ppermute(to_up, 'station', up)  3.42 us
    pallas_call x1, Pallas kernels, body(): pl.pallas_call(pack_first_kernel, out_shape=[jax.ShapeDtypeStruct(shape,...  1.91 us
    ppermute x1, starting transfers between devices, body(): halo_down = lax.ppermute(to_down, 'station', down)  1.29 us
  transfers between devices with their start and end apart: 15, of which 2 were waited for; matrix products, arithmetic and copies ran while one was open for 0% of the time, Pallas kernels for 22%

profile of v3, /device:TPU:0, one launch (start us, length us, event | category | flops | bytes accessed | tf_op | source)
XLA Modules:
  0.0 40.9 jit_solution(5961543869633464295)
XLA Ops:
  0.6 0.5 %collective-permute-start = (bf16[16,32,512]{2,1,0:T(8,128)(2,1)}, bf16[16,32,512]{2,1,0:T(8,128)(2,1)S(1)}, u32[]{:S(2)}, u32[]{:S(2)}) collective-permute-start(bf16[16,32,512]{2,1,0:T(8,128)(2,1)} %k_ref.5), channel_id=1, source_target_pairs={{0,1},{1,0},{2,3},{3,2},{4,5},{5,4},{6,7},{7,6},{8,9},{9,8},{10,11... | collective-permute-start | bytes 1572872 | tf_op jit(solution)/shard_map/ppermute | solution.py:301
  1.2 0.1 collective-permute-start.1
  1.2 1.9 %shard_map.86 = (bf16[16,8,512]{2,1,0:T(8,128)(2,1)}, bf16[3,32,512]{2,1,0:T(8,128)(2,1)}) custom-call(bf16[16,32,512]{2,1,0:T(8,128)(2,1)} %k_ref.5, bf16[16,32,512]{2,1,0:T(8,128)(2,1)} %v_ref.5, bf16[32,512]{1,0:T(8,128)(2,1)} %gq.3, bf16[32,512]{1,0:T(8,128)(2,1)} %refs_4_.1, bf16[32,512]{1,0:T(8,128)(2,1)} %refs_5_.2), custom_call_target="tpu_custom_call" | custom-call | flops 1000000 | bytes 1048576 | tf_op jit(solution)/shard_map/pallas_call | solution.py:309
  3.2 0.7 %collective-permute-start.2 = (bf16[16,8,512]{2,1,0:T(8,128)(2,1)}, bf16[16,8,512]{2,1,0:T(8,128)(2,1)S(1)}, u32[]{:S(2)}, u32[]{:S(2)}) collective-permute-start(bf16[16,8,512]{2,1,0:T(8,128)(2,1)} %get-tuple-element.16), channel_id=1, source_target_pairs={{1,2},{3,4},{5,6},{2,1},{4,3},{6,5},{9,10},{11,12},{13,14},{10,9},... | collective-permute-start | bytes 393224 | tf_op jit(solution)/shard_map/ppermute | solution.py:322
  3.8 0.0 copy-start.5
  3.9 4.3 %collective-permute-start.5 = (bf16[3,32,512]{2,1,0:T(8,128)(2,1)}, bf16[3,32,512]{2,1,0:T(8,128)(2,1)S(1)}, u32[]{:S(2)}, u32[]{:S(2)}) collective-permute-start(bf16[3,32,512]{2,1,0:T(8,128)(2,1)} %get-tuple-element.19), channel_id=1, source_target_pairs={{0,2},{1,3},{2,0},{3,1},{4,6},{5,7},{6,4},{7,5},{8,10},{9,11},{10,... | collective-permute-start | bytes 294920 | tf_op jit(solution)/shard_map/ppermute | solution.py:301
  8.2 2.7 %collective-permute-start.6 = (bf16[3,32,512]{2,1,0:T(8,128)(2,1)}, bf16[3,32,512]{2,1,0:T(8,128)(2,1)S(1)}, u32[]{:S(2)}, u32[]{:S(2)}) collective-permute-start(bf16[3,32,512]{2,1,0:T(8,128)(2,1)} %get-tuple-element.19), channel_id=1, source_target_pairs={{0,4},{1,5},{2,6},{3,7},{4,0},{5,1},{6,2},{7,3},{8,12},{9,13},{10,... | collective-permute-start | bytes 294920 | tf_op jit(solution)/shard_map/ppermute | solution.py:301
  10.9 0.0 collective-permute-done.2.outer_ref
  10.9 4.4 %collective-permute-start.7 = (bf16[3,32,512]{2,1,0:T(8,128)(2,1)}, bf16[3,32,512]{2,1,0:T(8,128)(2,1)S(1)}, u32[]{:S(2)}, u32[]{:S(2)}) collective-permute-start(bf16[3,32,512]{2,1,0:T(8,128)(2,1)} %get-tuple-element.19), channel_id=1, source_target_pairs={{0,6},{1,7},{2,4},{3,5},{4,2},{5,3},{6,0},{7,1},{8,14},{9,15},{10,... | collective-permute-start | bytes 294920 | tf_op jit(solution)/shard_map/ppermute | solution.py:301
  15.3 0.1 shard_map.87
  15.5 3.4 %collective-permute-start.3 = (bf16[8,40,512]{2,1,0:T(8,128)(2,1)S(1)}, bf16[8,40,512]{2,1,0:T(8,128)(2,1)S(1)}, u32[]{:S(2)}, u32[]{:S(2)}) collective-permute-start(bf16[8,40,512]{2,1,0:T(8,128)(2,1)S(1)} %get-tuple-element.17), channel_id=1, source_target_pairs={{0,8},{8,16},{16,24},{1,9},{9,17},{17,25},{2,10},{10,18},{18,26},{... | collective-permute-start | bytes 983048 | tf_op jit(solution)/shard_map/ppermute | solution.py:329
  18.9 0.0 copy-start.3
  18.9 0.0 copy-start.4
  18.9 1.3 %collective-permute-start.4 = (bf16[8,40,512]{2,1,0:T(8,128)(2,1)S(1)}, bf16[8,40,512]{2,1,0:T(8,128)(2,1)S(1)}, u32[]{:S(2)}, u32[]{:S(2)}) collective-permute-start(bf16[8,40,512]{2,1,0:T(8,128)(2,1)S(1)} %get-tuple-element.18), channel_id=1, source_target_pairs={{8,0},{16,8},{24,16},{9,1},{17,9},{25,17},{10,2},{18,10},{26,18},{... | collective-permute-start | bytes 983048 | tf_op jit(solution)/shard_map/ppermute | solution.py:330
  20.2 0.0 collective-permute-done.7.refs_7_.refs_8_
  20.2 0.0 copy-start.6
  20.3 1.7 %shard_map.88 = (bf16[32,640]{1,0:T(8,128)(2,1)S(1)}, bf16[32,640]{1,0:T(8,128)(2,1)S(1)}, bf16[32,640]{1,0:T(8,128)(2,1)S(1)}, bf16[32,640]{1,0:T(8,128)(2,1)S(1)}) custom-call(bf16[32,512]{1,0:T(8,128)(2,1)S(1)} %copy-done.5, bf16[16,32,512]{2,1,0:T(8,128)(2,1)S(1)} %copy-done, bf16[16,32,512]{2,1,0:T(8,128)(2,1)S(1)} %copy-done.1, ...), custom_call_target="tpu_custom_call" | custom-call | flops 2000000000 | bytes 1048576 | tf_op jit(solution)/shard_map/pallas_call | solution.py:283
  22.0 0.0 copy-start.2
  22.0 1.9 %collective-permute-start.8 = (bf16[32,640]{1,0:T(8,128)(2,1)S(1)}, bf16[32,640]{1,0:T(8,128)(2,1)S(1)}, u32[]{:S(2)}, u32[]{:S(2)}) collective-permute-start(bf16[32,640]{1,0:T(8,128)(2,1)S(1)} %get-tuple-element.21), channel_id=1, source_target_pairs={{0,2},{1,3},{2,0},{3,1},{4,6},{5,7},{6,4},{7,5},{8,10},{9,11},{10,... | collective-permute-start | bytes 122888 | tf_op jit(solution)/shard_map/ppermute | solution.py:301
  24.0 0.6 %collective-permute-start.9 = (bf16[32,640]{1,0:T(8,128)(2,1)S(1)}, bf16[32,640]{1,0:T(8,128)(2,1)S(1)}, u32[]{:S(2)}, u32[]{:S(2)}) collective-permute-start(bf16[32,640]{1,0:T(8,128)(2,1)S(1)} %get-tuple-element.22), channel_id=1, source_target_pairs={{0,4},{1,5},{2,6},{3,7},{4,0},{5,1},{6,2},{7,3},{8,12},{9,13},{10,... | collective-permute-start | bytes 122888 | tf_op jit(solution)/shard_map/ppermute | solution.py:301
  24.6 1.9 %collective-permute-start.10 = (bf16[32,640]{1,0:T(8,128)(2,1)S(1)}, bf16[32,640]{1,0:T(8,128)(2,1)S(1)}, u32[]{:S(2)}, u32[]{:S(2)}) collective-permute-start(bf16[32,640]{1,0:T(8,128)(2,1)S(1)} %get-tuple-element.23), channel_id=1, source_target_pairs={{0,6},{1,7},{2,4},{3,5},{4,2},{5,3},{6,0},{7,1},{8,14},{9,15},{10,... | collective-permute-start | bytes 122888 | tf_op jit(solution)/shard_map/ppermute | solution.py:301
  26.5 3.3 %collective-permute-done.9.refs_2_ = bf16[32,640]{1,0:T(8,128)(2,1)S(1)} collective-permute-done((bf16[32,640]{1,0:T(8,128)(2,1)S(1)}, bf16[32,640]{1,0:T(8,128)(2,1)S(1)}, u32[]{:S(2)}, u32[]{:S(2)}) %collective-permute-start.9) | collective-permute-done | bytes 40992 | tf_op jit(solution)/shard_map/ppermute | solution.py:301
  29.8 0.7 %collective-permute-done.10.refs_3_ = bf16[32,640]{1,0:T(8,128)(2,1)S(1)} collective-permute-done((bf16[32,640]{1,0:T(8,128)(2,1)S(1)}, bf16[32,640]{1,0:T(8,128)(2,1)S(1)}, u32[]{:S(2)}, u32[]{:S(2)}) %collective-permute-start.10) | collective-permute-done | bytes 40992 | tf_op jit(solution)/shard_map/ppermute | solution.py:301
  30.5 0.3 shard_map.89
  30.8 0.1 collective-permute-start.11
  30.9 1.6 %collective-permute-start.12 = (bf16[32,640]{1,0:T(8,128)(2,1)S(1)}, bf16[32,640]{1,0:T(8,128)(2,1)S(1)}, u32[]{:S(2)}, u32[]{:S(2)}) collective-permute-start(bf16[32,640]{1,0:T(8,128)(2,1)S(1)} %get-tuple-element.28.refs_0_), channel_id=1, source_target_pairs={{0,8},{8,0},{16,24},{24,16},{1,9},{9,1},{17,25},{25,17},{2,10},{10... | collective-permute-start | bytes 122888 | tf_op jit(solution)/shard_map/ppermute | solution.py:304
  32.5 1.5 %collective-permute-start.13 = (bf16[32,640]{1,0:T(8,128)(2,1)S(1)}, bf16[32,640]{1,0:T(8,128)(2,1)S(1)}, u32[]{:S(2)}, u32[]{:S(2)}) collective-permute-start(bf16[32,640]{1,0:T(8,128)(2,1)S(1)} %get-tuple-element.28.refs_0_), channel_id=1, source_target_pairs={{0,16},{8,24},{16,0},{24,8},{1,17},{9,25},{17,1},{25,9},{2,18},{10... | collective-permute-start | bytes 122888 | tf_op jit(solution)/shard_map/ppermute | solution.py:304
  34.0 0.0 collective-permute-done.11.gk_other
  34.0 0.9 %collective-permute-start.14 = (bf16[32,640]{1,0:T(8,128)(2,1)S(1)}, bf16[32,640]{1,0:T(8,128)(2,1)S(1)}, u32[]{:S(2)}, u32[]{:S(2)}) collective-permute-start(bf16[32,640]{1,0:T(8,128)(2,1)S(1)} %get-tuple-element.28.refs_0_), channel_id=1, source_target_pairs={{0,24},{8,16},{16,8},{24,0},{1,25},{9,17},{17,9},{25,1},{2,26},{10... | collective-permute-start | bytes 122888 | tf_op jit(solution)/shard_map/ppermute | solution.py:304
  34.9 0.0 collective-permute-done.3.halo_up
  34.9 4.9 %shard_map.90 = (bf16[16,32,512]{2,1,0:T(8,128)(2,1)}, bf16[32,640]{1,0:T(8,128)(2,1)S(1)}) custom-call(bf16[16,32,512]{2,1,0:T(8,128)(2,1)S(1)} %copy-done.6, bf16[16,32,512]{2,1,0:T(8,128)(2,1)S(1)} %copy-done, bf16[16,32,512]{2,1,0:T(8,128)(2,1)S(1)} %copy-done.1, bf16[8,40,512]{2,1,0:T(8,128)(2,1)S(1)} %collective-permute-done.3.halo_up, ...), custom_call_target="tpu_custom_call" | custom-call | flops 6000000000 | bytes 1048576 | tf_op jit(solution)/shard_map/pallas_call | solution.py:283
  39.8 1.1 %shard_map.91 = bf16[32,512]{1,0:T(8,128)(2,1)} custom-call(bf16[32,640]{1,0:T(8,128)(2,1)S(1)} %get-tuple-element.28.refs_0_, bf16[32,640]{1,0:T(8,128)(2,1)S(1)} %collective-permute-done.12.refs_1_, bf16[32,640]{1,0:T(8,128)(2,1)S(1)} %collective-permute-done.13.refs_2_, bf16[32,640]{1,0:T(8,128)(2,1)S(1)} %collective-permute-done.14.refs_3_, ...), custom_call_target="tpu_custom_call" | custom-call | flops 100000000 | bytes 1048576 | tf_op jit(solution)/shard_map/pallas_call | solution.py:283
  (18 shorter events, 0.0 us)
Async XLA Ops:
  0.6 14.7 %copy-start = (bf16[16,32,512]{2,1,0:T(8,128)(2,1)S(1)}, bf16[16,32,512]{2,1,0:T(8,128)(2,1)}, u32[]{:S(2)}) copy-start(bf16[16,32,512]{2,1,0:T(8,128)(2,1)} %k_ref.5) | copy-start | bytes 1572868
  0.6 14.7 %copy-start.1 = (bf16[16,32,512]{2,1,0:T(8,128)(2,1)S(1)}, bf16[16,32,512]{2,1,0:T(8,128)(2,1)}, u32[]{:S(2)}) copy-start(bf16[16,32,512]{2,1,0:T(8,128)(2,1)} %v_ref.5) | copy-start | bytes 1572868
  0.6 14.7 %collective-permute-start = (bf16[16,32,512]{2,1,0:T(8,128)(2,1)}, bf16[16,32,512]{2,1,0:T(8,128)(2,1)S(1)}, u32[]{:S(2)}, u32[]{:S(2)}) collective-permute-start(bf16[16,32,512]{2,1,0:T(8,128)(2,1)} %k_ref.5), channel_id=1, source_target_pairs={{0,1},{1,0},{2,3},{3,2},{4,5},{5,4},{6,7},{7,6},{8,9},{9,8},{10,11... | collective-permute-start | bytes 1572872 | tf_op jit(solution)/shard_map/ppermute | solution.py:301
  1.2 14.1 %collective-permute-start.1 = (bf16[16,32,512]{2,1,0:T(8,128)(2,1)}, bf16[16,32,512]{2,1,0:T(8,128)(2,1)S(1)}, u32[]{:S(2)}, u32[]{:S(2)}) collective-permute-start(bf16[16,32,512]{2,1,0:T(8,128)(2,1)} %v_ref.5), channel_id=1, source_target_pairs={{0,1},{1,0},{2,3},{3,2},{4,5},{5,4},{6,7},{7,6},{8,9},{9,8},{10,11... | collective-permute-start | bytes 1572872 | tf_op jit(solution)/shard_map/ppermute | solution.py:301
  3.2 7.7 %collective-permute-start.2 = (bf16[16,8,512]{2,1,0:T(8,128)(2,1)}, bf16[16,8,512]{2,1,0:T(8,128)(2,1)S(1)}, u32[]{:S(2)}, u32[]{:S(2)}) collective-permute-start(bf16[16,8,512]{2,1,0:T(8,128)(2,1)} %get-tuple-element.16), channel_id=1, source_target_pairs={{1,2},{3,4},{5,6},{2,1},{4,3},{6,5},{9,10},{11,12},{13,14},{10,9},... | collective-permute-start | bytes 393224 | tf_op jit(solution)/shard_map/ppermute | solution.py:322
  3.8 16.4 %copy-start.5 = (bf16[32,512]{1,0:T(8,128)(2,1)S(1)}, bf16[32,512]{1,0:T(8,128)(2,1)}, u32[]{:S(2)}) copy-start(bf16[32,512]{1,0:T(8,128)(2,1)} %gq.3) | copy-start | bytes 98308
  3.9 16.4 %collective-permute-start.5 = (bf16[3,32,512]{2,1,0:T(8,128)(2,1)}, bf16[3,32,512]{2,1,0:T(8,128)(2,1)S(1)}, u32[]{:S(2)}, u32[]{:S(2)}) collective-permute-start(bf16[3,32,512]{2,1,0:T(8,128)(2,1)} %get-tuple-element.19), channel_id=1, source_target_pairs={{0,2},{1,3},{2,0},{3,1},{4,6},{5,7},{6,4},{7,5},{8,10},{9,11},{10,... | collective-permute-start | bytes 294920 | tf_op jit(solution)/shard_map/ppermute | solution.py:301
  8.2 12.0 %collective-permute-start.6 = (bf16[3,32,512]{2,1,0:T(8,128)(2,1)}, bf16[3,32,512]{2,1,0:T(8,128)(2,1)S(1)}, u32[]{:S(2)}, u32[]{:S(2)}) collective-permute-start(bf16[3,32,512]{2,1,0:T(8,128)(2,1)} %get-tuple-element.19), channel_id=1, source_target_pairs={{0,4},{1,5},{2,6},{3,7},{4,0},{5,1},{6,2},{7,3},{8,12},{9,13},{10,... | collective-permute-start | bytes 294920 | tf_op jit(solution)/shard_map/ppermute | solution.py:301
  10.9 9.3 %collective-permute-start.7 = (bf16[3,32,512]{2,1,0:T(8,128)(2,1)}, bf16[3,32,512]{2,1,0:T(8,128)(2,1)S(1)}, u32[]{:S(2)}, u32[]{:S(2)}) collective-permute-start(bf16[3,32,512]{2,1,0:T(8,128)(2,1)} %get-tuple-element.19), channel_id=1, source_target_pairs={{0,6},{1,7},{2,4},{3,5},{4,2},{5,3},{6,0},{7,1},{8,14},{9,15},{10,... | collective-permute-start | bytes 294920 | tf_op jit(solution)/shard_map/ppermute | solution.py:301
  15.5 19.4 %collective-permute-start.3 = (bf16[8,40,512]{2,1,0:T(8,128)(2,1)S(1)}, bf16[8,40,512]{2,1,0:T(8,128)(2,1)S(1)}, u32[]{:S(2)}, u32[]{:S(2)}) collective-permute-start(bf16[8,40,512]{2,1,0:T(8,128)(2,1)S(1)} %get-tuple-element.17), channel_id=1, source_target_pairs={{0,8},{8,16},{16,24},{1,9},{9,17},{17,25},{2,10},{10,18},{18,26},{... | collective-permute-start | bytes 983048 | tf_op jit(solution)/shard_map/ppermute | solution.py:329
  18.9 11.6 %copy-start.3 = (bf16[32,512]{1,0:T(8,128)(2,1)S(1)}, bf16[32,512]{1,0:T(8,128)(2,1)}, u32[]{:S(2)}) copy-start(bf16[32,512]{1,0:T(8,128)(2,1)} %refs_4_.1) | copy-start | bytes 98308
  18.9 11.6 %copy-start.4 = (bf16[32,512]{1,0:T(8,128)(2,1)S(1)}, bf16[32,512]{1,0:T(8,128)(2,1)}, u32[]{:S(2)}) copy-start(bf16[32,512]{1,0:T(8,128)(2,1)} %refs_5_.2) | copy-start | bytes 98308
  18.9 16.0 %collective-permute-start.4 = (bf16[8,40,512]{2,1,0:T(8,128)(2,1)S(1)}, bf16[8,40,512]{2,1,0:T(8,128)(2,1)S(1)}, u32[]{:S(2)}, u32[]{:S(2)}) collective-permute-start(bf16[8,40,512]{2,1,0:T(8,128)(2,1)S(1)} %get-tuple-element.18), channel_id=1, source_target_pairs={{8,0},{16,8},{24,16},{9,1},{17,9},{25,17},{10,2},{18,10},{26,18},{... | collective-permute-start | bytes 983048 | tf_op jit(solution)/shard_map/ppermute | solution.py:330
  20.2 14.7 %copy-start.6 = (bf16[16,32,512]{2,1,0:T(8,128)(2,1)S(1)}, bf16[16,32,512]{2,1,0:T(8,128)(2,1)}, u32[]{:S(2)}) copy-start(bf16[16,32,512]{2,1,0:T(8,128)(2,1)} %q_ref.1) | copy-start | bytes 1572868
  22.0 12.9 %copy-start.2 = (bf16[512,512]{1,0:T(8,128)(2,1)S(1)}, bf16[512,512]{1,0:T(8,128)(2,1)}, u32[]{:S(2)}) copy-start(bf16[512,512]{1,0:T(8,128)(2,1)} %refs_5_.3) | copy-start | bytes 1572868
  22.0 4.5 %collective-permute-start.8 = (bf16[32,640]{1,0:T(8,128)(2,1)S(1)}, bf16[32,640]{1,0:T(8,128)(2,1)S(1)}, u32[]{:S(2)}, u32[]{:S(2)}) collective-permute-start(bf16[32,640]{1,0:T(8,128)(2,1)S(1)} %get-tuple-element.21), channel_id=1, source_target_pairs={{0,2},{1,3},{2,0},{3,1},{4,6},{5,7},{6,4},{7,5},{8,10},{9,11},{10,... | collective-permute-start | bytes 122888 | tf_op jit(solution)/shard_map/ppermute | solution.py:301
  24.0 5.8 %collective-permute-start.9 = (bf16[32,640]{1,0:T(8,128)(2,1)S(1)}, bf16[32,640]{1,0:T(8,128)(2,1)S(1)}, u32[]{:S(2)}, u32[]{:S(2)}) collective-permute-start(bf16[32,640]{1,0:T(8,128)(2,1)S(1)} %get-tuple-element.22), channel_id=1, source_target_pairs={{0,4},{1,5},{2,6},{3,7},{4,0},{5,1},{6,2},{7,3},{8,12},{9,13},{10,... | collective-permute-start | bytes 122888 | tf_op jit(solution)/shard_map/ppermute | solution.py:301
  24.6 5.9 %collective-permute-start.10 = (bf16[32,640]{1,0:T(8,128)(2,1)S(1)}, bf16[32,640]{1,0:T(8,128)(2,1)S(1)}, u32[]{:S(2)}, u32[]{:S(2)}) collective-permute-start(bf16[32,640]{1,0:T(8,128)(2,1)S(1)} %get-tuple-element.23), channel_id=1, source_target_pairs={{0,6},{1,7},{2,4},{3,5},{4,2},{5,3},{6,0},{7,1},{8,14},{9,15},{10,... | collective-permute-start | bytes 122888 | tf_op jit(solution)/shard_map/ppermute | solution.py:301
  30.8 3.2 %collective-permute-start.11 = (bf16[4,2,32,512]{3,2,1,0:T(8,128)(2,1)S(1)}, bf16[4,2,32,512]{3,2,1,0:T(8,128)(2,1)S(1)}, u32[]{:S(2)}, u32[]{:S(2)}) collective-permute-start(bf16[4,2,32,512]{3,2,1,0:T(8,128)(2,1)S(1)} %get-tuple-element.24.gk_own), channel_id=1, source_target_pairs={{0,1},{1,0},{2,3},{3,2},{4,5},{5,4},{6,7},{7,6},{8,9},{9,8},{10,11... | collective-permute-start | bytes 786440 | tf_op jit(solution)/shard_map/ppermute | solution.py:301
  30.9 8.9 %collective-permute-start.12 = (bf16[32,640]{1,0:T(8,128)(2,1)S(1)}, bf16[32,640]{1,0:T(8,128)(2,1)S(1)}, u32[]{:S(2)}, u32[]{:S(2)}) collective-permute-start(bf16[32,640]{1,0:T(8,128)(2,1)S(1)} %get-tuple-element.28.refs_0_), channel_id=1, source_target_pairs={{0,8},{8,0},{16,24},{24,16},{1,9},{9,1},{17,25},{25,17},{2,10},{10... | collective-permute-start | bytes 122888 | tf_op jit(solution)/shard_map/ppermute | solution.py:304
  32.5 7.3 %collective-permute-start.13 = (bf16[32,640]{1,0:T(8,128)(2,1)S(1)}, bf16[32,640]{1,0:T(8,128)(2,1)S(1)}, u32[]{:S(2)}, u32[]{:S(2)}) collective-permute-start(bf16[32,640]{1,0:T(8,128)(2,1)S(1)} %get-tuple-element.28.refs_0_), channel_id=1, source_target_pairs={{0,16},{8,24},{16,0},{24,8},{1,17},{9,25},{17,1},{25,9},{2,18},{10... | collective-permute-start | bytes 122888 | tf_op jit(solution)/shard_map/ppermute | solution.py:304
  34.0 5.8 %collective-permute-start.14 = (bf16[32,640]{1,0:T(8,128)(2,1)S(1)}, bf16[32,640]{1,0:T(8,128)(2,1)S(1)}, u32[]{:S(2)}, u32[]{:S(2)}) collective-permute-start(bf16[32,640]{1,0:T(8,128)(2,1)S(1)} %get-tuple-element.28.refs_0_), channel_id=1, source_target_pairs={{0,24},{8,16},{16,8},{24,0},{1,25},{9,17},{17,9},{25,1},{2,26},{10... | collective-permute-start | bytes 122888 | tf_op jit(solution)/shard_map/ppermute | solution.py:304

commit v4 on v3

--- a/solution.py
+++ b/solution.py
@@ -123,10 +123,9 @@
         outer = swap_halves(outer)
 
 
-def global_kernel(pieces, *refs):
-    gq, *blocks = refs[:5]
-    others, outs = refs[5 : pieces + 4], refs[pieces + 4 :]
-    q = jnp.concatenate([gq[...]] + [ref[0] for ref in others], 0)
+def global_kernel(count, *refs):
+    blocks, queries, outs = refs[:4], refs[4 : 4 + count], refs[4 + count :]
+    q = jnp.concatenate([ref[...] if len(ref.shape) == 2 else ref[0] for ref in queries], 0)
     own_k, own_v, facing_k, facing_v = [ref[...].reshape(-1, ref.shape[2]) for ref in blocks]
     partial_softmax(q, [own_k, facing_k], [own_v, facing_v], outs)
 
@@ -330,12 +329,14 @@
     halo_down = lax.ppermute(to_down, "station", down)
     pieces = [over_tm(glob, 2 * m) for m in range(1, chips)]
 
-    parts = list(call(
-        functools.partial(global_kernel, chips),
-        [glob_queries, grid_keys, values, *facing, *pieces],
-        [(own, payload)] * chips,
-        2 * 10**9,
-    ))
+    parts, arrived = [], [glob_queries, *pieces]
+    for some in (arrived[: chips // 2], arrived[chips // 2 :]):
+        parts += call(
+            functools.partial(global_kernel, len(some)),
+            [grid_keys, values, *facing, *some],
+            [(own, payload)] * len(some),
+            10**9,
+        )
     parts = parts[:1] + [over_tm(part, 2 * m) for m, part in enumerate(parts) if m]
     merged, kv_own = call(
         functools.partial(merge_kernel, chips),

time: 41.1 us -> 40.9 us (level)
  waiting for transfers between devices: 4.07 us -> 2.8 us
  starting transfers between devices: 26 us -> 26.7 us
    ppermute x9, waiting for transfers between devices: 4.05 us -> 2.79 us  [over_tm(): return lax.ppermute(x, 'tm', [(i, i ^ mask) for i in range(across)])]
    ppermute x3, starting transfers between devices: 4.04 us -> 4.76 us  [over_station(): return lax.ppermute(x, 'station', [(i, i ^ mask) for i in range(stations)])]
    pallas_call x5 -> x6, Pallas kernels: 8.05 us -> 8.34 us  [call(): pl.pallas_call(kernel, out_shape=[jax.ShapeDtypeStruct(s, BF) for s in ou...]
  transfers between devices with their start and end apart: 15 -> 15, of which waited for: 2 -> 2; matrix products, arithmetic and copies ran while one was open for 0% -> 0% of each run, Pallas kernels for 22% -> 23%
where the time goes in v4:
time: 40.9 us; the launch traced here: 40.7 us
  starting transfers between devices  26.7 us (65%)
  Pallas kernels  10.3 us (25%)
  waiting for transfers between devices  2.8 us (7%)
  between operations  0.83 us (2%)
    ppermute x9, starting transfers between devices, over_tm(): return lax.ppermute(x, 'tm', [(i, i ^ mask) for i in range(across)])  16.6 us
    pallas_call x6, Pallas kernels, call(): pl.pallas_call(kernel, out_shape=[jax.ShapeDtypeStruct(s, BF) for s in ou...  8.34 us
    ppermute x3, starting transfers between devices, over_station(): return lax.ppermute(x, 'station', [(i, i ^ mask) for i in range(stations)])  4.76 us
    ppermute x1, starting transfers between devices, body(): halo_up = lax.ppermute(to_up, 'station', up)  3.42 us
    ppermute x9, waiting for transfers between devices, over_tm(): return lax.ppermute(x, 'tm', [(i, i ^ mask) for i in range(across)])  2.79 us
    pallas_call x1, Pallas kernels, body(): pl.pallas_call(pack_first_kernel, out_shape=[jax.ShapeDtypeStruct(shape,...  1.91 us
    ppermute x1, starting transfers between devices, body(): halo_down = lax.ppermute(to_down, 'station', down)  1.29 us
  transfers between devices with their start and end apart: 15, of which 2 were waited for; matrix products, arithmetic and copies ran while one was open for 0% of the time, Pallas kernels for 23%

profile of v4, /device:TPU:0, one launch (start us, length us, event | category | flops | bytes accessed | tf_op | source)
XLA Modules:
  0.0 40.7 jit_solution(7324375767007992114)
XLA Ops:
  0.6 0.5 %collective-permute-start = (bf16[16,32,512]{2,1,0:T(8,128)(2,1)}, bf16[16,32,512]{2,1,0:T(8,128)(2,1)S(1)}, u32[]{:S(2)}, u32[]{:S(2)}) collective-permute-start(bf16[16,32,512]{2,1,0:T(8,128)(2,1)} %k_ref.5), channel_id=1, source_target_pairs={{0,1},{1,0},{2,3},{3,2},{4,5},{5,4},{6,7},{7,6},{8,9},{9,8},{10,11... | collective-permute-start | bytes 1572872 | tf_op jit(solution)/shard_map/ppermute | solution.py:300
  1.2 0.1 collective-permute-start.1
  1.2 1.9 %shard_map.86 = (bf16[16,8,512]{2,1,0:T(8,128)(2,1)}, bf16[3,32,512]{2,1,0:T(8,128)(2,1)}) custom-call(bf16[16,32,512]{2,1,0:T(8,128)(2,1)} %k_ref.5, bf16[16,32,512]{2,1,0:T(8,128)(2,1)} %v_ref.5, bf16[32,512]{1,0:T(8,128)(2,1)} %gq.3, bf16[32,512]{1,0:T(8,128)(2,1)} %refs_4_.3, bf16[32,512]{1,0:T(8,128)(2,1)} %refs_5_.2), custom_call_target="tpu_custom_call" | custom-call | flops 1000000 | bytes 1048576 | tf_op jit(solution)/shard_map/pallas_call | solution.py:308
  3.2 0.7 %collective-permute-start.2 = (bf16[16,8,512]{2,1,0:T(8,128)(2,1)}, bf16[16,8,512]{2,1,0:T(8,128)(2,1)S(1)}, u32[]{:S(2)}, u32[]{:S(2)}) collective-permute-start(bf16[16,8,512]{2,1,0:T(8,128)(2,1)} %get-tuple-element.16), channel_id=1, source_target_pairs={{1,2},{3,4},{5,6},{2,1},{4,3},{6,5},{9,10},{11,12},{13,14},{10,9},... | collective-permute-start | bytes 393224 | tf_op jit(solution)/shard_map/ppermute | solution.py:321
  3.8 0.0 copy-start.5
  3.9 4.3 %collective-permute-start.5 = (bf16[3,32,512]{2,1,0:T(8,128)(2,1)}, bf16[3,32,512]{2,1,0:T(8,128)(2,1)S(1)}, u32[]{:S(2)}, u32[]{:S(2)}) collective-permute-start(bf16[3,32,512]{2,1,0:T(8,128)(2,1)} %get-tuple-element.19), channel_id=1, source_target_pairs={{0,2},{1,3},{2,0},{3,1},{4,6},{5,7},{6,4},{7,5},{8,10},{9,11},{10,... | collective-permute-start | bytes 294920 | tf_op jit(solution)/shard_map/ppermute | solution.py:300
  8.2 2.7 %collective-permute-start.7 = (bf16[3,32,512]{2,1,0:T(8,128)(2,1)}, bf16[3,32,512]{2,1,0:T(8,128)(2,1)S(1)}, u32[]{:S(2)}, u32[]{:S(2)}) collective-permute-start(bf16[3,32,512]{2,1,0:T(8,128)(2,1)} %get-tuple-element.19), channel_id=1, source_target_pairs={{0,4},{1,5},{2,6},{3,7},{4,0},{5,1},{6,2},{7,3},{8,12},{9,13},{10,... | collective-permute-start | bytes 294920 | tf_op jit(solution)/shard_map/ppermute | solution.py:300
  10.9 0.0 collective-permute-done.2.outer_ref
  10.9 4.4 %collective-permute-start.8 = (bf16[3,32,512]{2,1,0:T(8,128)(2,1)}, bf16[3,32,512]{2,1,0:T(8,128)(2,1)S(1)}, u32[]{:S(2)}, u32[]{:S(2)}) collective-permute-start(bf16[3,32,512]{2,1,0:T(8,128)(2,1)} %get-tuple-element.19), channel_id=1, source_target_pairs={{0,6},{1,7},{2,4},{3,5},{4,2},{5,3},{6,0},{7,1},{8,14},{9,15},{10,... | collective-permute-start | bytes 294920 | tf_op jit(solution)/shard_map/ppermute | solution.py:300
  15.3 0.0 collective-permute-done.facing_k.refs_2_
  15.3 0.0 collective-permute-done.1.facing_v.refs_3_
  15.3 0.1 shard_map.87
  15.5 3.4 %collective-permute-start.3 = (bf16[8,40,512]{2,1,0:T(8,128)(2,1)S(1)}, bf16[8,40,512]{2,1,0:T(8,128)(2,1)S(1)}, u32[]{:S(2)}, u32[]{:S(2)}) collective-permute-start(bf16[8,40,512]{2,1,0:T(8,128)(2,1)S(1)} %get-tuple-element.17), channel_id=1, source_target_pairs={{0,8},{8,16},{16,24},{1,9},{9,17},{17,25},{2,10},{10,18},{18,26},{... | collective-permute-start | bytes 983048 | tf_op jit(solution)/shard_map/ppermute | solution.py:328
  18.9 1.3 %collective-permute-start.4 = (bf16[8,40,512]{2,1,0:T(8,128)(2,1)S(1)}, bf16[8,40,512]{2,1,0:T(8,128)(2,1)S(1)}, u32[]{:S(2)}, u32[]{:S(2)}) collective-permute-start(bf16[8,40,512]{2,1,0:T(8,128)(2,1)S(1)} %get-tuple-element.18), channel_id=1, source_target_pairs={{8,0},{16,8},{24,16},{9,1},{17,9},{25,17},{10,2},{18,10},{26,18},{... | collective-permute-start | bytes 983048 | tf_op jit(solution)/shard_map/ppermute | solution.py:329
  20.2 1.0 %shard_map.88 = (bf16[32,640]{1,0:T(8,128)(2,1)S(1)}, bf16[32,640]{1,0:T(8,128)(2,1)S(1)}) custom-call(bf16[16,32,512]{2,1,0:T(8,128)(2,1)S(1)} %copy-done, bf16[16,32,512]{2,1,0:T(8,128)(2,1)S(1)} %copy-done.1, bf16[16,32,512]{2,1,0:T(8,128)(2,1)S(1)} %collective-permute-done.facing_k.refs_2_, ...), custom_call_target="tpu_custom_call" | custom-call | flops 1000000000 | bytes 1048576 | tf_op jit(solution)/shard_map/pallas_call | solution.py:282
  21.2 0.0 copy-start.3
  21.3 0.0 copy-start.4
  21.3 0.1 collective-permute-start.6
  21.4 0.0 copy-start.6
  21.4 1.0 %shard_map.89 = (bf16[32,640]{1,0:T(8,128)(2,1)S(1)}, bf16[32,640]{1,0:T(8,128)(2,1)S(1)}) custom-call(bf16[16,32,512]{2,1,0:T(8,128)(2,1)S(1)} %copy-done, bf16[16,32,512]{2,1,0:T(8,128)(2,1)S(1)} %copy-done.1, bf16[16,32,512]{2,1,0:T(8,128)(2,1)S(1)} %collective-permute-done.facing_k.refs_2_, ...), custom_call_target="tpu_custom_call" | custom-call | flops 1000000000 | bytes 1048576 | tf_op jit(solution)/shard_map/pallas_call | solution.py:282
  22.4 0.0 copy-start.2
  22.4 1.4 %collective-permute-start.9 = (bf16[32,640]{1,0:T(8,128)(2,1)S(1)}, bf16[32,640]{1,0:T(8,128)(2,1)S(1)}, u32[]{:S(2)}, u32[]{:S(2)}) collective-permute-start(bf16[32,640]{1,0:T(8,128)(2,1)S(1)} %get-tuple-element.22), channel_id=1, source_target_pairs={{0,4},{1,5},{2,6},{3,7},{4,0},{5,1},{6,2},{7,3},{8,12},{9,13},{10,... | collective-permute-start | bytes 122888 | tf_op jit(solution)/shard_map/ppermute | solution.py:300
  23.8 3.0 %collective-permute-start.10 = (bf16[32,640]{1,0:T(8,128)(2,1)S(1)}, bf16[32,640]{1,0:T(8,128)(2,1)S(1)}, u32[]{:S(2)}, u32[]{:S(2)}) collective-permute-start(bf16[32,640]{1,0:T(8,128)(2,1)S(1)} %get-tuple-element.23), channel_id=1, source_target_pairs={{0,6},{1,7},{2,4},{3,5},{4,2},{5,3},{6,0},{7,1},{8,14},{9,15},{10,... | collective-permute-start | bytes 122888 | tf_op jit(solution)/shard_map/ppermute | solution.py:300
  26.8 0.5 %collective-permute-done.9.refs_2_ = bf16[32,640]{1,0:T(8,128)(2,1)S(1)} collective-permute-done((bf16[32,640]{1,0:T(8,128)(2,1)S(1)}, bf16[32,640]{1,0:T(8,128)(2,1)S(1)}, u32[]{:S(2)}, u32[]{:S(2)}) %collective-permute-start.9) | collective-permute-done | bytes 40992 | tf_op jit(solution)/shard_map/ppermute | solution.py:300
  27.4 2.2 %collective-permute-done.10.refs_3_ = bf16[32,640]{1,0:T(8,128)(2,1)S(1)} collective-permute-done((bf16[32,640]{1,0:T(8,128)(2,1)S(1)}, bf16[32,640]{1,0:T(8,128)(2,1)S(1)}, u32[]{:S(2)}, u32[]{:S(2)}) %collective-permute-start.10) | collective-permute-done | bytes 40992 | tf_op jit(solution)/shard_map/ppermute | solution.py:300
  29.6 0.3 shard_map.90
  29.9 0.1 collective-permute-start.11
  30.0 2.4 %collective-permute-start.12 = (bf16[32,640]{1,0:T(8,128)(2,1)S(1)}, bf16[32,640]{1,0:T(8,128)(2,1)S(1)}, u32[]{:S(2)}, u32[]{:S(2)}) collective-permute-start(bf16[32,640]{1,0:T(8,128)(2,1)S(1)} %get-tuple-element.28.refs_0_), channel_id=1, source_target_pairs={{0,8},{8,0},{16,24},{24,16},{1,9},{9,1},{17,25},{25,17},{2,10},{10... | collective-permute-start | bytes 122888 | tf_op jit(solution)/shard_map/ppermute | solution.py:303
  32.3 1.5 %collective-permute-start.13 = (bf16[32,640]{1,0:T(8,128)(2,1)S(1)}, bf16[32,640]{1,0:T(8,128)(2,1)S(1)}, u32[]{:S(2)}, u32[]{:S(2)}) collective-permute-start(bf16[32,640]{1,0:T(8,128)(2,1)S(1)} %get-tuple-element.28.refs_0_), channel_id=1, source_target_pairs={{0,16},{8,24},{16,0},{24,8},{1,17},{9,25},{17,1},{25,9},{2,18},{10... | collective-permute-start | bytes 122888 | tf_op jit(solution)/shard_map/ppermute | solution.py:303
  33.8 0.9 %collective-permute-start.14 = (bf16[32,640]{1,0:T(8,128)(2,1)S(1)}, bf16[32,640]{1,0:T(8,128)(2,1)S(1)}, u32[]{:S(2)}, u32[]{:S(2)}) collective-permute-start(bf16[32,640]{1,0:T(8,128)(2,1)S(1)} %get-tuple-element.28.refs_0_), channel_id=1, source_target_pairs={{0,24},{8,16},{16,8},{24,0},{1,25},{9,17},{17,9},{25,1},{2,26},{10... | collective-permute-start | bytes 122888 | tf_op jit(solution)/shard_map/ppermute | solution.py:303
  34.8 4.8 %shard_map.91 = (bf16[16,32,512]{2,1,0:T(8,128)(2,1)}, bf16[32,640]{1,0:T(8,128)(2,1)S(1)}) custom-call(bf16[16,32,512]{2,1,0:T(8,128)(2,1)S(1)} %copy-done.6, bf16[16,32,512]{2,1,0:T(8,128)(2,1)S(1)} %copy-done, bf16[16,32,512]{2,1,0:T(8,128)(2,1)S(1)} %copy-done.1, bf16[8,40,512]{2,1,0:T(8,128)(2,1)S(1)} %collective-permute-done.3.halo_up, ...), custom_call_target="tpu_custom_call" | custom-call | flops 6000000000 | bytes 1048576 | tf_op jit(solution)/shard_map/pallas_call | solution.py:282
  39.6 1.1 %shard_map.92 = bf16[32,512]{1,0:T(8,128)(2,1)} custom-call(bf16[32,640]{1,0:T(8,128)(2,1)S(1)} %get-tuple-element.28.refs_0_, bf16[32,640]{1,0:T(8,128)(2,1)S(1)} %collective-permute-done.12.refs_1_, bf16[32,640]{1,0:T(8,128)(2,1)S(1)} %collective-permute-done.13.refs_2_, bf16[32,640]{1,0:T(8,128)(2,1)S(1)} %collective-permute-done.14.refs_3_, ...), custom_call_target="tpu_custom_call" | custom-call | flops 100000000 | bytes 1048576 | tf_op jit(solution)/shard_map/pallas_call | solution.py:282
  (19 shorter events, 0.0 us)
Async XLA Ops:
  0.6 14.7 %copy-start = (bf16[16,32,512]{2,1,0:T(8,128)(2,1)S(1)}, bf16[16,32,512]{2,1,0:T(8,128)(2,1)}, u32[]{:S(2)}) copy-start(bf16[16,32,512]{2,1,0:T(8,128)(2,1)} %k_ref.5) | copy-start | bytes 1572868
  0.6 14.7 %copy-start.1 = (bf16[16,32,512]{2,1,0:T(8,128)(2,1)S(1)}, bf16[16,32,512]{2,1,0:T(8,128)(2,1)}, u32[]{:S(2)}) copy-start(bf16[16,32,512]{2,1,0:T(8,128)(2,1)} %v_ref.5) | copy-start | bytes 1572868
  0.6 14.7 %collective-permute-start = (bf16[16,32,512]{2,1,0:T(8,128)(2,1)}, bf16[16,32,512]{2,1,0:T(8,128)(2,1)S(1)}, u32[]{:S(2)}, u32[]{:S(2)}) collective-permute-start(bf16[16,32,512]{2,1,0:T(8,128)(2,1)} %k_ref.5), channel_id=1, source_target_pairs={{0,1},{1,0},{2,3},{3,2},{4,5},{5,4},{6,7},{7,6},{8,9},{9,8},{10,11... | collective-permute-start | bytes 1572872 | tf_op jit(solution)/shard_map/ppermute | solution.py:300
  1.2 14.1 %collective-permute-start.1 = (bf16[16,32,512]{2,1,0:T(8,128)(2,1)}, bf16[16,32,512]{2,1,0:T(8,128)(2,1)S(1)}, u32[]{:S(2)}, u32[]{:S(2)}) collective-permute-start(bf16[16,32,512]{2,1,0:T(8,128)(2,1)} %v_ref.5), channel_id=1, source_target_pairs={{0,1},{1,0},{2,3},{3,2},{4,5},{5,4},{6,7},{7,6},{8,9},{9,8},{10,11... | collective-permute-start | bytes 1572872 | tf_op jit(solution)/shard_map/ppermute | solution.py:300
  3.2 7.7 %collective-permute-start.2 = (bf16[16,8,512]{2,1,0:T(8,128)(2,1)}, bf16[16,8,512]{2,1,0:T(8,128)(2,1)S(1)}, u32[]{:S(2)}, u32[]{:S(2)}) collective-permute-start(bf16[16,8,512]{2,1,0:T(8,128)(2,1)} %get-tuple-element.16), channel_id=1, source_target_pairs={{1,2},{3,4},{5,6},{2,1},{4,3},{6,5},{9,10},{11,12},{13,14},{10,9},... | collective-permute-start | bytes 393224 | tf_op jit(solution)/shard_map/ppermute | solution.py:321
  3.8 16.4 %copy-start.5 = (bf16[32,512]{1,0:T(8,128)(2,1)S(1)}, bf16[32,512]{1,0:T(8,128)(2,1)}, u32[]{:S(2)}) copy-start(bf16[32,512]{1,0:T(8,128)(2,1)} %gq.3) | copy-start | bytes 98308
  3.9 16.3 %collective-permute-start.5 = (bf16[3,32,512]{2,1,0:T(8,128)(2,1)}, bf16[3,32,512]{2,1,0:T(8,128)(2,1)S(1)}, u32[]{:S(2)}, u32[]{:S(2)}) collective-permute-start(bf16[3,32,512]{2,1,0:T(8,128)(2,1)} %get-tuple-element.19), channel_id=1, source_target_pairs={{0,2},{1,3},{2,0},{3,1},{4,6},{5,7},{6,4},{7,5},{8,10},{9,11},{10,... | collective-permute-start | bytes 294920 | tf_op jit(solution)/shard_map/ppermute | solution.py:300
  8.2 13.2 %collective-permute-start.7 = (bf16[3,32,512]{2,1,0:T(8,128)(2,1)}, bf16[3,32,512]{2,1,0:T(8,128)(2,1)S(1)}, u32[]{:S(2)}, u32[]{:S(2)}) collective-permute-start(bf16[3,32,512]{2,1,0:T(8,128)(2,1)} %get-tuple-element.19), channel_id=1, source_target_pairs={{0,4},{1,5},{2,6},{3,7},{4,0},{5,1},{6,2},{7,3},{8,12},{9,13},{10,... | collective-permute-start | bytes 294920 | tf_op jit(solution)/shard_map/ppermute | solution.py:300
  10.9 10.5 %collective-permute-start.8 = (bf16[3,32,512]{2,1,0:T(8,128)(2,1)}, bf16[3,32,512]{2,1,0:T(8,128)(2,1)S(1)}, u32[]{:S(2)}, u32[]{:S(2)}) collective-permute-start(bf16[3,32,512]{2,1,0:T(8,128)(2,1)} %get-tuple-element.19), channel_id=1, source_target_pairs={{0,6},{1,7},{2,4},{3,5},{4,2},{5,3},{6,0},{7,1},{8,14},{9,15},{10,... | collective-permute-start | bytes 294920 | tf_op jit(solution)/shard_map/ppermute | solution.py:300
  15.5 19.3 %collective-permute-start.3 = (bf16[8,40,512]{2,1,0:T(8,128)(2,1)S(1)}, bf16[8,40,512]{2,1,0:T(8,128)(2,1)S(1)}, u32[]{:S(2)}, u32[]{:S(2)}) collective-permute-start(bf16[8,40,512]{2,1,0:T(8,128)(2,1)S(1)} %get-tuple-element.17), channel_id=1, source_target_pairs={{0,8},{8,16},{16,24},{1,9},{9,17},{17,25},{2,10},{10,18},{18,26},{... | collective-permute-start | bytes 983048 | tf_op jit(solution)/shard_map/ppermute | solution.py:328
  18.9 15.9 %collective-permute-start.4 = (bf16[8,40,512]{2,1,0:T(8,128)(2,1)S(1)}, bf16[8,40,512]{2,1,0:T(8,128)(2,1)S(1)}, u32[]{:S(2)}, u32[]{:S(2)}) collective-permute-start(bf16[8,40,512]{2,1,0:T(8,128)(2,1)S(1)} %get-tuple-element.18), channel_id=1, source_target_pairs={{8,0},{16,8},{24,16},{9,1},{17,9},{25,17},{10,2},{18,10},{26,18},{... | collective-permute-start | bytes 983048 | tf_op jit(solution)/shard_map/ppermute | solution.py:329
  21.2 8.4 %copy-start.3 = (bf16[32,512]{1,0:T(8,128)(2,1)S(1)}, bf16[32,512]{1,0:T(8,128)(2,1)}, u32[]{:S(2)}) copy-start(bf16[32,512]{1,0:T(8,128)(2,1)} %refs_4_.3) | copy-start | bytes 98308
  21.3 8.4 %copy-start.4 = (bf16[32,512]{1,0:T(8,128)(2,1)S(1)}, bf16[32,512]{1,0:T(8,128)(2,1)}, u32[]{:S(2)}) copy-start(bf16[32,512]{1,0:T(8,128)(2,1)} %refs_5_.2) | copy-start | bytes 98308
  21.3 5.6 %collective-permute-start.6 = (bf16[32,640]{1,0:T(8,128)(2,1)S(1)}, bf16[32,640]{1,0:T(8,128)(2,1)S(1)}, u32[]{:S(2)}, u32[]{:S(2)}) collective-permute-start(bf16[32,640]{1,0:T(8,128)(2,1)S(1)} %get-tuple-element.21), channel_id=1, source_target_pairs={{0,2},{1,3},{2,0},{3,1},{4,6},{5,7},{6,4},{7,5},{8,10},{9,11},{10,... | collective-permute-start | bytes 122888 | tf_op jit(solution)/shard_map/ppermute | solution.py:300
  21.4 13.4 %copy-start.6 = (bf16[16,32,512]{2,1,0:T(8,128)(2,1)S(1)}, bf16[16,32,512]{2,1,0:T(8,128)(2,1)}, u32[]{:S(2)}) copy-start(bf16[16,32,512]{2,1,0:T(8,128)(2,1)} %q_ref.1) | copy-start | bytes 1572868
  22.4 12.3 %copy-start.2 = (bf16[512,512]{1,0:T(8,128)(2,1)S(1)}, bf16[512,512]{1,0:T(8,128)(2,1)}, u32[]{:S(2)}) copy-start(bf16[512,512]{1,0:T(8,128)(2,1)} %refs_5_.3) | copy-start | bytes 1572868
  22.4 5.0 %collective-permute-start.9 = (bf16[32,640]{1,0:T(8,128)(2,1)S(1)}, bf16[32,640]{1,0:T(8,128)(2,1)S(1)}, u32[]{:S(2)}, u32[]{:S(2)}) collective-permute-start(bf16[32,640]{1,0:T(8,128)(2,1)S(1)} %get-tuple-element.22), channel_id=1, source_target_pairs={{0,4},{1,5},{2,6},{3,7},{4,0},{5,1},{6,2},{7,3},{8,12},{9,13},{10,... | collective-permute-start | bytes 122888 | tf_op jit(solution)/shard_map/ppermute | solution.py:300
  23.8 5.8 %collective-permute-start.10 = (bf16[32,640]{1,0:T(8,128)(2,1)S(1)}, bf16[32,640]{1,0:T(8,128)(2,1)S(1)}, u32[]{:S(2)}, u32[]{:S(2)}) collective-permute-start(bf16[32,640]{1,0:T(8,128)(2,1)S(1)} %get-tuple-element.23), channel_id=1, source_target_pairs={{0,6},{1,7},{2,4},{3,5},{4,2},{5,3},{6,0},{7,1},{8,14},{9,15},{10,... | collective-permute-start | bytes 122888 | tf_op jit(solution)/shard_map/ppermute | solution.py:300
  29.9 4.0 %collective-permute-start.11 = (bf16[4,2,32,512]{3,2,1,0:T(8,128)(2,1)S(1)}, bf16[4,2,32,512]{3,2,1,0:T(8,128)(2,1)S(1)}, u32[]{:S(2)}, u32[]{:S(2)}) collective-permute-start(bf16[4,2,32,512]{3,2,1,0:T(8,128)(2,1)S(1)} %get-tuple-element.24.gk_own), channel_id=1, source_target_pairs={{0,1},{1,0},{2,3},{3,2},{4,5},{5,4},{6,7},{7,6},{8,9},{9,8},{10,11... | collective-permute-start | bytes 786440 | tf_op jit(solution)/shard_map/ppermute | solution.py:300
  30.0 9.6 %collective-permute-start.12 = (bf16[32,640]{1,0:T(8,128)(2,1)S(1)}, bf16[32,640]{1,0:T(8,128)(2,1)S(1)}, u32[]{:S(2)}, u32[]{:S(2)}) collective-permute-start(bf16[32,640]{1,0:T(8,128)(2,1)S(1)} %get-tuple-element.28.refs_0_), channel_id=1, source_target_pairs={{0,8},{8,0},{16,24},{24,16},{1,9},{9,1},{17,25},{25,17},{2,10},{10... | collective-permute-start | bytes 122888 | tf_op jit(solution)/shard_map/ppermute | solution.py:303
  32.3 7.3 %collective-permute-start.13 = (bf16[32,640]{1,0:T(8,128)(2,1)S(1)}, bf16[32,640]{1,0:T(8,128)(2,1)S(1)}, u32[]{:S(2)}, u32[]{:S(2)}) collective-permute-start(bf16[32,640]{1,0:T(8,128)(2,1)S(1)} %get-tuple-element.28.refs_0_), channel_id=1, source_target_pairs={{0,16},{8,24},{16,0},{24,8},{1,17},{9,25},{17,1},{25,9},{2,18},{10... | collective-permute-start | bytes 122888 | tf_op jit(solution)/shard_map/ppermute | solution.py:303
  33.8 5.7 %collective-permute-start.14 = (bf16[32,640]{1,0:T(8,128)(2,1)S(1)}, bf16[32,640]{1,0:T(8,128)(2,1)S(1)}, u32[]{:S(2)}, u32[]{:S(2)}) collective-permute-start(bf16[32,640]{1,0:T(8,128)(2,1)S(1)} %get-tuple-element.28.refs_0_), channel_id=1, source_target_pairs={{0,24},{8,16},{16,8},{24,0},{1,25},{9,17},{17,9},{25,1},{2,26},{10... | collective-permute-start | bytes 122888 | tf_op jit(solution)/shard_map/ppermute | solution.py:303

commit v5 on v4

--- a/solution.py
+++ b/solution.py
@@ -226,12 +226,13 @@
 
 
 def grid_kernel(q_ref, k_ref, v_ref, halo_up, halo_down, gk_own, gk_other, edge_k, edge_v, gq, weight,
-                out_ref, extra_ref):
+                out_ref, extra_ref, rows_ref, sems):
     rows, cols, width = q_ref.shape
     blocks, across = rows // SIDE, cols // SIDE
     gks, gvs = global_views(gk_own, gk_other)
     group = slice(0, SIDE)
     beyond = slice(cols, cols + SIDE)
+    copies = []
     for block in range(blocks):
         biases = [window_bias(block, blocks, wrap) for wrap in (False, True)]
         q_rows = slice(block * SIDE, (block + 1) * SIDE)
@@ -273,8 +274,13 @@
         for j in range(across):
             before = projected[(j - 1) % across][:, RAD:]
             after = projected[j][:, :RAD]
-            out_ref[q_rows, j * SIDE : (j + 1) * SIDE, :] = jnp.concatenate([before, after], 1).astype(BF)
+            rows_ref[q_rows, j * SIDE : (j + 1) * SIDE, :] = jnp.concatenate([before, after], 1).astype(BF)
+        band = pl.ds(block * SIDE, SIDE)
+        copies.append(pltpu.make_async_copy(rows_ref.at[band], out_ref.at[band], sems.at[block]))
+        copies[-1].start()
     partial_softmax(gq[...], gks, gvs, [extra_ref])
+    for copy in copies:
+        copy.wait()
 
 
 def call(kernel, inputs, out_shapes, flops):
@@ -345,12 +351,16 @@
         10**8,
     )
     kv_other = over_tm(kv_own, 1)
-    grid_output, extra = call(
+    operands = [queries, grid_keys, values, halo_up, halo_down, kv_own, kv_other, *edges, glob_queries, out_weight]
+    grid_output, extra = pl.pallas_call(
         grid_kernel,
-        [queries, grid_keys, values, halo_up, halo_down, kv_own, kv_other, *edges, glob_queries, out_weight],
-        [(rows, cols, width), (own, payload)],
-        6 * 10**9,
-    )
+        out_shape=[jax.ShapeDtypeStruct(s, BF) for s in ((rows, cols, width), (own, payload))],
+        in_specs=[pl.BlockSpec(memory_space=VMEM)] * len(operands),
+        out_specs=[pl.BlockSpec(memory_space=pltpu.HBM), pl.BlockSpec(memory_space=VMEM)],
+        scratch_shapes=[VMEM((rows, cols, width), BF), pltpu.SemaphoreType.DMA((rows // SIDE,))],
+        compiler_params=pltpu.CompilerParams(vmem_limit_bytes=VMEM_GRANT),
+        cost_estimate=pl.CostEstimate(flops=6 * 10**9, bytes_accessed=2**20, transcendentals=0),
+    )(*operands)
 
     parts = [merged] + [over_station(merged, m) for m in range(1, stations)]
     (glob_output,) = call(

time: 40.9 us -> 40.8 us (level)
    pallas_call x6 -> x5, Pallas kernels: 8.34 us -> 3.52 us  [call(): pl.pallas_call(kernel, out_shape=[jax.ShapeDtypeStruct(s, BF) for s in ou...]
    pallas_call x0 -> x1, Pallas kernels: none -> 4.78 us  [body(): pl.pallas_call(grid_kernel, out_shape=[jax.ShapeDtypeStruct(s, BF) for s...]
  transfers between devices with their start and end apart: 15 -> 15, of which waited for: 2 -> 2; matrix products, arithmetic and copies ran while one was open for 0% -> 0% of each run, Pallas kernels for 23% -> 22%
where the time goes in v5:
time: 40.8 us; the launch traced here: 40.6 us
  starting transfers between devices  26.7 us (65%)
  Pallas kernels  10.2 us (25%)
  waiting for transfers between devices  2.8 us (7%)
  between operations  0.85 us (2%)
    ppermute x9, starting transfers between devices, over_tm(): return lax.ppermute(x, 'tm', [(i, i ^ mask) for i in range(across)])  16.6 us
    pallas_call x1, Pallas kernels, body(): pl.pallas_call(grid_kernel, out_shape=[jax.ShapeDtypeStruct(s, BF) for s...  4.78 us
    ppermute x3, starting transfers between devices, over_station(): return lax.ppermute(x, 'station', [(i, i ^ mask) for i in range(stations)])  4.76 us
    pallas_call x5, Pallas kernels, call(): pl.pallas_call(kernel, out_shape=[jax.ShapeDtypeStruct(s, BF) for s in ou...  3.52 us
    ppermute x1, starting transfers between devices, body(): halo_up = lax.ppermute(to_up, 'station', up)  3.42 us
    ppermute x9, waiting for transfers between devices, over_tm(): return lax.ppermute(x, 'tm', [(i, i ^ mask) for i in range(across)])  2.79 us
    pallas_call x1, Pallas kernels, body(): pl.pallas_call(pack_first_kernel, out_shape=[jax.ShapeDtypeStruct(shape,...  1.91 us
    ppermute x1, starting transfers between devices, body(): halo_down = lax.ppermute(to_down, 'station', down)  1.29 us
  transfers between devices with their start and end apart: 15, of which 2 were waited for; matrix products, arithmetic and copies ran while one was open for 0% of the time, Pallas kernels for 22%

profile of v5, /device:TPU:0, one launch (start us, length us, event | category | flops | bytes accessed | tf_op | source)
XLA Modules:
  0.0 40.6 jit_solution(1021307047187783066)
XLA Ops:
  0.6 0.5 %collective-permute-start = (bf16[16,32,512]{2,1,0:T(8,128)(2,1)}, bf16[16,32,512]{2,1,0:T(8,128)(2,1)S(1)}, u32[]{:S(2)}, u32[]{:S(2)}) collective-permute-start(bf16[16,32,512]{2,1,0:T(8,128)(2,1)} %k_ref.5), channel_id=1, source_target_pairs={{0,1},{1,0},{2,3},{3,2},{4,5},{5,4},{6,7},{7,6},{8,9},{9,8},{10,11... | collective-permute-start | bytes 1572872 | tf_op jit(solution)/shard_map/ppermute | solution.py:306
  1.2 0.1 collective-permute-start.1
  1.2 1.9 %shard_map.86 = (bf16[16,8,512]{2,1,0:T(8,128)(2,1)}, bf16[3,32,512]{2,1,0:T(8,128)(2,1)}) custom-call(bf16[16,32,512]{2,1,0:T(8,128)(2,1)} %k_ref.5, bf16[16,32,512]{2,1,0:T(8,128)(2,1)} %v_ref.5, bf16[32,512]{1,0:T(8,128)(2,1)} %gq.3, bf16[32,512]{1,0:T(8,128)(2,1)} %refs_4_.3, bf16[32,512]{1,0:T(8,128)(2,1)} %refs_5_.2), custom_call_target="tpu_custom_call" | custom-call | flops 1000000 | bytes 1048576 | tf_op jit(solution)/shard_map/pallas_call | solution.py:314
  3.2 0.7 %collective-permute-start.2 = (bf16[16,8,512]{2,1,0:T(8,128)(2,1)}, bf16[16,8,512]{2,1,0:T(8,128)(2,1)S(1)}, u32[]{:S(2)}, u32[]{:S(2)}) collective-permute-start(bf16[16,8,512]{2,1,0:T(8,128)(2,1)} %get-tuple-element.16), channel_id=1, source_target_pairs={{1,2},{3,4},{5,6},{2,1},{4,3},{6,5},{9,10},{11,12},{13,14},{10,9},... | collective-permute-start | bytes 393224 | tf_op jit(solution)/shard_map/ppermute | solution.py:327
  3.8 0.0 copy-start.5
  3.9 4.3 %collective-permute-start.5 = (bf16[3,32,512]{2,1,0:T(8,128)(2,1)}, bf16[3,32,512]{2,1,0:T(8,128)(2,1)S(1)}, u32[]{:S(2)}, u32[]{:S(2)}) collective-permute-start(bf16[3,32,512]{2,1,0:T(8,128)(2,1)} %get-tuple-element.19), channel_id=1, source_target_pairs={{0,2},{1,3},{2,0},{3,1},{4,6},{5,7},{6,4},{7,5},{8,10},{9,11},{10,... | collective-permute-start | bytes 294920 | tf_op jit(solution)/shard_map/ppermute | solution.py:306
  8.2 2.7 %collective-permute-start.7 = (bf16[3,32,512]{2,1,0:T(8,128)(2,1)}, bf16[3,32,512]{2,1,0:T(8,128)(2,1)S(1)}, u32[]{:S(2)}, u32[]{:S(2)}) collective-permute-start(bf16[3,32,512]{2,1,0:T(8,128)(2,1)} %get-tuple-element.19), channel_id=1, source_target_pairs={{0,4},{1,5},{2,6},{3,7},{4,0},{5,1},{6,2},{7,3},{8,12},{9,13},{10,... | collective-permute-start | bytes 294920 | tf_op jit(solution)/shard_map/ppermute | solution.py:306
  10.9 0.0 collective-permute-done.2.outer_ref
  10.9 4.4 %collective-permute-start.8 = (bf16[3,32,512]{2,1,0:T(8,128)(2,1)}, bf16[3,32,512]{2,1,0:T(8,128)(2,1)S(1)}, u32[]{:S(2)}, u32[]{:S(2)}) collective-permute-start(bf16[3,32,512]{2,1,0:T(8,128)(2,1)} %get-tuple-element.19), channel_id=1, source_target_pairs={{0,6},{1,7},{2,4},{3,5},{4,2},{5,3},{6,0},{7,1},{8,14},{9,15},{10,... | collective-permute-start | bytes 294920 | tf_op jit(solution)/shard_map/ppermute | solution.py:306
  15.3 0.0 collective-permute-done.facing_k.refs_2_
  15.3 0.0 collective-permute-done.1.facing_v.refs_3_
  15.3 0.1 shard_map.87
  15.5 3.4 %collective-permute-start.3 = (bf16[8,40,512]{2,1,0:T(8,128)(2,1)S(1)}, bf16[8,40,512]{2,1,0:T(8,128)(2,1)S(1)}, u32[]{:S(2)}, u32[]{:S(2)}) collective-permute-start(bf16[8,40,512]{2,1,0:T(8,128)(2,1)S(1)} %get-tuple-element.17), channel_id=1, source_target_pairs={{0,8},{8,16},{16,24},{1,9},{9,17},{17,25},{2,10},{10,18},{18,26},{... | collective-permute-start | bytes 983048 | tf_op jit(solution)/shard_map/ppermute | solution.py:334
  18.9 1.3 %collective-permute-start.4 = (bf16[8,40,512]{2,1,0:T(8,128)(2,1)S(1)}, bf16[8,40,512]{2,1,0:T(8,128)(2,1)S(1)}, u32[]{:S(2)}, u32[]{:S(2)}) collective-permute-start(bf16[8,40,512]{2,1,0:T(8,128)(2,1)S(1)} %get-tuple-element.18), channel_id=1, source_target_pairs={{8,0},{16,8},{24,16},{9,1},{17,9},{25,17},{10,2},{18,10},{26,18},{... | collective-permute-start | bytes 983048 | tf_op jit(solution)/shard_map/ppermute | solution.py:335
  20.2 1.0 %shard_map.88 = (bf16[32,640]{1,0:T(8,128)(2,1)S(1)}, bf16[32,640]{1,0:T(8,128)(2,1)S(1)}) custom-call(bf16[16,32,512]{2,1,0:T(8,128)(2,1)S(1)} %copy-done, bf16[16,32,512]{2,1,0:T(8,128)(2,1)S(1)} %copy-done.1, bf16[16,32,512]{2,1,0:T(8,128)(2,1)S(1)} %collective-permute-done.facing_k.refs_2_, ...), custom_call_target="tpu_custom_call" | custom-call | flops 1000000000 | bytes 1048576 | tf_op jit(solution)/shard_map/pallas_call | solution.py:288
  21.2 0.0 copy-start.3
  21.3 0.0 copy-start.4
  21.3 0.1 collective-permute-start.6
  21.4 0.0 copy-start.6
  21.4 1.0 %shard_map.89 = (bf16[32,640]{1,0:T(8,128)(2,1)S(1)}, bf16[32,640]{1,0:T(8,128)(2,1)S(1)}) custom-call(bf16[16,32,512]{2,1,0:T(8,128)(2,1)S(1)} %copy-done, bf16[16,32,512]{2,1,0:T(8,128)(2,1)S(1)} %copy-done.1, bf16[16,32,512]{2,1,0:T(8,128)(2,1)S(1)} %collective-permute-done.facing_k.refs_2_, ...), custom_call_target="tpu_custom_call" | custom-call | flops 1000000000 | bytes 1048576 | tf_op jit(solution)/shard_map/pallas_call | solution.py:288
  22.4 0.0 copy-start.2
  22.4 1.4 %collective-permute-start.9 = (bf16[32,640]{1,0:T(8,128)(2,1)S(1)}, bf16[32,640]{1,0:T(8,128)(2,1)S(1)}, u32[]{:S(2)}, u32[]{:S(2)}) collective-permute-start(bf16[32,640]{1,0:T(8,128)(2,1)S(1)} %get-tuple-element.22), channel_id=1, source_target_pairs={{0,4},{1,5},{2,6},{3,7},{4,0},{5,1},{6,2},{7,3},{8,12},{9,13},{10,... | collective-permute-start | bytes 122888 | tf_op jit(solution)/shard_map/ppermute | solution.py:306
  23.8 3.0 %collective-permute-start.10 = (bf16[32,640]{1,0:T(8,128)(2,1)S(1)}, bf16[32,640]{1,0:T(8,128)(2,1)S(1)}, u32[]{:S(2)}, u32[]{:S(2)}) collective-permute-start(bf16[32,640]{1,0:T(8,128)(2,1)S(1)} %get-tuple-element.23), channel_id=1, source_target_pairs={{0,6},{1,7},{2,4},{3,5},{4,2},{5,3},{6,0},{7,1},{8,14},{9,15},{10,... | collective-permute-start | bytes 122888 | tf_op jit(solution)/shard_map/ppermute | solution.py:306
  26.8 0.5 %collective-permute-done.9.refs_2_ = bf16[32,640]{1,0:T(8,128)(2,1)S(1)} collective-permute-done((bf16[32,640]{1,0:T(8,128)(2,1)S(1)}, bf16[32,640]{1,0:T(8,128)(2,1)S(1)}, u32[]{:S(2)}, u32[]{:S(2)}) %collective-permute-start.9) | collective-permute-done | bytes 40992 | tf_op jit(solution)/shard_map/ppermute | solution.py:306
  27.4 2.2 %collective-permute-done.10.refs_3_ = bf16[32,640]{1,0:T(8,128)(2,1)S(1)} collective-permute-done((bf16[32,640]{1,0:T(8,128)(2,1)S(1)}, bf16[32,640]{1,0:T(8,128)(2,1)S(1)}, u32[]{:S(2)}, u32[]{:S(2)}) %collective-permute-start.10) | collective-permute-done | bytes 40992 | tf_op jit(solution)/shard_map/ppermute | solution.py:306
  29.6 0.3 shard_map.90
  29.9 0.1 collective-permute-start.11
  30.0 2.4 %collective-permute-start.12 = (bf16[32,640]{1,0:T(8,128)(2,1)S(1)}, bf16[32,640]{1,0:T(8,128)(2,1)S(1)}, u32[]{:S(2)}, u32[]{:S(2)}) collective-permute-start(bf16[32,640]{1,0:T(8,128)(2,1)S(1)} %get-tuple-element.28.refs_0_), channel_id=1, source_target_pairs={{0,8},{8,0},{16,24},{24,16},{1,9},{9,1},{17,25},{25,17},{2,10},{10... | collective-permute-start | bytes 122888 | tf_op jit(solution)/shard_map/ppermute | solution.py:309
  32.3 1.5 %collective-permute-start.13 = (bf16[32,640]{1,0:T(8,128)(2,1)S(1)}, bf16[32,640]{1,0:T(8,128)(2,1)S(1)}, u32[]{:S(2)}, u32[]{:S(2)}) collective-permute-start(bf16[32,640]{1,0:T(8,128)(2,1)S(1)} %get-tuple-element.28.refs_0_), channel_id=1, source_target_pairs={{0,16},{8,24},{16,0},{24,8},{1,17},{9,25},{17,1},{25,9},{2,18},{10... | collective-permute-start | bytes 122888 | tf_op jit(solution)/shard_map/ppermute | solution.py:309
  33.8 0.9 %collective-permute-start.14 = (bf16[32,640]{1,0:T(8,128)(2,1)S(1)}, bf16[32,640]{1,0:T(8,128)(2,1)S(1)}, u32[]{:S(2)}, u32[]{:S(2)}) collective-permute-start(bf16[32,640]{1,0:T(8,128)(2,1)S(1)} %get-tuple-element.28.refs_0_), channel_id=1, source_target_pairs={{0,24},{8,16},{16,8},{24,0},{1,25},{9,17},{17,9},{25,1},{2,26},{10... | collective-permute-start | bytes 122888 | tf_op jit(solution)/shard_map/ppermute | solution.py:309
  34.8 4.8 %shard_map.91 = (bf16[16,32,512]{2,1,0:T(8,128)(2,1)}, bf16[32,640]{1,0:T(8,128)(2,1)S(1)}) custom-call(bf16[16,32,512]{2,1,0:T(8,128)(2,1)S(1)} %copy-done.6, bf16[16,32,512]{2,1,0:T(8,128)(2,1)S(1)} %copy-done, bf16[16,32,512]{2,1,0:T(8,128)(2,1)S(1)} %copy-done.1, bf16[8,40,512]{2,1,0:T(8,128)(2,1)S(1)} %collective-permute-done.3.halo_up, ...), custom_call_target="tpu_custom_call" | custom-call | flops 6000000000 | bytes 1048576 | tf_op jit(solution)/shard_map/pallas_call | solution.py:355
  39.6 1.1 %shard_map.92 = bf16[32,512]{1,0:T(8,128)(2,1)} custom-call(bf16[32,640]{1,0:T(8,128)(2,1)S(1)} %get-tuple-element.28.refs_0_, bf16[32,640]{1,0:T(8,128)(2,1)S(1)} %collective-permute-done.12.refs_1_, bf16[32,640]{1,0:T(8,128)(2,1)S(1)} %collective-permute-done.13.refs_2_, bf16[32,640]{1,0:T(8,128)(2,1)S(1)} %collective-permute-done.14.refs_3_, ...), custom_call_target="tpu_custom_call" | custom-call | flops 100000000 | bytes 1048576 | tf_op jit(solution)/shard_map/pallas_call | solution.py:288
  (19 shorter events, 0.0 us)
Async XLA Ops:
  0.6 14.7 %copy-start = (bf16[16,32,512]{2,1,0:T(8,128)(2,1)S(1)}, bf16[16,32,512]{2,1,0:T(8,128)(2,1)}, u32[]{:S(2)}) copy-start(bf16[16,32,512]{2,1,0:T(8,128)(2,1)} %k_ref.5) | copy-start | bytes 1572868
  0.6 14.7 %copy-start.1 = (bf16[16,32,512]{2,1,0:T(8,128)(2,1)S(1)}, bf16[16,32,512]{2,1,0:T(8,128)(2,1)}, u32[]{:S(2)}) copy-start(bf16[16,32,512]{2,1,0:T(8,128)(2,1)} %v_ref.5) | copy-start | bytes 1572868
  0.6 14.7 %collective-permute-start = (bf16[16,32,512]{2,1,0:T(8,128)(2,1)}, bf16[16,32,512]{2,1,0:T(8,128)(2,1)S(1)}, u32[]{:S(2)}, u32[]{:S(2)}) collective-permute-start(bf16[16,32,512]{2,1,0:T(8,128)(2,1)} %k_ref.5), channel_id=1, source_target_pairs={{0,1},{1,0},{2,3},{3,2},{4,5},{5,4},{6,7},{7,6},{8,9},{9,8},{10,11... | collective-permute-start | bytes 1572872 | tf_op jit(solution)/shard_map/ppermute | solution.py:306
  1.2 14.1 %collective-permute-start.1 = (bf16[16,32,512]{2,1,0:T(8,128)(2,1)}, bf16[16,32,512]{2,1,0:T(8,128)(2,1)S(1)}, u32[]{:S(2)}, u32[]{:S(2)}) collective-permute-start(bf16[16,32,512]{2,1,0:T(8,128)(2,1)} %v_ref.5), channel_id=1, source_target_pairs={{0,1},{1,0},{2,3},{3,2},{4,5},{5,4},{6,7},{7,6},{8,9},{9,8},{10,11... | collective-permute-start | bytes 1572872 | tf_op jit(solution)/shard_map/ppermute | solution.py:306
  3.2 7.7 %collective-permute-start.2 = (bf16[16,8,512]{2,1,0:T(8,128)(2,1)}, bf16[16,8,512]{2,1,0:T(8,128)(2,1)S(1)}, u32[]{:S(2)}, u32[]{:S(2)}) collective-permute-start(bf16[16,8,512]{2,1,0:T(8,128)(2,1)} %get-tuple-element.16), channel_id=1, source_target_pairs={{1,2},{3,4},{5,6},{2,1},{4,3},{6,5},{9,10},{11,12},{13,14},{10,9},... | collective-permute-start | bytes 393224 | tf_op jit(solution)/shard_map/ppermute | solution.py:327
  3.8 16.4 %copy-start.5 = (bf16[32,512]{1,0:T(8,128)(2,1)S(1)}, bf16[32,512]{1,0:T(8,128)(2,1)}, u32[]{:S(2)}) copy-start(bf16[32,512]{1,0:T(8,128)(2,1)} %gq.3) | copy-start | bytes 98308
  3.9 16.3 %collective-permute-start.5 = (bf16[3,32,512]{2,1,0:T(8,128)(2,1)}, bf16[3,32,512]{2,1,0:T(8,128)(2,1)S(1)}, u32[]{:S(2)}, u32[]{:S(2)}) collective-permute-start(bf16[3,32,512]{2,1,0:T(8,128)(2,1)} %get-tuple-element.19), channel_id=1, source_target_pairs={{0,2},{1,3},{2,0},{3,1},{4,6},{5,7},{6,4},{7,5},{8,10},{9,11},{10,... | collective-permute-start | bytes 294920 | tf_op jit(solution)/shard_map/ppermute | solution.py:306
  8.2 13.2 %collective-permute-start.7 = (bf16[3,32,512]{2,1,0:T(8,128)(2,1)}, bf16[3,32,512]{2,1,0:T(8,128)(2,1)S(1)}, u32[]{:S(2)}, u32[]{:S(2)}) collective-permute-start(bf16[3,32,512]{2,1,0:T(8,128)(2,1)} %get-tuple-element.19), channel_id=1, source_target_pairs={{0,4},{1,5},{2,6},{3,7},{4,0},{5,1},{6,2},{7,3},{8,12},{9,13},{10,... | collective-permute-start | bytes 294920 | tf_op jit(solution)/shard_map/ppermute | solution.py:306
  10.9 10.5 %collective-permute-start.8 = (bf16[3,32,512]{2,1,0:T(8,128)(2,1)}, bf16[3,32,512]{2,1,0:T(8,128)(2,1)S(1)}, u32[]{:S(2)}, u32[]{:S(2)}) collective-permute-start(bf16[3,32,512]{2,1,0:T(8,128)(2,1)} %get-tuple-element.19), channel_id=1, source_target_pairs={{0,6},{1,7},{2,4},{3,5},{4,2},{5,3},{6,0},{7,1},{8,14},{9,15},{10,... | collective-permute-start | bytes 294920 | tf_op jit(solution)/shard_map/ppermute | solution.py:306
  15.5 19.3 %collective-permute-start.3 = (bf16[8,40,512]{2,1,0:T(8,128)(2,1)S(1)}, bf16[8,40,512]{2,1,0:T(8,128)(2,1)S(1)}, u32[]{:S(2)}, u32[]{:S(2)}) collective-permute-start(bf16[8,40,512]{2,1,0:T(8,128)(2,1)S(1)} %get-tuple-element.17), channel_id=1, source_target_pairs={{0,8},{8,16},{16,24},{1,9},{9,17},{17,25},{2,10},{10,18},{18,26},{... | collective-permute-start | bytes 983048 | tf_op jit(solution)/shard_map/ppermute | solution.py:334
  18.9 15.9 %collective-permute-start.4 = (bf16[8,40,512]{2,1,0:T(8,128)(2,1)S(1)}, bf16[8,40,512]{2,1,0:T(8,128)(2,1)S(1)}, u32[]{:S(2)}, u32[]{:S(2)}) collective-permute-start(bf16[8,40,512]{2,1,0:T(8,128)(2,1)S(1)} %get-tuple-element.18), channel_id=1, source_target_pairs={{8,0},{16,8},{24,16},{9,1},{17,9},{25,17},{10,2},{18,10},{26,18},{... | collective-permute-start | bytes 983048 | tf_op jit(solution)/shard_map/ppermute | solution.py:335
  21.2 8.4 %copy-start.3 = (bf16[32,512]{1,0:T(8,128)(2,1)S(1)}, bf16[32,512]{1,0:T(8,128)(2,1)}, u32[]{:S(2)}) copy-start(bf16[32,512]{1,0:T(8,128)(2,1)} %refs_4_.3) | copy-start | bytes 98308
  21.3 8.4 %copy-start.4 = (bf16[32,512]{1,0:T(8,128)(2,1)S(1)}, bf16[32,512]{1,0:T(8,128)(2,1)}, u32[]{:S(2)}) copy-start(bf16[32,512]{1,0:T(8,128)(2,1)} %refs_5_.2) | copy-start | bytes 98308
  21.3 5.6 %collective-permute-start.6 = (bf16[32,640]{1,0:T(8,128)(2,1)S(1)}, bf16[32,640]{1,0:T(8,128)(2,1)S(1)}, u32[]{:S(2)}, u32[]{:S(2)}) collective-permute-start(bf16[32,640]{1,0:T(8,128)(2,1)S(1)} %get-tuple-element.21), channel_id=1, source_target_pairs={{0,2},{1,3},{2,0},{3,1},{4,6},{5,7},{6,4},{7,5},{8,10},{9,11},{10,... | collective-permute-start | bytes 122888 | tf_op jit(solution)/shard_map/ppermute | solution.py:306
  21.4 13.4 %copy-start.6 = (bf16[16,32,512]{2,1,0:T(8,128)(2,1)S(1)}, bf16[16,32,512]{2,1,0:T(8,128)(2,1)}, u32[]{:S(2)}) copy-start(bf16[16,32,512]{2,1,0:T(8,128)(2,1)} %q_ref.1) | copy-start | bytes 1572868
  22.4 12.3 %copy-start.2 = (bf16[512,512]{1,0:T(8,128)(2,1)S(1)}, bf16[512,512]{1,0:T(8,128)(2,1)}, u32[]{:S(2)}) copy-start(bf16[512,512]{1,0:T(8,128)(2,1)} %refs_5_.3) | copy-start | bytes 1572868
  22.4 5.0 %collective-permute-start.9 = (bf16[32,640]{1,0:T(8,128)(2,1)S(1)}, bf16[32,640]{1,0:T(8,128)(2,1)S(1)}, u32[]{:S(2)}, u32[]{:S(2)}) collective-permute-start(bf16[32,640]{1,0:T(8,128)(2,1)S(1)} %get-tuple-element.22), channel_id=1, source_target_pairs={{0,4},{1,5},{2,6},{3,7},{4,0},{5,1},{6,2},{7,3},{8,12},{9,13},{10,... | collective-permute-start | bytes 122888 | tf_op jit(solution)/shard_map/ppermute | solution.py:306
  23.8 5.8 %collective-permute-start.10 = (bf16[32,640]{1,0:T(8,128)(2,1)S(1)}, bf16[32,640]{1,0:T(8,128)(2,1)S(1)}, u32[]{:S(2)}, u32[]{:S(2)}) collective-permute-start(bf16[32,640]{1,0:T(8,128)(2,1)S(1)} %get-tuple-element.23), channel_id=1, source_target_pairs={{0,6},{1,7},{2,4},{3,5},{4,2},{5,3},{6,0},{7,1},{8,14},{9,15},{10,... | collective-permute-start | bytes 122888 | tf_op jit(solution)/shard_map/ppermute | solution.py:306
  29.9 4.0 %collective-permute-start.11 = (bf16[4,2,32,512]{3,2,1,0:T(8,128)(2,1)S(1)}, bf16[4,2,32,512]{3,2,1,0:T(8,128)(2,1)S(1)}, u32[]{:S(2)}, u32[]{:S(2)}) collective-permute-start(bf16[4,2,32,512]{3,2,1,0:T(8,128)(2,1)S(1)} %get-tuple-element.24.gk_own), channel_id=1, source_target_pairs={{0,1},{1,0},{2,3},{3,2},{4,5},{5,4},{6,7},{7,6},{8,9},{9,8},{10,11... | collective-permute-start | bytes 786440 | tf_op jit(solution)/shard_map/ppermute | solution.py:306
  30.0 9.6 %collective-permute-start.12 = (bf16[32,640]{1,0:T(8,128)(2,1)S(1)}, bf16[32,640]{1,0:T(8,128)(2,1)S(1)}, u32[]{:S(2)}, u32[]{:S(2)}) collective-permute-start(bf16[32,640]{1,0:T(8,128)(2,1)S(1)} %get-tuple-element.28.refs_0_), channel_id=1, source_target_pairs={{0,8},{8,0},{16,24},{24,16},{1,9},{9,1},{17,25},{25,17},{2,10},{10... | collective-permute-start | bytes 122888 | tf_op jit(solution)/shard_map/ppermute | solution.py:309
  32.3 7.2 %collective-permute-start.13 = (bf16[32,640]{1,0:T(8,128)(2,1)S(1)}, bf16[32,640]{1,0:T(8,128)(2,1)S(1)}, u32[]{:S(2)}, u32[]{:S(2)}) collective-permute-start(bf16[32,640]{1,0:T(8,128)(2,1)S(1)} %get-tuple-element.28.refs_0_), channel_id=1, source_target_pairs={{0,16},{8,24},{16,0},{24,8},{1,17},{9,25},{17,1},{25,9},{2,18},{10... | collective-permute-start | bytes 122888 | tf_op jit(solution)/shard_map/ppermute | solution.py:309
  33.8 5.7 %collective-permute-start.14 = (bf16[32,640]{1,0:T(8,128)(2,1)S(1)}, bf16[32,640]{1,0:T(8,128)(2,1)S(1)}, u32[]{:S(2)}, u32[]{:S(2)}) collective-permute-start(bf16[32,640]{1,0:T(8,128)(2,1)S(1)} %get-tuple-element.28.refs_0_), channel_id=1, source_target_pairs={{0,24},{8,16},{16,8},{24,0},{1,25},{9,17},{17,9},{25,1},{2,26},{10... | collective-permute-start | bytes 122888 | tf_op jit(solution)/shard_map/ppermute | solution.py:309
